TPU v7x, 128 devices: a whole 4x4x4 slice. The times are simulated.
128 devices in a mesh: dp: 8 (over y, core), ctx: 16 (over z, x).
Axes of the slice: x: 4, y: 4, z: 4, core: 2. Of those that a mesh axis runs over, the one named last changes fastest.
Arguments:
- queries: bfloat16 [16384, 2048], P(('dp', 'ctx')), may hold values from -6 to 6
- key_rows: bfloat16 [16384, 2048], P(('dp', 'ctx')), may hold values from -6 to 6
- value_rows: bfloat16 [16384, 2048], P(('dp', 'ctx')), may hold values from -6 to 6
- hidden_in: bfloat16 [16384, 2304], P(('dp', 'ctx')), may hold values from -24 to 24
- beta_weight: bfloat16 [2304, 16], replicated, may hold values from -0.125 to 0.125
- log_gate: float32 [16, 16384], P(None, ('dp', 'ctx')), may hold values from -1 to 0
- out_grad: bfloat16 [16384, 2048], P(('dp', 'ctx')), may hold values from -24 to 24
- lengths: int32 [8, 4], P('dp'), may hold values from 1 to 1024, 2048 in all within a row
- rewards: float32 [32], replicated, may hold values from -6 to 6
- prompts: int32 [32], replicated, may hold values from 0 to 7
Outputs:
- query_grad: bfloat16 [16384, 2048], P(('dp', 'ctx'))
- key_grad: bfloat16 [16384, 2048], P(('dp', 'ctx'))
- value_grad: bfloat16 [16384, 2048], P(('dp', 'ctx'))
- gate_grad: float32 [16, 16384], P(None, ('dp', 'ctx'))
- beta_weight_grad: float32 [2304, 16], P(('dp', 'ctx'))
Inputs may be any that keep to these rules, and one draw needn't show every extreme that they name: `lengths`: each row sums to 2048; its largest entry is exactly 1024.
All inputs are finite; a program needn't handle non-finite values.
Results may differ from a plain program's by a relative error of at most 0.001.
Values sent between devices are 32-bit elements; how exact they have to be, the bound alone decides.
No kernel may reach another device: no remote copies, remote signals or barrier semaphores. Data moves between devices by JAX's collectives and lax.ppermute only.
A program may use at most 128 MiB of HBM per device.

v0:
```python
import jax
import jax.numpy as jnp
from jax import lax
from jax.sharding import PartitionSpec as P

BLOCK = 64


highest = lax.Precision.HIGHEST


def from_behind(x, axis, by):
    length = lax.axis_size(axis)
    pairs = [(i, i + by) for i in range(length) if 0 <= i + by < length]
    return lax.ppermute(x, axis, pairs)


def unit_rows(rows):
    return rows * lax.rsqrt(jnp.sum(rows * rows, axis=-1, keepdims=True) + 1e-06)


def unit_inverse(lower_part):
    size = lower_part.shape[-1]
    nilpotent = -lower_part
    total = jnp.eye(size, dtype=jnp.float32) + nilpotent
    power = nilpotent
    for level in range(max(1, (size - 1).bit_length()) - 1):
        power = jnp.einsum("nhij,nhjk->nhik", power, power, precision=highest)
        total = total + jnp.einsum("nhij,nhjk->nhik", total, power, precision=highest)
    return total


def block_terms(queries, key_rows, value_rows, beta, gate_log, starts):
    size = queries.shape[2]
    row_ids = lax.broadcasted_iota(jnp.int32, (size, size), 0)
    col_ids = lax.broadcasted_iota(jnp.int32, (size, size), 1)
    gamma = jnp.cumsum(gate_log, axis=-1)
    count = jnp.cumsum(starts, axis=-1)
    linked = (count[:, :, None] == count[:, None, :]) & (row_ids >= col_ids)
    linked = linked[:, None, :, :]
    spread = gamma[..., :, None] - gamma[..., None, :]
    decay = jnp.where(linked, jnp.exp(jnp.where(linked, spread, 0.0)), 0.0)
    head_decay = jnp.where(count == 0.0, 1.0, 0.0)[:, None, :] * jnp.exp(gamma)
    tail_decay = decay[..., size - 1, :]
    key_key = jnp.einsum("nhik,nhjk->nhij", key_rows, key_rows, precision=highest)
    lower_part = jnp.where(row_ids > col_ids, beta[..., :, None] * decay * key_key, 0.0)
    inverse = unit_inverse(lower_part)
    rhs_value = beta[..., None] * value_rows
    rhs_key = (beta * head_decay)[..., None] * key_rows
    u_zero = jnp.einsum("nhij,nhjv->nhiv", inverse, rhs_value, precision=highest)
    z_rows = jnp.einsum("nhij,nhjk->nhik", inverse, rhs_key, precision=highest)
    mixing = decay * jnp.einsum("nhik,nhjk->nhij", queries, key_rows, precision=highest)
    out_zero = jnp.einsum("nhij,nhjv->nhiv", mixing, u_zero, precision=highest)
    carry_q = head_decay[..., None] * queries - jnp.einsum(
        "nhij,nhjk->nhik", mixing, z_rows, precision=highest
    )
    weighted = tail_decay[..., None] * key_rows
    state_zero = jnp.einsum("nhcv,nhck->nhvk", u_zero, weighted, precision=highest)
    identity = jnp.eye(key_rows.shape[-1], dtype=jnp.float32)
    transfer = head_decay[..., size - 1][..., None, None] * identity - jnp.einsum(
        "nhck,nhcj->nhkj", z_rows, weighted, precision=highest
    )
    return (out_zero, carry_q, state_zero, transfer)


def run_blocks(out_zero, carry_q, state_zero, transfer, state_in):

    def advance(state, pieces):
        piece_out, piece_q, piece_state, piece_map = pieces
        result = piece_out + jnp.einsum("hck,hvk->hcv", piece_q, state, precision=highest)
        updated = jnp.einsum("hvk,hkj->hvj", state, piece_map, precision=highest) + piece_state
        return (updated, result)

    final, outputs = lax.scan(advance, state_in, (out_zero, carry_q, state_zero, transfer))
    return (outputs, final)


def segment_terms(query_f, key_f, value_f, logits, gate_log, starts):
    token_count, heads = logits.shape
    blocks = token_count // BLOCK

    def split(rows):
        return rows.reshape(blocks, BLOCK, heads, -1).transpose(0, 2, 1, 3)

    beta = jax.nn.sigmoid(logits).reshape(blocks, BLOCK, heads).transpose(0, 2, 1)
    gates = gate_log.reshape(heads, blocks, BLOCK).transpose(1, 0, 2)
    return block_terms(
        unit_rows(split(query_f)),
        unit_rows(split(key_f)),
        split(value_f),
        beta,
        gates,
        starts.reshape(blocks, BLOCK),
    )


def output_from_terms(terms, state_in):
    outputs, final = run_blocks(terms[0], terms[1], terms[2], terms[3], state_in)
    token_count = outputs.shape[0] * outputs.shape[2]
    return (outputs.transpose(0, 2, 1, 3).reshape(token_count, -1), final)


def segment_map(terms, zero_state):

    def compose_step(carry, pieces):
        linear, offset = carry
        piece_state, piece_map = pieces
        linear = jnp.einsum("hij,hjk->hik", linear, piece_map, precision=highest)
        offset = jnp.einsum("hvk,hkj->hvj", offset, piece_map, precision=highest) + piece_state
        return ((linear, offset), None)

    start_map = jnp.broadcast_to(jnp.eye(zero_state.shape[-1], dtype=jnp.float32), zero_state.shape)
    result, unused = lax.scan(compose_step, (start_map, zero_state), (terms[2], terms[3]))
    return result


def token_plan(row_lengths, positions):
    ends = jnp.cumsum(row_lengths)
    begins = ends - row_lengths
    starts = jnp.any(positions[:, None] == begins[None, :], axis=1).astype(jnp.float32)
    member = (
        (positions[:, None] >= begins[None, :]) & (positions[:, None] < ends[None, :])
    ).astype(jnp.float32)
    return (starts, member)


def advantages(rewards, prompts):
    same = (prompts[:, None] == prompts[None, :]).astype(jnp.float32)
    return rewards - jnp.sum(same * rewards[None, :], axis=1) / jnp.sum(same, axis=1)


def forward_chain(linear, offset, zero_state):

    def hop(step_index, incoming):
        outgoing = jnp.einsum("hvk,hkj->hvj", incoming, linear, precision=highest) + offset
        return from_behind(outgoing, "ctx", 1)

    return lax.fori_loop(0, lax.axis_size("ctx") - 1, hop, zero_state)


def backward_chain(linear, local_back, zero_state):
    flipped = jnp.swapaxes(linear, 1, 2)

    def back_hop(step_index, incoming):
        outgoing = jnp.einsum("hvk,hkj->hvj", incoming, flipped, precision=highest) + local_back
        return from_behind(outgoing, "ctx", -1)

    return lax.fori_loop(0, lax.axis_size("ctx") - 1, back_hop, zero_state)


def local(
    queries,
    key_rows,
    value_rows,
    hidden_in,
    beta_weight,
    log_gate,
    out_grad,
    lengths,
    rewards,
    prompts,
):
    token_count = queries.shape[0]
    heads = beta_weight.shape[1]
    width = queries.shape[1] // heads
    ctx_count = lax.axis_size("ctx")
    roll_count = lengths.shape[1]
    group_tokens = token_count * ctx_count
    positions = lax.axis_index("ctx") * token_count + jnp.arange(token_count, dtype=jnp.int32)
    starts, member = token_plan(lengths[0], positions)
    own_advantage = lax.dynamic_slice_in_dim(
        advantages(rewards, prompts), lax.axis_index("dp") * roll_count, roll_count
    )
    roll_weight = own_advantage * group_tokens / (roll_count * lengths[0].astype(jnp.float32))
    token_weight = jnp.sum(member * roll_weight[None, :], axis=-1)
    cotangent = out_grad.astype(jnp.float32) * token_weight[:, None]
    logits = jnp.dot(hidden_in, beta_weight, preferred_element_type=jnp.float32)
    query_f = queries.astype(jnp.float32)
    key_f = key_rows.astype(jnp.float32)
    value_f = value_rows.astype(jnp.float32)
    zero_state = jnp.zeros((heads, width, width), jnp.float32)

    def local_terms(a_rows, b_rows, c_rows, d_rows, e_rows):
        return segment_terms(a_rows, b_rows, c_rows, d_rows, e_rows, starts)

    terms, terms_back = jax.vjp(local_terms, query_f, key_f, value_f, logits, log_gate)
    linear, offset = segment_map(terms, zero_state)
    state_in = forward_chain(linear, offset, zero_state)
    unused, full_pull = jax.vjp(output_from_terms, terms, state_in)
    local_back = full_pull((cotangent, zero_state))[1]
    end_grad = backward_chain(linear, local_back, zero_state)
    term_grads = full_pull((cotangent, end_grad))[0]
    grads = terms_back(term_grads)
    logit_grad = grads[3]
    piece = hidden_in.astype(jnp.float32)
    beta_weight_grad = lax.psum_scatter(
        jnp.dot(piece.T, logit_grad, precision=highest, preferred_element_type=jnp.float32),
        ("dp", "ctx"),
        scatter_dimension=0,
        tiled=True,
    )
    return (
        grads[0].astype(jnp.bfloat16),
        grads[1].astype(jnp.bfloat16),
        grads[2].astype(jnp.bfloat16),
        grads[4],
        beta_weight_grad,
    )


def solution(mesh):
    in_specs = (
        P(("dp", "ctx"), None),
        P(("dp", "ctx"), None),
        P(("dp", "ctx"), None),
        P(("dp", "ctx"), None),
        P(),
        P(None, ("dp", "ctx")),
        P(("dp", "ctx"), None),
        P("dp", None),
        P(),
        P(),
    )
    out_specs = (
        P(("dp", "ctx"), None),
        P(("dp", "ctx"), None),
        P(("dp", "ctx"), None),
        P(None, ("dp", "ctx")),
        P(("dp", "ctx"), None),
    )
    return jax.shard_map(local, mesh=mesh, in_specs=in_specs, out_specs=out_specs, check_vma=False)
```

profile of v0, /device:TPU:1, one launch (start us, length us, event | category | flops | bytes accessed | tf_op | source)
XLA Modules:
  0.0 1245.1 jit_solution(14263243995911322668)
XLA Ops:
  40.8 7.1 fusion.95
  47.9 5.6 multiply_subtract_fusion
  56.5 13.0 %while.86 = (s32[]{:T(128)}, f32[16,128,128]{1,2,0:T(8,128)S(1)}, f32[16,128,128]{1,2,0:T(8,128)}, f32[2,16,128,128]{2,3,1,0:T(8,128)}, f32[2,16,128,128]{2,3,1,0:T(8,128)}, /*index=5*/s32[]{:T(128)}, s32[]{:T(128)}) while((s32[]{:T(128)}, f32[16,128,128]{1,2,0:T(8,128)S(1)}, f32[16,128,128]{1,2,0:T(8,128)}, ...), condition=%wide.region_6.7_spmd.clone, body=%wide.region_5.6_spmd.clone.sunk | while | flops 805830656 | bytes 19924088 | solution.py:113
  74.7 385.5 %while.83 = (s32[]{:T(128)}, f32[16,128,128]{2,1,0:T(8,128)}, f32[16,128,128]{2,1,0:T(8,128)}, f32[16,128,128]{2,1,0:T(8,128)}, s32[]{:T(128)}) while((s32[]{:T(128)}, f32[16,128,128]{2,1,0:T(8,128)}, f32[16,128,128]{2,1,0:T(8,128)}, f32[16,128,128]{2,1,0:T(8,128)}, s32[]{:T(128)}) %tuple.180), condition=%wide.region_16.17_spmd, body=%wide.region_15.16_spmd.sunk | while | flops 402915328 | bytes 8388709 | solution.py:138
  74.7 4.0 convolution_add_fusion.31
  78.7 5.0 collective-permute-start.1
  83.6 21.1 %collective-permute-done.1 = f32[16,128,128]{2,1,0:T(8,128)} collective-permute-done((f32[16,128,128]{2,1,0:T(8,128)}, f32[16,128,128]{2,1,0:T(8,128)}, u32[]{:S(2)}, u32[]{:S(2)}) %collective-permute-start.1) | collective-permute-done | bytes 1048608 | tf_op jit(solution)/shard_map/while/body/eval_jaxpr/ppermute | solution.py:15
  104.7 4.0 convolution_add_fusion.31
  108.7 5.1 collective-permute-start.1
  113.8 20.2 %collective-permute-done.1 = f32[16,128,128]{2,1,0:T(8,128)} collective-permute-done((f32[16,128,128]{2,1,0:T(8,128)}, f32[16,128,128]{2,1,0:T(8,128)}, u32[]{:S(2)}, u32[]{:S(2)}) %collective-permute-start.1) | collective-permute-done | bytes 1048608 | tf_op jit(solution)/shard_map/while/body/eval_jaxpr/ppermute | solution.py:15
  134.0 4.0 convolution_add_fusion.31
  138.0 5.1 collective-permute-start.1
  143.1 19.2 %collective-permute-done.1 = f32[16,128,128]{2,1,0:T(8,128)} collective-permute-done((f32[16,128,128]{2,1,0:T(8,128)}, f32[16,128,128]{2,1,0:T(8,128)}, u32[]{:S(2)}, u32[]{:S(2)}) %collective-permute-start.1) | collective-permute-done | bytes 1048608 | tf_op jit(solution)/shard_map/while/body/eval_jaxpr/ppermute | solution.py:15
  162.3 4.0 convolution_add_fusion.31
  166.3 5.1 collective-permute-start.1
  171.5 18.3 %collective-permute-done.1 = f32[16,128,128]{2,1,0:T(8,128)} collective-permute-done((f32[16,128,128]{2,1,0:T(8,128)}, f32[16,128,128]{2,1,0:T(8,128)}, u32[]{:S(2)}, u32[]{:S(2)}) %collective-permute-start.1) | collective-permute-done | bytes 1048608 | tf_op jit(solution)/shard_map/while/body/eval_jaxpr/ppermute | solution.py:15
  193.7 5.1 collective-permute-start.1
  198.9 17.4 %collective-permute-done.1 = f32[16,128,128]{2,1,0:T(8,128)} collective-permute-done((f32[16,128,128]{2,1,0:T(8,128)}, f32[16,128,128]{2,1,0:T(8,128)}, u32[]{:S(2)}, u32[]{:S(2)}) %collective-permute-start.1) | collective-permute-done | bytes 1048608 | tf_op jit(solution)/shard_map/while/body/eval_jaxpr/ppermute | solution.py:15
  220.2 6.4 collective-permute-start.1
  226.7 16.5 %collective-permute-done.1 = f32[16,128,128]{2,1,0:T(8,128)} collective-permute-done((f32[16,128,128]{2,1,0:T(8,128)}, f32[16,128,128]{2,1,0:T(8,128)}, u32[]{:S(2)}, u32[]{:S(2)}) %collective-permute-start.1) | collective-permute-done | bytes 1048608 | tf_op jit(solution)/shard_map/while/body/eval_jaxpr/ppermute | solution.py:15
  247.1 7.3 collective-permute-start.1
  254.4 15.5 %collective-permute-done.1 = f32[16,128,128]{2,1,0:T(8,128)} collective-permute-done((f32[16,128,128]{2,1,0:T(8,128)}, f32[16,128,128]{2,1,0:T(8,128)}, u32[]{:S(2)}, u32[]{:S(2)}) %collective-permute-start.1) | collective-permute-done | bytes 1048608 | tf_op jit(solution)/shard_map/while/body/eval_jaxpr/ppermute | solution.py:15
  273.9 7.3 collective-permute-start.1
  281.2 14.6 %collective-permute-done.1 = f32[16,128,128]{2,1,0:T(8,128)} collective-permute-done((f32[16,128,128]{2,1,0:T(8,128)}, f32[16,128,128]{2,1,0:T(8,128)}, u32[]{:S(2)}, u32[]{:S(2)}) %collective-permute-start.1) | collective-permute-done | bytes 1048608 | tf_op jit(solution)/shard_map/while/body/eval_jaxpr/ppermute | solution.py:15
  299.7 7.3 collective-permute-start.1
  307.0 13.7 %collective-permute-done.1 = f32[16,128,128]{2,1,0:T(8,128)} collective-permute-done((f32[16,128,128]{2,1,0:T(8,128)}, f32[16,128,128]{2,1,0:T(8,128)}, u32[]{:S(2)}, u32[]{:S(2)}) %collective-permute-start.1) | collective-permute-done | bytes 1048608 | tf_op jit(solution)/shard_map/while/body/eval_jaxpr/ppermute | solution.py:15
  324.7 7.3 collective-permute-start.1
  331.9 12.8 %collective-permute-done.1 = f32[16,128,128]{2,1,0:T(8,128)} collective-permute-done((f32[16,128,128]{2,1,0:T(8,128)}, f32[16,128,128]{2,1,0:T(8,128)}, u32[]{:S(2)}, u32[]{:S(2)}) %collective-permute-start.1) | collective-permute-done | bytes 1048608 | tf_op jit(solution)/shard_map/while/body/eval_jaxpr/ppermute | solution.py:15
  348.7 7.3 collective-permute-start.1
  355.9 11.9 collective-permute-done.1
  371.8 7.3 collective-permute-start.1
  379.0 11.0 collective-permute-done.1
  394.0 7.3 collective-permute-start.1
  401.3 11.2 collective-permute-done.1
  416.5 7.3 collective-permute-start.1
  423.7 12.0 collective-permute-done.1
  439.7 7.3 collective-permute-start.1
  447.0 12.8 %collective-permute-done.1 = f32[16,128,128]{2,1,0:T(8,128)} collective-permute-done((f32[16,128,128]{2,1,0:T(8,128)}, f32[16,128,128]{2,1,0:T(8,128)}, u32[]{:S(2)}, u32[]{:S(2)}) %collective-permute-start.1) | collective-permute-done | bytes 1048608 | tf_op jit(solution)/shard_map/while/body/eval_jaxpr/ppermute | solution.py:15
  464.3 9.8 while.84
  486.0 11.2 while.87
  500.9 440.0 %while.82 = (s32[]{:T(128)}, f32[16,128,128]{2,1,0:T(8,128)}, f32[16,128,128]{2,1,0:T(8,128)S(1)}, f32[16,128,128]{2,1,0:T(8,128)}, s32[]{:T(128)}) while((s32[]{:T(128)}, f32[16,128,128]{2,1,0:T(8,128)}, f32[16,128,128]{2,1,0:T(8,128)S(1)}, f32[16,128,128]{2,1,0:T(8,128)}, s32[]{:T(128)}) %tuple.192), condition=%wide.region_14.15_spmd, body=%wide.region_13.14_spmd.sunk | while | flops 402915328 | bytes 8388709 | solution.py:148
  506.0 18.0 %collective-permute-done = f32[16,128,128]{2,1,0:T(8,128)} collective-permute-done((f32[16,128,128]{2,1,0:T(8,128)}, f32[16,128,128]{2,1,0:T(8,128)}, u32[]{:S(2)}, u32[]{:S(2)}) %collective-permute-start) | collective-permute-done | bytes 1048608 | tf_op jit(solution)/shard_map/while/body/eval_jaxpr/ppermute | solution.py:15
  529.0 21.2 %collective-permute-done = f32[16,128,128]{2,1,0:T(8,128)} collective-permute-done((f32[16,128,128]{2,1,0:T(8,128)}, f32[16,128,128]{2,1,0:T(8,128)}, u32[]{:S(2)}, u32[]{:S(2)}) %collective-permute-start) | collective-permute-done | bytes 1048608 | tf_op jit(solution)/shard_map/while/body/eval_jaxpr/ppermute | solution.py:15
  555.3 22.3 %collective-permute-done = f32[16,128,128]{2,1,0:T(8,128)} collective-permute-done((f32[16,128,128]{2,1,0:T(8,128)}, f32[16,128,128]{2,1,0:T(8,128)}, u32[]{:S(2)}, u32[]{:S(2)}) %collective-permute-start) | collective-permute-done | bytes 1048608 | tf_op jit(solution)/shard_map/while/body/eval_jaxpr/ppermute | solution.py:15
  582.7 23.4 %collective-permute-done = f32[16,128,128]{2,1,0:T(8,128)} collective-permute-done((f32[16,128,128]{2,1,0:T(8,128)}, f32[16,128,128]{2,1,0:T(8,128)}, u32[]{:S(2)}, u32[]{:S(2)}) %collective-permute-start) | collective-permute-done | bytes 1048608 | tf_op jit(solution)/shard_map/while/body/eval_jaxpr/ppermute | solution.py:15
  611.2 26.2 %collective-permute-done = f32[16,128,128]{2,1,0:T(8,128)} collective-permute-done((f32[16,128,128]{2,1,0:T(8,128)}, f32[16,128,128]{2,1,0:T(8,128)}, u32[]{:S(2)}, u32[]{:S(2)}) %collective-permute-start) | collective-permute-done | bytes 1048608 | tf_op jit(solution)/shard_map/while/body/eval_jaxpr/ppermute | solution.py:15
  642.4 27.0 %collective-permute-done = f32[16,128,128]{2,1,0:T(8,128)} collective-permute-done((f32[16,128,128]{2,1,0:T(8,128)}, f32[16,128,128]{2,1,0:T(8,128)}, u32[]{:S(2)}, u32[]{:S(2)}) %collective-permute-start) | collective-permute-done | bytes 1048608 | tf_op jit(solution)/shard_map/while/body/eval_jaxpr/ppermute | solution.py:15
  674.4 27.2 %collective-permute-done = f32[16,128,128]{2,1,0:T(8,128)} collective-permute-done((f32[16,128,128]{2,1,0:T(8,128)}, f32[16,128,128]{2,1,0:T(8,128)}, u32[]{:S(2)}, u32[]{:S(2)}) %collective-permute-start) | collective-permute-done | bytes 1048608 | tf_op jit(solution)/shard_map/while/body/eval_jaxpr/ppermute | solution.py:15
  706.7 28.3 %collective-permute-done = f32[16,128,128]{2,1,0:T(8,128)} collective-permute-done((f32[16,128,128]{2,1,0:T(8,128)}, f32[16,128,128]{2,1,0:T(8,128)}, u32[]{:S(2)}, u32[]{:S(2)}) %collective-permute-start) | collective-permute-done | bytes 1048608 | tf_op jit(solution)/shard_map/while/body/eval_jaxpr/ppermute | solution.py:15
  740.1 29.1 %collective-permute-done = f32[16,128,128]{2,1,0:T(8,128)} collective-permute-done((f32[16,128,128]{2,1,0:T(8,128)}, f32[16,128,128]{2,1,0:T(8,128)}, u32[]{:S(2)}, u32[]{:S(2)}) %collective-permute-start) | collective-permute-done | bytes 1048608 | tf_op jit(solution)/shard_map/while/body/eval_jaxpr/ppermute | solution.py:15
  774.3 26.3 %collective-permute-done = f32[16,128,128]{2,1,0:T(8,128)} collective-permute-done((f32[16,128,128]{2,1,0:T(8,128)}, f32[16,128,128]{2,1,0:T(8,128)}, u32[]{:S(2)}, u32[]{:S(2)}) %collective-permute-start) | collective-permute-done | bytes 1048608 | tf_op jit(solution)/shard_map/while/body/eval_jaxpr/ppermute | solution.py:15
  805.6 25.0 %collective-permute-done = f32[16,128,128]{2,1,0:T(8,128)} collective-permute-done((f32[16,128,128]{2,1,0:T(8,128)}, f32[16,128,128]{2,1,0:T(8,128)}, u32[]{:S(2)}, u32[]{:S(2)}) %collective-permute-start) | collective-permute-done | bytes 1048608 | tf_op jit(solution)/shard_map/while/body/eval_jaxpr/ppermute | solution.py:15
  835.6 23.8 %collective-permute-done = f32[16,128,128]{2,1,0:T(8,128)} collective-permute-done((f32[16,128,128]{2,1,0:T(8,128)}, f32[16,128,128]{2,1,0:T(8,128)}, u32[]{:S(2)}, u32[]{:S(2)}) %collective-permute-start) | collective-permute-done | bytes 1048608 | tf_op jit(solution)/shard_map/while/body/eval_jaxpr/ppermute | solution.py:15
  864.5 23.0 %collective-permute-done = f32[16,128,128]{2,1,0:T(8,128)} collective-permute-done((f32[16,128,128]{2,1,0:T(8,128)}, f32[16,128,128]{2,1,0:T(8,128)}, u32[]{:S(2)}, u32[]{:S(2)}) %collective-permute-start) | collective-permute-done | bytes 1048608 | tf_op jit(solution)/shard_map/while/body/eval_jaxpr/ppermute | solution.py:15
  892.6 22.1 %collective-permute-done = f32[16,128,128]{2,1,0:T(8,128)} collective-permute-done((f32[16,128,128]{2,1,0:T(8,128)}, f32[16,128,128]{2,1,0:T(8,128)}, u32[]{:S(2)}, u32[]{:S(2)}) %collective-permute-start) | collective-permute-done | bytes 1048608 | tf_op jit(solution)/shard_map/while/body/eval_jaxpr/ppermute | solution.py:15
  919.7 21.2 %collective-permute-done = f32[16,128,128]{2,1,0:T(8,128)} collective-permute-done((f32[16,128,128]{2,1,0:T(8,128)}, f32[16,128,128]{2,1,0:T(8,128)}, u32[]{:S(2)}, u32[]{:S(2)}) %collective-permute-start) | collective-permute-done | bytes 1048608 | tf_op jit(solution)/shard_map/while/body/eval_jaxpr/ppermute | solution.py:15
  948.0 26.4 %while.85 = (s32[]{:T(128)}, f32[16,128,128]{1,2,0:T(8,128)S(1)}, f32[2,16,64,128]{3,2,1,0:T(8,128)}, f32[2,16,64,128]{3,2,1,0:T(8,128)}, f32[2,16,128,128]{2,3,...) while((s32[]{:T(128)}, f32[16,128,128]{1,2,0:T(8,128)S(1)}, ...), condition=%wide.region_20.21_spmd, body=%wide.region_19.20_spmd.sunk | while | flops 1208221696 | bytes 65015652 | solution.py:74
  948.0 4.7 fusion.299
  961.1 4.6 fusion.299
  974.3 6.2 fusion.167
  984.6 4.2 fusion.55
  1051.9 4.4 multiply_reduce_fusion.1
  1059.3 5.7 multiply_reduce_fusion.4
  1077.5 158.9 %all-reduce.5.cloned.1.call-done = f32[2304,16]{0,1:T(8,128)} async-done(((f32[2304,16]{0,1:T(8,128)}), f32[2304,16]{0,1:T(8,128)}) %all-reduce.5.cloned.1.call-update) | async-done | bytes 147472
  (361 shorter events, 321.4 us)
Async XLA Ops:
  7.2 2.9 copy-start
  7.2 1229.2 %all-reduce.5.cloned.1.call-start = ((), (), s32[]{:S(2)}) async-start(), calls=%async_computation | async-start | bytes 294912
  16.1 4.2 copy-start.23
  19.1 3.5 copy-start.28
  20.3 3.4 copy-start.8
  22.5 3.1 copy-start.61
  23.7 3.1 copy-start.10
  25.6 3.5 copy-start.48
  26.8 3.4 copy-start.12
  29.1 3.1 copy-start.50
  30.3 2.9 copy-start.46
  35.1 3.2 copy-start.25
  40.7 7.2 copy-start.20
  78.7 26.1 %collective-permute-start.1 = (f32[16,128,128]{2,1,0:T(8,128)}, f32[16,128,128]{2,1,0:T(8,128)}, u32[]{:S(2)}, u32[]{:S(2)}) collective-permute-start(f32[16,128,128]{2,1,0:T(8,128)} %convolution_add_fusion.31), channel_id=1, source_target_pairs={{0,1},{1,2},{2,3},{3,4},{4,5},{5,6},{6,7},{7,8},{8,9},{9,10},{10,1... | collective-permute-start | bytes 3145736 | tf_op jit(solution)/shard_map/while/body/eval_jaxpr/ppermute | solution.py:15
  108.7 25.3 %collective-permute-start.1 = (f32[16,128,128]{2,1,0:T(8,128)}, f32[16,128,128]{2,1,0:T(8,128)}, u32[]{:S(2)}, u32[]{:S(2)}) collective-permute-start(f32[16,128,128]{2,1,0:T(8,128)} %convolution_add_fusion.31), channel_id=1, source_target_pairs={{0,1},{1,2},{2,3},{3,4},{4,5},{5,6},{6,7},{7,8},{8,9},{9,10},{10,1... | collective-permute-start | bytes 3145736 | tf_op jit(solution)/shard_map/while/body/eval_jaxpr/ppermute | solution.py:15
  138.0 24.4 %collective-permute-start.1 = (f32[16,128,128]{2,1,0:T(8,128)}, f32[16,128,128]{2,1,0:T(8,128)}, u32[]{:S(2)}, u32[]{:S(2)}) collective-permute-start(f32[16,128,128]{2,1,0:T(8,128)} %convolution_add_fusion.31), channel_id=1, source_target_pairs={{0,1},{1,2},{2,3},{3,4},{4,5},{5,6},{6,7},{7,8},{8,9},{9,10},{10,1... | collective-permute-start | bytes 3145736 | tf_op jit(solution)/shard_map/while/body/eval_jaxpr/ppermute | solution.py:15
  166.3 23.5 %collective-permute-start.1 = (f32[16,128,128]{2,1,0:T(8,128)}, f32[16,128,128]{2,1,0:T(8,128)}, u32[]{:S(2)}, u32[]{:S(2)}) collective-permute-start(f32[16,128,128]{2,1,0:T(8,128)} %convolution_add_fusion.31), channel_id=1, source_target_pairs={{0,1},{1,2},{2,3},{3,4},{4,5},{5,6},{6,7},{7,8},{8,9},{9,10},{10,1... | collective-permute-start | bytes 3145736 | tf_op jit(solution)/shard_map/while/body/eval_jaxpr/ppermute | solution.py:15
  193.7 22.5 %collective-permute-start.1 = (f32[16,128,128]{2,1,0:T(8,128)}, f32[16,128,128]{2,1,0:T(8,128)}, u32[]{:S(2)}, u32[]{:S(2)}) collective-permute-start(f32[16,128,128]{2,1,0:T(8,128)} %convolution_add_fusion.31), channel_id=1, source_target_pairs={{0,1},{1,2},{2,3},{3,4},{4,5},{5,6},{6,7},{7,8},{8,9},{9,10},{10,1... | collective-permute-start | bytes 3145736 | tf_op jit(solution)/shard_map/while/body/eval_jaxpr/ppermute | solution.py:15
  220.2 22.9 %collective-permute-start.1 = (f32[16,128,128]{2,1,0:T(8,128)}, f32[16,128,128]{2,1,0:T(8,128)}, u32[]{:S(2)}, u32[]{:S(2)}) collective-permute-start(f32[16,128,128]{2,1,0:T(8,128)} %convolution_add_fusion.31), channel_id=1, source_target_pairs={{0,1},{1,2},{2,3},{3,4},{4,5},{5,6},{6,7},{7,8},{8,9},{9,10},{10,1... | collective-permute-start | bytes 3145736 | tf_op jit(solution)/shard_map/while/body/eval_jaxpr/ppermute | solution.py:15
  247.1 22.8 %collective-permute-start.1 = (f32[16,128,128]{2,1,0:T(8,128)}, f32[16,128,128]{2,1,0:T(8,128)}, u32[]{:S(2)}, u32[]{:S(2)}) collective-permute-start(f32[16,128,128]{2,1,0:T(8,128)} %convolution_add_fusion.31), channel_id=1, source_target_pairs={{0,1},{1,2},{2,3},{3,4},{4,5},{5,6},{6,7},{7,8},{8,9},{9,10},{10,1... | collective-permute-start | bytes 3145736 | tf_op jit(solution)/shard_map/while/body/eval_jaxpr/ppermute | solution.py:15
  273.9 21.9 %collective-permute-start.1 = (f32[16,128,128]{2,1,0:T(8,128)}, f32[16,128,128]{2,1,0:T(8,128)}, u32[]{:S(2)}, u32[]{:S(2)}) collective-permute-start(f32[16,128,128]{2,1,0:T(8,128)} %convolution_add_fusion.31), channel_id=1, source_target_pairs={{0,1},{1,2},{2,3},{3,4},{4,5},{5,6},{6,7},{7,8},{8,9},{9,10},{10,1... | collective-permute-start | bytes 3145736 | tf_op jit(solution)/shard_map/while/body/eval_jaxpr/ppermute | solution.py:15
  299.7 21.0 %collective-permute-start.1 = (f32[16,128,128]{2,1,0:T(8,128)}, f32[16,128,128]{2,1,0:T(8,128)}, u32[]{:S(2)}, u32[]{:S(2)}) collective-permute-start(f32[16,128,128]{2,1,0:T(8,128)} %convolution_add_fusion.31), channel_id=1, source_target_pairs={{0,1},{1,2},{2,3},{3,4},{4,5},{5,6},{6,7},{7,8},{8,9},{9,10},{10,1... | collective-permute-start | bytes 3145736 | tf_op jit(solution)/shard_map/while/body/eval_jaxpr/ppermute | solution.py:15
  324.7 20.0 %collective-permute-start.1 = (f32[16,128,128]{2,1,0:T(8,128)}, f32[16,128,128]{2,1,0:T(8,128)}, u32[]{:S(2)}, u32[]{:S(2)}) collective-permute-start(f32[16,128,128]{2,1,0:T(8,128)} %convolution_add_fusion.31), channel_id=1, source_target_pairs={{0,1},{1,2},{2,3},{3,4},{4,5},{5,6},{6,7},{7,8},{8,9},{9,10},{10,1... | collective-permute-start | bytes 3145736 | tf_op jit(solution)/shard_map/while/body/eval_jaxpr/ppermute | solution.py:15
  348.7 19.1 %collective-permute-start.1 = (f32[16,128,128]{2,1,0:T(8,128)}, f32[16,128,128]{2,1,0:T(8,128)}, u32[]{:S(2)}, u32[]{:S(2)}) collective-permute-start(f32[16,128,128]{2,1,0:T(8,128)} %convolution_add_fusion.31), channel_id=1, source_target_pairs={{0,1},{1,2},{2,3},{3,4},{4,5},{5,6},{6,7},{7,8},{8,9},{9,10},{10,1... | collective-permute-start | bytes 3145736 | tf_op jit(solution)/shard_map/while/body/eval_jaxpr/ppermute | solution.py:15
  371.8 18.3 %collective-permute-start.1 = (f32[16,128,128]{2,1,0:T(8,128)}, f32[16,128,128]{2,1,0:T(8,128)}, u32[]{:S(2)}, u32[]{:S(2)}) collective-permute-start(f32[16,128,128]{2,1,0:T(8,128)} %convolution_add_fusion.31), channel_id=1, source_target_pairs={{0,1},{1,2},{2,3},{3,4},{4,5},{5,6},{6,7},{7,8},{8,9},{9,10},{10,1... | collective-permute-start | bytes 3145736 | tf_op jit(solution)/shard_map/while/body/eval_jaxpr/ppermute | solution.py:15
  394.0 18.5 %collective-permute-start.1 = (f32[16,128,128]{2,1,0:T(8,128)}, f32[16,128,128]{2,1,0:T(8,128)}, u32[]{:S(2)}, u32[]{:S(2)}) collective-permute-start(f32[16,128,128]{2,1,0:T(8,128)} %convolution_add_fusion.31), channel_id=1, source_target_pairs={{0,1},{1,2},{2,3},{3,4},{4,5},{5,6},{6,7},{7,8},{8,9},{9,10},{10,1... | collective-permute-start | bytes 3145736 | tf_op jit(solution)/shard_map/while/body/eval_jaxpr/ppermute | solution.py:15
  416.5 19.3 %collective-permute-start.1 = (f32[16,128,128]{2,1,0:T(8,128)}, f32[16,128,128]{2,1,0:T(8,128)}, u32[]{:S(2)}, u32[]{:S(2)}) collective-permute-start(f32[16,128,128]{2,1,0:T(8,128)} %convolution_add_fusion.31), channel_id=1, source_target_pairs={{0,1},{1,2},{2,3},{3,4},{4,5},{5,6},{6,7},{7,8},{8,9},{9,10},{10,1... | collective-permute-start | bytes 3145736 | tf_op jit(solution)/shard_map/while/body/eval_jaxpr/ppermute | solution.py:15
  439.7 20.1 %collective-permute-start.1 = (f32[16,128,128]{2,1,0:T(8,128)}, f32[16,128,128]{2,1,0:T(8,128)}, u32[]{:S(2)}, u32[]{:S(2)}) collective-permute-start(f32[16,128,128]{2,1,0:T(8,128)} %convolution_add_fusion.31), channel_id=1, source_target_pairs={{0,1},{1,2},{2,3},{3,4},{4,5},{5,6},{6,7},{7,8},{8,9},{9,10},{10,1... | collective-permute-start | bytes 3145736 | tf_op jit(solution)/shard_map/while/body/eval_jaxpr/ppermute | solution.py:15
  475.5 3.8 copy-start.21
  479.3 3.6 copy-start.65
  479.3 3.6 copy-start.66
  479.3 3.8 copy-start.67
  491.5 2.8 copy-start.3
  491.5 2.9 copy-start.16
  504.7 19.3 %collective-permute-start = (f32[16,128,128]{2,1,0:T(8,128)}, f32[16,128,128]{2,1,0:T(8,128)}, u32[]{:S(2)}, u32[]{:S(2)}) collective-permute-start(f32[16,128,128]{2,1,0:T(8,128)} %convolution_add_fusion.30), channel_id=1, source_target_pairs={{1,0},{2,1},{3,2},{4,3},{5,4},{6,5},{7,6},{8,7},{9,8},{10,9},{11,1... | collective-permute-start | bytes 3145736 | tf_op jit(solution)/shard_map/while/body/eval_jaxpr/ppermute | solution.py:15
  527.7 22.5 %collective-permute-start = (f32[16,128,128]{2,1,0:T(8,128)}, f32[16,128,128]{2,1,0:T(8,128)}, u32[]{:S(2)}, u32[]{:S(2)}) collective-permute-start(f32[16,128,128]{2,1,0:T(8,128)} %convolution_add_fusion.30), channel_id=1, source_target_pairs={{1,0},{2,1},{3,2},{4,3},{5,4},{6,5},{7,6},{8,7},{9,8},{10,9},{11,1... | collective-permute-start | bytes 3145736 | tf_op jit(solution)/shard_map/while/body/eval_jaxpr/ppermute | solution.py:15
  554.0 23.6 %collective-permute-start = (f32[16,128,128]{2,1,0:T(8,128)}, f32[16,128,128]{2,1,0:T(8,128)}, u32[]{:S(2)}, u32[]{:S(2)}) collective-permute-start(f32[16,128,128]{2,1,0:T(8,128)} %convolution_add_fusion.30), channel_id=1, source_target_pairs={{1,0},{2,1},{3,2},{4,3},{5,4},{6,5},{7,6},{8,7},{9,8},{10,9},{11,1... | collective-permute-start | bytes 3145736 | tf_op jit(solution)/shard_map/while/body/eval_jaxpr/ppermute | solution.py:15
  581.4 24.7 %collective-permute-start = (f32[16,128,128]{2,1,0:T(8,128)}, f32[16,128,128]{2,1,0:T(8,128)}, u32[]{:S(2)}, u32[]{:S(2)}) collective-permute-start(f32[16,128,128]{2,1,0:T(8,128)} %convolution_add_fusion.30), channel_id=1, source_target_pairs={{1,0},{2,1},{3,2},{4,3},{5,4},{6,5},{7,6},{8,7},{9,8},{10,9},{11,1... | collective-permute-start | bytes 3145736 | tf_op jit(solution)/shard_map/while/body/eval_jaxpr/ppermute | solution.py:15
  609.9 27.5 %collective-permute-start = (f32[16,128,128]{2,1,0:T(8,128)}, f32[16,128,128]{2,1,0:T(8,128)}, u32[]{:S(2)}, u32[]{:S(2)}) collective-permute-start(f32[16,128,128]{2,1,0:T(8,128)} %convolution_add_fusion.30), channel_id=1, source_target_pairs={{1,0},{2,1},{3,2},{4,3},{5,4},{6,5},{7,6},{8,7},{9,8},{10,9},{11,1... | collective-permute-start | bytes 3145736 | tf_op jit(solution)/shard_map/while/body/eval_jaxpr/ppermute | solution.py:15
  641.1 28.3 %collective-permute-start = (f32[16,128,128]{2,1,0:T(8,128)}, f32[16,128,128]{2,1,0:T(8,128)}, u32[]{:S(2)}, u32[]{:S(2)}) collective-permute-start(f32[16,128,128]{2,1,0:T(8,128)} %convolution_add_fusion.30), channel_id=1, source_target_pairs={{1,0},{2,1},{3,2},{4,3},{5,4},{6,5},{7,6},{8,7},{9,8},{10,9},{11,1... | collective-permute-start | bytes 3145736 | tf_op jit(solution)/shard_map/while/body/eval_jaxpr/ppermute | solution.py:15
  673.2 28.5 %collective-permute-start = (f32[16,128,128]{2,1,0:T(8,128)}, f32[16,128,128]{2,1,0:T(8,128)}, u32[]{:S(2)}, u32[]{:S(2)}) collective-permute-start(f32[16,128,128]{2,1,0:T(8,128)} %convolution_add_fusion.30), channel_id=1, source_target_pairs={{1,0},{2,1},{3,2},{4,3},{5,4},{6,5},{7,6},{8,7},{9,8},{10,9},{11,1... | collective-permute-start | bytes 3145736 | tf_op jit(solution)/shard_map/while/body/eval_jaxpr/ppermute | solution.py:15
  705.4 29.6 %collective-permute-start = (f32[16,128,128]{2,1,0:T(8,128)}, f32[16,128,128]{2,1,0:T(8,128)}, u32[]{:S(2)}, u32[]{:S(2)}) collective-permute-start(f32[16,128,128]{2,1,0:T(8,128)} %convolution_add_fusion.30), channel_id=1, source_target_pairs={{1,0},{2,1},{3,2},{4,3},{5,4},{6,5},{7,6},{8,7},{9,8},{10,9},{11,1... | collective-permute-start | bytes 3145736 | tf_op jit(solution)/shard_map/while/body/eval_jaxpr/ppermute | solution.py:15
  738.8 30.4 %collective-permute-start = (f32[16,128,128]{2,1,0:T(8,128)}, f32[16,128,128]{2,1,0:T(8,128)}, u32[]{:S(2)}, u32[]{:S(2)}) collective-permute-start(f32[16,128,128]{2,1,0:T(8,128)} %convolution_add_fusion.30), channel_id=1, source_target_pairs={{1,0},{2,1},{3,2},{4,3},{5,4},{6,5},{7,6},{8,7},{9,8},{10,9},{11,1... | collective-permute-start | bytes 3145736 | tf_op jit(solution)/shard_map/while/body/eval_jaxpr/ppermute | solution.py:15
  773.0 27.6 %collective-permute-start = (f32[16,128,128]{2,1,0:T(8,128)}, f32[16,128,128]{2,1,0:T(8,128)}, u32[]{:S(2)}, u32[]{:S(2)}) collective-permute-start(f32[16,128,128]{2,1,0:T(8,128)} %convolution_add_fusion.30), channel_id=1, source_target_pairs={{1,0},{2,1},{3,2},{4,3},{5,4},{6,5},{7,6},{8,7},{9,8},{10,9},{11,1... | collective-permute-start | bytes 3145736 | tf_op jit(solution)/shard_map/while/body/eval_jaxpr/ppermute | solution.py:15
  804.3 26.2 %collective-permute-start = (f32[16,128,128]{2,1,0:T(8,128)}, f32[16,128,128]{2,1,0:T(8,128)}, u32[]{:S(2)}, u32[]{:S(2)}) collective-permute-start(f32[16,128,128]{2,1,0:T(8,128)} %convolution_add_fusion.30), channel_id=1, source_target_pairs={{1,0},{2,1},{3,2},{4,3},{5,4},{6,5},{7,6},{8,7},{9,8},{10,9},{11,1... | collective-permute-start | bytes 3145736 | tf_op jit(solution)/shard_map/while/body/eval_jaxpr/ppermute | solution.py:15
  834.3 25.1 %collective-permute-start = (f32[16,128,128]{2,1,0:T(8,128)}, f32[16,128,128]{2,1,0:T(8,128)}, u32[]{:S(2)}, u32[]{:S(2)}) collective-permute-start(f32[16,128,128]{2,1,0:T(8,128)} %convolution_add_fusion.30), channel_id=1, source_target_pairs={{1,0},{2,1},{3,2},{4,3},{5,4},{6,5},{7,6},{8,7},{9,8},{10,9},{11,1... | collective-permute-start | bytes 3145736 | tf_op jit(solution)/shard_map/while/body/eval_jaxpr/ppermute | solution.py:15
  863.2 24.3 %collective-permute-start = (f32[16,128,128]{2,1,0:T(8,128)}, f32[16,128,128]{2,1,0:T(8,128)}, u32[]{:S(2)}, u32[]{:S(2)}) collective-permute-start(f32[16,128,128]{2,1,0:T(8,128)} %convolution_add_fusion.30), channel_id=1, source_target_pairs={{1,0},{2,1},{3,2},{4,3},{5,4},{6,5},{7,6},{8,7},{9,8},{10,9},{11,1... | collective-permute-start | bytes 3145736 | tf_op jit(solution)/shard_map/while/body/eval_jaxpr/ppermute | solution.py:15
  891.3 23.4 %collective-permute-start = (f32[16,128,128]{2,1,0:T(8,128)}, f32[16,128,128]{2,1,0:T(8,128)}, u32[]{:S(2)}, u32[]{:S(2)}) collective-permute-start(f32[16,128,128]{2,1,0:T(8,128)} %convolution_add_fusion.30), channel_id=1, source_target_pairs={{1,0},{2,1},{3,2},{4,3},{5,4},{6,5},{7,6},{8,7},{9,8},{10,9},{11,1... | collective-permute-start | bytes 3145736 | tf_op jit(solution)/shard_map/while/body/eval_jaxpr/ppermute | solution.py:15
  918.4 22.5 %collective-permute-start = (f32[16,128,128]{2,1,0:T(8,128)}, f32[16,128,128]{2,1,0:T(8,128)}, u32[]{:S(2)}, u32[]{:S(2)}) collective-permute-start(f32[16,128,128]{2,1,0:T(8,128)} %convolution_add_fusion.30), channel_id=1, source_target_pairs={{1,0},{2,1},{3,2},{4,3},{5,4},{6,5},{7,6},{8,7},{9,8},{10,9},{11,1... | collective-permute-start | bytes 3145736 | tf_op jit(solution)/shard_map/while/body/eval_jaxpr/ppermute | solution.py:15
  948.0 4.7 copy-start.5
  954.3 4.9 copy-start.33
  961.1 4.6 copy-start.5
  967.4 4.9 copy-start.33
  974.3 6.2 copy-start.34
  991.0 3.0 copy-start.40
  1032.2 4.6 copy-start.35
  1034.0 12.9 %copy-start.54 = (f32[2,16,64,128]{3,2,1,0:T(8,128)}, f32[2,16,64,128]{3,2,1,0:T(8,128)S(1)}, u32[]{:S(2)}) copy-start(f32[2,16,64,128]{3,2,1,0:T(8,128)S(1)} %fusion.102) | copy-start | bytes 3145732
  1036.8 10.2 copy-start.56
  1040.7 6.3 copy-start.58
  1040.7 4.4 copy-start.15
  1047.0 3.5 copy-start.59
  1051.9 4.4 copy-start.27
  1051.9 4.4 copy-start.53
  1059.2 5.8 copy-start.19
  (48 other events, 96.3 us)
Sparse Core Ops, SparseCore 0:
  1059.4 176.9 all-reduce.4
where the time goes:
time: 1260 us; the launch traced here: 1250 us
  waiting for transfers between devices  751 us (60%)
  matrix products  287 us (23%)
  starting transfers between devices  117 us (9%)
  local copies, waits for them, and re-layouts  54 us (4%)
  other arithmetic  19.2 us (2%)
  between operations  15.7 us (1%)
    ppermute x30, waiting for transfers between devices, from_behind(): return lax.ppermute(x, axis, pairs)  592 us
    unnamed x2, waiting for transfers between devices  159 us
    ppermute x30, starting transfers between devices, from_behind(): return lax.ppermute(x, axis, pairs)  117 us
    dot_general x15, matrix products, hop(): jnp.einsum('hvk,hkj->hvj', incoming, linear, precision=highest) + offset  59.6 us
    dot_general x15, matrix products, back_hop(): jnp.einsum('hvk,hkj->hvj', incoming, flipped, precision=highest)  56.6 us
    dot_general x15, matrix products, unit_inverse(): power = jnp.einsum('nhij,nhjk->nhik', power, power, precision=highest)  27.1 us
    dot_general x15, matrix products, unit_inverse(): jnp.einsum('nhij,nhjk->nhik', total, power, precision=highest)  25.7 us
  transfers between devices with their start and end apart: 31, of which 31 were waited for; matrix products, arithmetic and copies ran while one was open for 1% of the time, Pallas kernels for 0%

commit v1 on v0

--- a/solution.py
+++ b/solution.py
@@ -34,8 +34,9 @@
     size = queries.shape[2]
     row_ids = lax.broadcasted_iota(jnp.int32, (size, size), 0)
     col_ids = lax.broadcasted_iota(jnp.int32, (size, size), 1)
-    gamma = jnp.cumsum(gate_log, axis=-1)
-    count = jnp.cumsum(starts, axis=-1)
+    upto = (row_ids <= col_ids).astype(jnp.float32)
+    gamma = jnp.einsum("nhi,ij->nhj", gate_log, upto, precision=highest)
+    count = jnp.einsum("ni,ij->nj", starts, upto, precision=highest)
     linked = (count[:, :, None] == count[:, None, :]) & (row_ids >= col_ids)
     linked = linked[:, None, :, :]
     spread = gamma[..., :, None] - gamma[..., None, :]
@@ -115,7 +116,8 @@
 
 
 def token_plan(row_lengths, positions):
-    ends = jnp.cumsum(row_lengths)
+    slots = jnp.arange(row_lengths.shape[0])
+    ends = jnp.sum(jnp.where(slots[:, None] <= slots[None, :], row_lengths[:, None], 0), axis=0)
     begins = ends - row_lengths
     starts = jnp.any(positions[:, None] == begins[None, :], axis=1).astype(jnp.float32)
     member = (
@@ -129,23 +131,20 @@
     return rewards - jnp.sum(same * rewards[None, :], axis=1) / jnp.sum(same, axis=1)
 
 
-def forward_chain(linear, offset, zero_state):
-
-    def hop(step_index, incoming):
-        outgoing = jnp.einsum("hvk,hkj->hvj", incoming, linear, precision=highest) + offset
-        return from_behind(outgoing, "ctx", 1)
-
-    return lax.fori_loop(0, lax.axis_size("ctx") - 1, hop, zero_state)
-
-
-def backward_chain(linear, local_back, zero_state):
+def chains(linear, offset, local_back):
+    def step(state, pieces):
+        piece_map, piece_add = pieces
+        return (jnp.dot(state, piece_map, precision=highest) + piece_add, state)
+
+    zero = jnp.zeros_like(offset[0])
+    state_in = lax.scan(step, zero, (linear, offset))[1]
     flipped = jnp.swapaxes(linear, 1, 2)
-
-    def back_hop(step_index, incoming):
-        outgoing = jnp.einsum("hvk,hkj->hvj", incoming, flipped, precision=highest) + local_back
-        return from_behind(outgoing, "ctx", -1)
-
-    return lax.fori_loop(0, lax.axis_size("ctx") - 1, back_hop, zero_state)
+    end_grad = lax.scan(step, zero, (flipped, local_back), reverse=True)[1]
+    return (state_in, end_grad)
+
+
+def to_owners(x):
+    return lax.all_to_all(x, "ctx", 0, 0, tiled=True)
 
 
 def local(
@@ -185,19 +184,21 @@
 
     terms, terms_back = jax.vjp(local_terms, query_f, key_f, value_f, logits, log_gate)
     linear, offset = segment_map(terms, zero_state)
-    state_in = forward_chain(linear, offset, zero_state)
+    local_back = jax.vjp(output_from_terms, terms, zero_state)[1]((cotangent, zero_state))[1]
+    owned = to_owners(jnp.stack([linear, offset, local_back], axis=1))
+    owned = jnp.stack(chains(owned[:, 0], owned[:, 1], owned[:, 2]), axis=1)
+    owned = to_owners(owned)
+    state_in, end_grad = owned[:, 0], owned[:, 1]
     unused, full_pull = jax.vjp(output_from_terms, terms, state_in)
-    local_back = full_pull((cotangent, zero_state))[1]
-    end_grad = backward_chain(linear, local_back, zero_state)
     term_grads = full_pull((cotangent, end_grad))[0]
     grads = terms_back(term_grads)
     logit_grad = grads[3]
     piece = hidden_in.astype(jnp.float32)
-    beta_weight_grad = lax.psum_scatter(
-        jnp.dot(piece.T, logit_grad, precision=highest, preferred_element_type=jnp.float32),
-        ("dp", "ctx"),
-        scatter_dimension=0,
-        tiled=True,
+    partial = jnp.dot(piece.T, logit_grad, precision=highest, preferred_element_type=jnp.float32)
+    parts = lax.axis_size("dp") * ctx_count
+    partial = partial.reshape(parts, partial.shape[0] // parts, heads)
+    beta_weight_grad = jnp.sum(
+        lax.all_to_all(partial, ("dp", "ctx"), 0, 0, tiled=True), axis=0
     )
     return (
         grads[0].astype(jnp.bfloat16),

time: 1260 us -> 401 us (0.32)
  waiting for transfers between devices: 751 us -> 74.3 us
  starting transfers between devices: 117 us -> 22.1 us
  matrix products: 287 us -> 208 us
  other arithmetic: 19.2 us -> 33.6 us
  between operations: 15.7 us -> 2.39 us
    ppermute x30 -> x0, waiting for transfers between devices: 592 us -> none  [from_behind(): return lax.ppermute(x, axis, pairs)]
    unnamed x2 -> x0, waiting for transfers between devices: 159 us -> none
    ppermute x30 -> x0, starting transfers between devices: 117 us -> none  [from_behind(): return lax.ppermute(x, axis, pairs)]
    dot_general x30 -> x35, matrix products: 116 us -> 36.3 us  [the longest x32 35.8 us: step(): return (jnp.dot(state, piece_map, precision=highest) + piece_add, state)]
    all_to_all x0 -> x3, waiting for transfers between devices: none -> 74.3 us  [the longest x2 74.3 us: to_owners(): return lax.all_to_all(x, 'ctx', 0, 0, tiled=True)]
    all_to_all x0 -> x3, starting transfers between devices: none -> 22.1 us  [the longest x2 13.1 us: to_owners(): return lax.all_to_all(x, 'ctx', 0, 0, tiled=True)]
  transfers between devices with their start and end apart: 31 -> 3, of which waited for: 31 -> 2; matrix products, arithmetic and copies ran while one was open for 1% -> 3% of each run, Pallas kernels for 0% -> 0%
where the time goes in v1:
time: 401 us; the launch traced here: 397 us
  matrix products  208 us (52%)
  waiting for transfers between devices  74.3 us (19%)
  local copies, waits for them, and re-layouts  54.6 us (14%)
  other arithmetic  33.6 us (8%)
  starting transfers between devices  22.1 us (6%)
    all_to_all x2, waiting for transfers between devices, to_owners(): return lax.all_to_all(x, 'ctx', 0, 0, tiled=True)  74.3 us
    dot_general x32, matrix products, step(): return (jnp.dot(state, piece_map, precision=highest) + piece_add, state)  35.8 us
    dot_general x15, matrix products, unit_inverse(): power = jnp.einsum('nhij,nhjk->nhik', power, power, precision=highest)  26.9 us
    dot_general x15, matrix products, unit_inverse(): jnp.einsum('nhij,nhjk->nhik', total, power, precision=highest)  25.7 us
    dot_general x8, matrix products, advance(): jnp.einsum('hvk,hkj->hvj', state, piece_map, precision=highest)  21.1 us
    dot_general x3, matrix products, block_terms(): jnp.einsum('nhcv,nhck->nhvk', u_zero, weighted, precision=highest)  15.6 us
    dot_general x6, matrix products, advance(): jnp.einsum('hck,hvk->hcv', piece_q, state, precision=highest)  13.5 us
    unnamed x163, local copies, waits for them, and re-layouts  13.4 us
  transfers between devices with their start and end apart: 3, of which 2 were waited for; matrix products, arithmetic and copies ran while one was open for 3% of the time, Pallas kernels for 0%

profile of v1, /device:TPU:1, one launch (start us, length us, event | category | flops | bytes accessed | tf_op | source)
XLA Modules:
  0.0 396.6 jit_solution(867590032869116338)
XLA Ops:
  4.3 2.9 fusion.196
  9.3 2.5 fusion.199
  13.1 2.2 convolution_add_fusion.11
  19.7 2.1 convolution_add_fusion.9
  27.8 3.1 fusion.93
  30.9 2.4 fusion.100
  33.6 7.0 %fusion.111 = f32[2,16,128,128]{2,3,1,0:T(8,128)} fusion(f32[2,16,64,128]{3,2,1,0:T(8,128)} %fusion.93, f32[2,16,64]{2,1,0:T(8,128)S(1)} %slice_reduce_fusion, f32[2,64,16,128]{3,2,1,0:T(8,128)S(1)} %bitcast.467, f32[2,16,64]{2,1,0:T(8,128)S(1)} %get-tuple-element.795), kind=kOutput, calls=%fused_computation.189 | convolution fusion | flops 403177472 | bytes 4210688 | tf_op jit(solution)/shard_map/jvp(nhcv,nhck->nhvk)/dot_general | solution.py:59
  40.6 5.7 %multiply_subtract_fusion = f32[2,16,128,128]{3,2,1,0:T(8,128)} fusion(f32[2,16,64,128]{3,2,1,0:T(8,128)S(1)} %fusion.100, f32[128,128]{1,0:T(8,128)S(1)} %fusion.156, f32[2,16]{1,0:T(2,128)S(1)} %slice_reduce_fusion.1, f32[2,16,64]{2,1,0:T(8,128)S(1)} %slice_reduce_fusion, f32[2,64,16,128]{3,2,1,0:T(8,128)S(1)} %bitcast.468, ...), kind=kOutput, calls=%fused_computation.81 | convolution fusion | flops 404226048 | bytes 4276352 | tf_op jit(solution)/shard_map/jvp(nhck,nhcj->nhkj)/dot_general | solution.py:61
  46.2 3.0 copy.254
  49.3 13.1 %while.94 = (s32[]{:T(128)}, f32[16,128,128]{1,2,0:T(8,128)S(1)}, f32[16,128,128]{1,2,0:T(8,128)}, f32[2,16,128,128]{2,3,1,0:T(8,128)}, f32[2,16,128,128]{2,3,1,0:T(8,128)}, /*index=5*/s32[]{:T(128)}, s32[]{:T(128)}) while((s32[]{:T(128)}, f32[16,128,128]{1,2,0:T(8,128)S(1)}, f32[16,128,128]{1,2,0:T(8,128)}, ...), condition=%wide.region_4.5_spmd.clone, body=%wide.region_3.4_spmd.clone.sunk | while | flops 805830656 | bytes 19924088 | solution.py:114
  51.2 3.4 fusion.337
  57.8 3.4 fusion.337
  62.5 3.9 fusion.107
  67.4 4.0 %convolution_subtract_fusion = f32[2,16,64,128]{3,2,1,0:T(8,128)} fusion(f32[2,16,64,128]{3,2,1,0:T(8,128)S(1)} %copy-done.22, f32[2,64,16,128]{3,2,1,0:T(8,128)S(1)} %bitcast.481, f32[2,16,64]{2,1,0:T(8,128)S(1)} %get-tuple-element.794, f32[2,16,64]{2,1,0:T(8,128)S(1)} %get-tuple-element.771, f32[2,16,64,64]{2,3,1,0:T(8,128)S(1)} %fusion.107, ...), kind=kOutput, calls=%fused_computation.115 | convolution fusion | flops 202637312 | bytes 3702784 | tf_op jit(solution)/shard_map/jvp(nhij,nhjk->nhik)/dot_general | solution.py:55
  72.6 10.9 %while.95 = (s32[]{:T(128)}, f32[16,128,128]{1,2,0:T(8,128)}, f32[2,16,128,128]{3,2,1,0:T(8,128)}, f32[2,16,64,128]{3,2,1,0:T(8,128)S(1)}, f32[2,16,64,128]{3,2,1,0:T(8,128)}, /*index=5*/s32[]{:T(128)}, s32[]{:T(128)}) while((s32[]{:T(128)}, f32[16,128,128]{1,2,0:T(8,128)}, f32[2,16,128,128]{3,2,1,0:T(8,128)}, ...), condition=%wide.region_10.11_spmd.clone, body=%wide.region_9.10_spmd.clone.sunk | while | flops 604504064 | bytes 10486915 | solution.py:75
  72.6 2.5 convolution_bitcast_fusion.16
  75.1 2.8 convolution_add_fusion.27
  77.9 2.8 convolution_bitcast_fusion.16
  80.7 2.8 convolution_add_fusion.27
  83.5 4.3 %pad_maximum_fusion = f32[16,3,128,128]{2,3,1,0:T(8,128)} fusion(f32[16,1,128,128]{2,3,1,0:T(8,128)} %bitcast.485, f32[16,1,128,128]{2,3,1,0:T(8,128)} %bitcast.486, f32[16,1,128,128]{2,3,1,0:T(8,128)} %bitcast.478), kind=kLoop, calls=%fused_computation.78 | loop fusion | flops 1572864 | bytes 6291456 | tf_op jit(solution)/shard_map/stack | solution.py:188
  87.8 8.5 %all-to-all-start = ((f32[16,3,128,128]{2,3,1,0:T(8,128)}), f32[16,3,128,128]{2,3,1,0:T(8,128)}, u32[]{:S(2)}, u32[]{:S(2)}) async-start(f32[16,3,128,128]{2,3,1,0:T(8,128)} %pad_maximum_fusion), calls=%async_computation | async-start | bytes 6291456 | tf_op jit(solution)/shard_map/all_to_all | solution.py:147
  96.3 46.7 %all-to-all-done = f32[16,3,128,128]{2,3,1,0:T(8,128)} async-done(((f32[16,3,128,128]{2,3,1,0:T(8,128)}), f32[16,3,128,128]{2,3,1,0:T(8,128)}, u32[]{:S(2)}, u32[]{:S(2)}) %all-to-all-start) | async-done | bytes 3145760 | tf_op jit(solution)/shard_map/all_to_all | solution.py:147
  142.9 4.1 %slice_bitcast_fusion.3 = (f32[16,128,128]{1,2,0:T(8,128)}, f32[16,128,128]{2,1,0:T(8,128)}, f32[16,128,128]{1,2,0:T(8,128)}, f32[16,128,128]{1,2,0:T(8,128)}) fusion(f32[16,3,128,128]{2,3,1,0:T(8,128)} %all-to-all-done), kind=kLoop, calls=%fused_computation.128 | loop fusion | bytes 7340032 | tf_op jit(solution)/shard_map/squeeze | solution.py:189
  147.2 18.2 %while.96 = (s32[]{:T(128)}, f32[128,128]{0,1:T(8,128)S(1)}, f32[16,128,128]{1,2,0:T(8,128)S(1)}, f32[16,128,128]{1,2,0:T(8,128)}, f32[16,128,128]{1,2,0:T(8,128)}, /*index=5*/s32[]{:T(128)}, s32[]{:T(128)}) while((s32[]{:T(128)}, f32[128,128]{0,1:T(8,128)S(1)}, f32[16,128,128]{1,2,0:T(8,128)S(1)}, f32[16,128,128]{1,2,0:T(8,128)}, ...), condition=%wide.region_12.13_spmd.clone, body=%wide.region_11.12_spmd.clone.sunk | while | flops 25214980 | bytes 525404 | solution.py:140
  166.5 29.2 %while.97 = (s32[]{:T(128)}, f32[128,128]{0,1:T(8,128)S(1)}, f32[16,128,128]{1,2,0:T(8,128)}, f32[16,128,128]{2,1,0:T(8,128)}, f32[16,128,128]{1,2,0:T(8,128)}, /*index=5*/s32[]{:T(128)}, s32[]{:T(128)}, s32[]{:T(128)}) while((s32[]{:T(128)}, f32[128,128]{0,1:T(8,128)S(1)}, f32[16,128,128]{1,2,0:T(8,128)}, ...), condition=%wide.region_14.15_spmd.clone, body=%wide.region_13.14_spmd.clone.sunk | while | flops 25214980 | bytes 525935 | solution.py:142
  195.7 2.8 pad_maximum_fusion.1
  198.4 4.6 %all-to-all-start.1 = ((f32[16,2,128,128]{2,3,1,0:T(8,128)}), f32[16,2,128,128]{2,3,1,0:T(8,128)}, u32[]{:S(2)}, u32[]{:S(2)}) async-start(f32[16,2,128,128]{2,3,1,0:T(8,128)} %pad_maximum_fusion.1), calls=%async_computation.1 | async-start | bytes 4194304 | tf_op jit(solution)/shard_map/all_to_all | solution.py:147
  203.0 27.6 %all-to-all-done.1 = f32[16,2,128,128]{2,3,1,0:T(8,128)} async-done(((f32[16,2,128,128]{2,3,1,0:T(8,128)}), f32[16,2,128,128]{2,3,1,0:T(8,128)}, u32[]{:S(2)}, u32[]{:S(2)}) %all-to-all-start.1) | async-done | bytes 2097184 | tf_op jit(solution)/shard_map/all_to_all | solution.py:147
  230.7 2.7 slice_bitcast_fusion
  235.0 9.8 %while.92 = (s32[]{:T(128)}, f32[16,128,128]{1,2,0:T(8,128)}, f32[2,16,128,128]{2,3,1,0:T(8,128)}, f32[2,16,128,128]{2,3,1,0:T(8,128)}, f32[2,16,128,128]{2,3,1,0:T(8,128)}, /*index=5*/s32[]{:T(128)}) while((s32[]{:T(128)}, f32[16,128,128]{1,2,0:T(8,128)}, f32[2,16,128,128]{2,3,1,0:T(8,128)}, f32[2,16,128,128]{2,3,1,0:T(8,128)}, ...), condition=%wide.region_16.17_spmd, body=%wide.region_15.16_spmd.sunk | while | flops 402915328 | bytes 25167484 | solution.py:75
  237.7 2.1 fusion.322
  242.6 2.1 fusion.322
  250.1 26.2 %while.93 = (s32[]{:T(128)}, f32[16,128,128]{1,2,0:T(8,128)S(1)}, f32[2,16,64,128]{3,2,1,0:T(8,128)}, f32[2,16,64,128]{3,2,1,0:T(8,128)}, f32[2,16,128,128]{2,3,...) while((s32[]{:T(128)}, f32[16,128,128]{1,2,0:T(8,128)S(1)}, ...), condition=%wide.region_18.19_spmd, body=%wide.region_17.18_spmd.sunk | while | flops 1208221696 | bytes 65015652 | solution.py:75
  250.1 4.6 %fusion.332 = f32[2,16,128,128]{3,2,1,0:T(8,128)} fusion(f32[2,16,128,128]{3,2,1,0:T(8,128)} %get-tuple-element.1133, s32[]{:T(128)S(6)} %sub.178, f32[16,128,128]{1,2,0:T(8,128)S(1)} %get-tuple-element.1129, f32[2,16,128,128]{2,3,1,0:T(8,128)} %get-tuple-element.1148), kind=kOutput, calls=%fused_computation.7.clone.1 | convolution fusion | flops 402653184 | bytes 3146752 | tf_op jit(solution)/shard_map/transpose(jvp())/while/body/eval_jaxpr/hvk,hkj->hvj/dot_general | solution.py:72
  259.2 2.1 fusion.331
  263.1 4.6 %fusion.332 = f32[2,16,128,128]{3,2,1,0:T(8,128)} fusion(f32[2,16,128,128]{3,2,1,0:T(8,128)} %get-tuple-element.1133, s32[]{:T(128)S(6)} %sub.178, f32[16,128,128]{1,2,0:T(8,128)S(1)} %get-tuple-element.1129, f32[2,16,128,128]{2,3,1,0:T(8,128)} %get-tuple-element.1148), kind=kOutput, calls=%fused_computation.7.clone.1 | convolution fusion | flops 402653184 | bytes 3146752 | tf_op jit(solution)/shard_map/transpose(jvp())/while/body/eval_jaxpr/hvk,hkj->hvj/dot_general | solution.py:72
  272.2 2.1 fusion.331
  276.3 6.2 %fusion.205 = f32[2,16,64,128]{3,2,1,0:T(8,128)S(1)} fusion(f32[2,16,64,128]{3,2,1,0:T(8,128)} %fusion.93, f32[2,16,128,128]{2,3,1,0:T(8,128)} %get-tuple-element.503), kind=kOutput, calls=%fused_computation.310 | convolution fusion | flops 402653184 | bytes 4194304 | tf_op jit(solution)/shard_map/transpose(jvp(nhcv,nhck->nhvk))/dot_general | solution.py:59
  282.6 2.4 fusion.108
  286.6 4.3 %fusion.71 = f32[2,16,64,128]{3,2,1,0:T(8,128)S(1)} fusion(f32[2,16,64,128]{3,2,1,0:T(8,128)S(1)} %fusion.94, f32[2,16,128,128]{3,2,1,0:T(8,128)S(1)} %copy-done.20, f32[2,16,64]{2,1,0:T(8,128)S(1)} %slice_reduce_fusion, f32[2,64,16,128]{3,2,1,0:T(8,128)S(1)} %bitcast.471, f32[2,16,64]{2,1,0:T(8,128)S(1)} %get-tuple-element.795), kind=kOutput, calls=%fused_computation.102 | convolution fusion | flops 403963904 | bytes 5259264 | tf_op jit(solution)/shard_map/transpose(jvp(nhck,nhcj->nhkj))/dot_general | solution.py:61
  290.9 2.2 fusion.98
  293.1 3.1 convolution_add_fusion.21
  296.3 2.1 convolution_add_fusion.20
  305.0 1.9 fusion.207
  306.9 2.0 convolution_add_fusion.19
  310.8 1.9 fusion.208
  316.4 1.9 fusion.209
  320.1 2.0 convolution_add_fusion.14
  322.2 1.9 fusion.210
  326.0 2.2 convolution_add_fusion.12
  328.2 2.2 fusion.198
  330.4 2.3 fusion.197
  336.3 2.7 fusion.116
  340.9 2.4 fusion.85
  343.2 3.1 convolution_add_fusion.23
  348.2 4.9 %multiply_reduce_fusion.4 = (f32[2,16,64]{2,1,0:T(8,128)S(1)}, f32[2,16,64]{2,1,0:T(8,128)S(1)}, f32[2,16,64,128]{3,2,1,0:T(8,128)}) fusion(f32[2,16,64,128]{3,2,1,0:T(8,128)S(1)} %copy-done.38, f32[2,64,16,128]{3,2,1,0:T(8,128)S(1)} %bitcast.483, f32[2,16,64]{2,1,0:T(8,128)S(1)} %get-tuple-element.794, f32[2,64,16,128]{3,2,1,0:T(8,128)S(1)} %bitcast.475, ...), kind=kOutput, calls=%fused_computation.160 | convolution fusion | flops 203943936 | bytes 4775936 | tf_op jit(solution)/shard_map/transpose(jvp(nhik,nhjk->nhij))/dot_general | solution.py:53
  353.4 2.1 fusion.68
  355.6 3.4 multiply_reduce_fusion.3
  360.4 4.3 %multiply_reduce_fusion.1 = (f32[2,16,64]{2,1,0:T(8,128)S(1)}, f32[2,16,64,64]{2,3,1,0:T(8,128)}) fusion(f32[2,16,64]{2,1,0:T(8,128)S(1)} %bitcast.503, pred[2,64,64]{1,2,0:T(8,128)(4,1)S(1)} %compare_and_fusion, f32[2,16,64,64]{2,3,1,0:T(8,128)} %copy-done.35, f32[2,16,64,64]{2,3,1,0:T(8,128)} %copy-done.24, f32[2,16,1,64]{2,3,1,0:T(8,128)} %copy.298, ...), kind=kLoop, calls=%fused_computation.156 | loop fusion | flops 1701888 | bytes 2662400 | tf_op jit(solution)/shard_map/transpose(jvp())/reduce_sum | solution.py:47
  365.1 2.1 reshape.161
  367.2 2.8 copy.458
  370.0 2.7 reshape.170
  372.7 9.0 %all-to-all-start.2 = ((f32[128,1,288]{2,1,0:T(1,128)}), f32[128,1,288]{2,1,0:T(1,128)S(1)}, u32[]{:S(2)}, u32[]{:S(2)}) async-start(f32[128,1,288]{2,1,0:T(1,128)} %reshape.170), calls=%async_computation.2 | async-start | bytes 393216 | tf_op jit(solution)/shard_map/all_to_all | solution.py:201
  387.4 2.6 fusion.79
  (410 shorter events, 136.3 us)
Async XLA Ops:
  0.6 7.5 %copy-start = (bf16[128,2304]{1,0:T(8,128)(2,1)S(1)}, bf16[128,2304]{1,0:T(8,128)(2,1)}, u32[]{:S(2)}) copy-start(bf16[128,2304]{1,0:T(8,128)(2,1)} %param.25) | copy-start | bytes 1769476
  0.7 12.4 %copy-start.64 = (pred[64,64]{0,1:T(8,128)(4,1)}, pred[64,64]{0,1:T(8,128)(4,1)S(1)}, u32[]{:S(2)}) copy-start(pred[64,64]{0,1:T(8,128)(4,1)S(1)} %get-tuple-element.792) | copy-start | bytes 12292
  0.7 12.3 %copy-start.70 = (f32[64,64]{0,1:T(8,128)}, f32[64,64]{0,1:T(8,128)S(1)}, u32[]{:S(2)}) copy-start(f32[64,64]{0,1:T(8,128)S(1)} %get-tuple-element.793) | copy-start | bytes 49156
  2.9 4.3 %copy-start.86 = (s32[1,4]{1,0:T(1,128)S(1)}, s32[1,4]{1,0:T(1,128)}, u32[]{:S(2)}) copy-start(s32[1,4]{1,0:T(1,128)} %param.29) | copy-start | bytes 52
  2.9 5.3 %copy-start.74 = (bf16[2304,16]{0,1:T(8,128)(2,1)S(1)}, bf16[2304,16]{0,1:T(8,128)(2,1)}, u32[]{:S(2)}) copy-start(bf16[2304,16]{0,1:T(8,128)(2,1)} %param.26) | copy-start | bytes 221188
  2.9 5.6 %copy-start.77 = (f32[16,128]{1,0:T(8,128)S(1)}, f32[16,128]{1,0:T(8,128)}, u32[]{:S(2)}) copy-start(f32[16,128]{1,0:T(8,128)} %param.27) | copy-start | bytes 24580
  4.2 4.6 %copy-start.66 = (f32[2,16,64]{2,1,0:T(8,128)}, f32[2,16,64]{2,1,0:T(8,128)S(1)}, u32[]{:S(2)}) copy-start(f32[2,16,64]{2,1,0:T(8,128)S(1)} %fusion.83) | copy-start | bytes 24580
  7.2 5.9 %copy-start.24 = (f32[2,16,64,64]{2,3,1,0:T(8,128)}, f32[2,16,64,64]{2,3,1,0:T(8,128)S(1)}, u32[]{:S(2)}) copy-start(f32[2,16,64,64]{2,3,1,0:T(8,128)S(1)} %fusion.196) | copy-start | bytes 1572868
  8.2 3.6 copy-start.75
  8.4 3.4 copy-start.72
  11.8 3.5 copy-start.26
  13.0 3.5 copy-start.8
  15.3 3.1 copy-start.58
  16.5 3.1 copy-start.10
  18.4 3.3 copy-start.47
  19.6 3.3 copy-start.12
  21.7 3.1 copy-start.49
  23.0 2.9 copy-start.45
  25.2 2.6 copy-start.40
  27.8 5.6 %copy-start.30 = (f32[2,16,64,64]{2,3,1,0:T(8,128)}, f32[2,16,64,64]{2,3,1,0:T(8,128)S(1)}, u32[]{:S(2)}) copy-start(f32[2,16,64,64]{2,3,1,0:T(8,128)S(1)} %convolution_add_fusion.7) | copy-start | bytes 1572868
  33.4 7.2 %copy-start.21 = (f32[2,16,64,128]{3,2,1,0:T(8,128)}, f32[2,16,64,128]{3,2,1,0:T(8,128)S(1)}, u32[]{:S(2)}) copy-start(f32[2,16,64,128]{3,2,1,0:T(8,128)S(1)} %fusion.100) | copy-start | bytes 3145732
  62.4 9.0 %copy-start.14 = (f32[16,128,128]{1,2,0:T(8,128)}, f32[16,128,128]{1,2,0:T(8,128)S(1)}, u32[]{:S(2)}) copy-start(f32[16,128,128]{1,2,0:T(8,128)S(1)} %get-tuple-element.494) | copy-start | bytes 3145732
  62.4 4.9 %copy-start.16 = (f32[16,8,16,128]{3,2,1,0:T(8,128)S(1)}, f32[16,8,16,128]{3,2,1,0:T(8,128)}, u32[]{:S(2)}) copy-start(f32[16,8,16,128]{3,2,1,0:T(8,128)} %copy-done.15) | copy-start | bytes 3145732
  62.5 4.9 %copy-start.22 = (f32[2,16,64,128]{3,2,1,0:T(8,128)S(1)}, f32[2,16,64,128]{3,2,1,0:T(8,128)}, u32[]{:S(2)}) copy-start(f32[2,16,64,128]{3,2,1,0:T(8,128)} %copy-done.21) | copy-start | bytes 3145732
  67.3 4.1 %copy-start.78 = (s32[32]{0:T(128)S(1)}, s32[32]{0:T(128)}, u32[]{:S(2)}) copy-start(s32[32]{0:T(128)} %param.31) | copy-start | bytes 388
  67.3 4.1 %copy-start.79 = (f32[32]{0:T(128)S(1)}, f32[32]{0:T(128)}, u32[]{:S(2)}) copy-start(f32[32]{0:T(128)} %param.30) | copy-start | bytes 388
  67.3 4.3 %copy-start.87 = (s32[1,4]{1,0:T(1,128)S(1)}, s32[1,4]{1,0:T(1,128)}, u32[]{:S(2)}) copy-start(s32[1,4]{1,0:T(1,128)} %param.29) | copy-start | bytes 52
  67.4 4.4 %copy-start.81 = (s32[128]{0:T(128)S(1)}, s32[128]{0:T(128)}, u32[]{:S(2)}) copy-start(s32[128]{0:T(128)} %copy-done.80) | copy-start | bytes 1540
  67.4 4.4 %copy-start.83 = (s32[4]{0:T(128)S(1)}, s32[4]{0:T(128)}, u32[]{:S(2)}) copy-start(s32[4]{0:T(128)} %copy-done.82) | copy-start | bytes 52
  67.4 4.4 %copy-start.85 = (s32[4]{0:T(128)S(1)}, s32[4]{0:T(128)}, u32[]{:S(2)}) copy-start(s32[4]{0:T(128)} %copy-done.84) | copy-start | bytes 52
  67.4 4.4 %copy-start.63 = (bf16[128,2048]{1,0:T(8,128)(2,1)S(1)}, bf16[128,2048]{1,0:T(8,128)(2,1)}, u32[]{:S(2)}) copy-start(bf16[128,2048]{1,0:T(8,128)(2,1)} %param.28) | copy-start | bytes 1572868
  72.6 2.5 copy-start.18
  77.9 2.8 copy-start.18
  83.5 4.3 %copy-start.3 = (f32[2,16,64,128]{3,2,1,0:T(8,128)}, f32[2,16,64,128]{3,2,1,0:T(8,128)S(1)}, u32[]{:S(2)}) copy-start(f32[2,16,64,128]{3,2,1,0:T(8,128)S(1)} %get-tuple-element.1151) | copy-start | bytes 3145732
  87.8 55.2 %all-to-all-start = ((f32[16,3,128,128]{2,3,1,0:T(8,128)}), f32[16,3,128,128]{2,3,1,0:T(8,128)}, u32[]{:S(2)}, u32[]{:S(2)}) async-start(f32[16,3,128,128]{2,3,1,0:T(8,128)} %pad_maximum_fusion), calls=%async_computation | async-start | bytes 6291456 | tf_op jit(solution)/shard_map/all_to_all | solution.py:147
  198.4 32.2 %all-to-all-start.1 = ((f32[16,2,128,128]{2,3,1,0:T(8,128)}), f32[16,2,128,128]{2,3,1,0:T(8,128)}, u32[]{:S(2)}, u32[]{:S(2)}) async-start(f32[16,2,128,128]{2,3,1,0:T(8,128)} %pad_maximum_fusion.1), calls=%async_computation.1 | async-start | bytes 4194304 | tf_op jit(solution)/shard_map/all_to_all | solution.py:147
  235.0 2.5 copy-start.2
  235.0 2.7 copy-start.6
  239.9 2.7 copy-start.6
  250.1 4.6 %copy-start.5 = (f32[2,16,128,128]{3,2,1,0:T(8,128)S(1)}, f32[2,16,128,128]{3,2,1,0:T(8,128)}, u32[]{:S(2)}) copy-start(f32[2,16,128,128]{3,2,1,0:T(8,128)} %get-tuple-element.1145) | copy-start | bytes 6291460 | tf_op jit(solution)/shard_map/transpose(jvp())/while
  256.5 4.9 %copy-start.33 = (f32[2,16,128,128]{2,3,1,0:T(8,128)}, f32[2,16,128,128]{2,3,1,0:T(8,128)S(1)}, u32[]{:S(2)}) copy-start(f32[2,16,128,128]{2,3,1,0:T(8,128)S(1)} %bitcast_dynamic-update-slice_fusion.9) | copy-start | bytes 6291460 | tf_op jit(solution)/shard_map/transpose(jvp())/while
  256.5 2.7 copy-start.36
  263.1 4.6 %copy-start.5 = (f32[2,16,128,128]{3,2,1,0:T(8,128)S(1)}, f32[2,16,128,128]{3,2,1,0:T(8,128)}, u32[]{:S(2)}) copy-start(f32[2,16,128,128]{3,2,1,0:T(8,128)} %get-tuple-element.1145) | copy-start | bytes 6291460 | tf_op jit(solution)/shard_map/transpose(jvp())/while
  269.4 4.9 %copy-start.33 = (f32[2,16,128,128]{2,3,1,0:T(8,128)}, f32[2,16,128,128]{2,3,1,0:T(8,128)S(1)}, u32[]{:S(2)}) copy-start(f32[2,16,128,128]{2,3,1,0:T(8,128)S(1)} %bitcast_dynamic-update-slice_fusion.9) | copy-start | bytes 6291460 | tf_op jit(solution)/shard_map/transpose(jvp())/while
  269.5 2.7 copy-start.36
  276.3 6.2 %copy-start.34 = (f32[2,16,128,128]{2,3,1,0:T(8,128)S(1)}, f32[2,16,128,128]{2,3,1,0:T(8,128)}, u32[]{:S(2)}) copy-start(f32[2,16,128,128]{2,3,1,0:T(8,128)} %get-tuple-element.503) | copy-start | bytes 6291460
  282.6 2.5 copy-start.29
  282.6 2.5 copy-start.38
  293.1 3.2 copy-start.41
  334.4 4.6 %copy-start.35 = (f32[2,16,64,64]{2,3,1,0:T(8,128)}, f32[2,16,64,64]{2,3,1,0:T(8,128)S(1)}, u32[]{:S(2)}) copy-start(f32[2,16,64,64]{2,3,1,0:T(8,128)S(1)} %fusion.74) | copy-start | bytes 1572868
  336.3 19.2 %copy-start.51 = (f32[2,16,64,128]{3,2,1,0:T(8,128)}, f32[2,16,64,128]{3,2,1,0:T(8,128)S(1)}, u32[]{:S(2)}) copy-start(f32[2,16,64,128]{3,2,1,0:T(8,128)S(1)} %fusion.118) | copy-start | bytes 3145732
  336.3 2.7 copy-start.23
  339.0 16.5 %copy-start.53 = (f32[2,16,64,128]{3,2,1,0:T(8,128)}, f32[2,16,64,128]{3,2,1,0:T(8,128)S(1)}, u32[]{:S(2)}) copy-start(f32[2,16,64,128]{3,2,1,0:T(8,128)S(1)} %fusion.116) | copy-start | bytes 3145732
  343.2 3.1 copy-start.17
  346.4 6.8 %copy-start.39 = (f32[2,16,64,64]{2,3,1,0:T(8,128)}, f32[2,16,64,64]{2,3,1,0:T(8,128)S(1)}, u32[]{:S(2)}) copy-start(f32[2,16,64,64]{2,3,1,0:T(8,128)S(1)} %convolution_add_fusion.23) | copy-start | bytes 1572868
  348.2 7.4 %copy-start.55 = (f32[2,16,64,128]{3,2,1,0:T(8,128)}, f32[2,16,64,128]{3,2,1,0:T(8,128)S(1)}, u32[]{:S(2)}) copy-start(f32[2,16,64,128]{3,2,1,0:T(8,128)S(1)} %fusion.106) | copy-start | bytes 3145732
  355.5 3.4 copy-start.57
  360.3 4.3 %copy-start.76 = (f32[2,64]{1,0:T(2,128)S(1)}, f32[2,64]{1,0:T(2,128)}, u32[]{:S(2)}) copy-start(f32[2,64]{1,0:T(2,128)} %copy-done.75) | copy-start | bytes 1540
  360.3 4.4 %copy-start.73 = (f32[128,16]{0,1:T(8,128)S(1)}, f32[128,16]{0,1:T(8,128)}, u32[]{:S(2)}) copy-start(f32[128,16]{0,1:T(8,128)} %copy-done.72) | copy-start | bytes 24580
  372.7 20.6 %all-to-all-start.2 = ((f32[128,1,288]{2,1,0:T(1,128)}), f32[128,1,288]{2,1,0:T(1,128)S(1)}, u32[]{:S(2)}, u32[]{:S(2)}) async-start(f32[128,1,288]{2,1,0:T(1,128)} %reshape.170), calls=%async_computation.2 | async-start | bytes 393216 | tf_op jit(solution)/shard_map/all_to_all | solution.py:201
  383.3 4.0 %copy-start.69 = (f32[2,16,64]{2,1,0:T(8,128)S(1)}, f32[2,16,64]{2,1,0:T(8,128)}, u32[]{:S(2)}) copy-start(f32[2,16,64]{2,1,0:T(8,128)} %copy-done.68) | copy-start | bytes 24580
  384.4 3.0 copy-start.52
  384.4 3.0 copy-start.54
  384.4 3.0 copy-start.56
  (39 other events, 65.4 us)

commit v2 on v1

v2 whole, which is shorter than its diff:
```python
import jax
import jax.numpy as jnp
from jax import lax
from jax.experimental import pallas as pl
from jax.experimental.pallas import tpu as pltpu
from jax.sharding import PartitionSpec as P

F32 = jnp.float32
BF16 = jnp.bfloat16
N = 128
HP = 4
VMEM_LIMIT = 56 * 1024 * 1024
NN = (((1,), (0,)), ((), ()))
NT = (((1,), (1,)), ((), ()))
TN = (((0,), (0,)), ((), ()))


def split(x):
    hi = x.astype(BF16)
    return hi, (x - hi.astype(F32)).astype(BF16)


def dot(a, b, dims):
    return lax.dot_general(a, b, dims, preferred_element_type=F32)


def dot3(a, b, dims):
    ah, al = split(a)
    bh, bl = split(b)
    return dot(ah, bh, dims) + (dot(ah, bl, dims) + dot(al, bh, dims))


def dot2l(a, b, dims):
    ah, al = split(a)
    return dot(ah, b, dims) + dot(al, b, dims)


def dot2r(a, b, dims):
    bh, bl = split(b)
    return dot(a, bh, dims) + dot(a, bl, dims)


def iota(axis):
    return lax.broadcasted_iota(jnp.int32, (N, N), axis)


def unit_inverse(lower):
    rows, cols = iota(0), iota(1)
    size = 2
    inverse = jnp.where(rows == cols, 1.0, 0.0) - jnp.where(rows // 2 == cols // 2, lower, 0.0)
    while size < N:
        off = (rows // (2 * size) == cols // (2 * size)) & (rows // size != cols // size)
        step = dot3(jnp.where(off, lower, 0.0), inverse, NN)
        inverse = inverse - dot3(inverse, step, NN)
        size *= 2
    return inverse


def begins_of(lens_ref):
    begins, at = [], jnp.int32(0)
    for i in range(lens_ref.shape[1]):
        begins.append(at)
        at = at + lens_ref[0, i]
    return begins


def plan(lens_ref, ctx):
    begins = begins_of(lens_ref)
    first = ctx * N
    row_pos, col_pos = iota(0) + first, iota(1) + first

    def count(at):
        return sum((b <= at).astype(jnp.int32) for b in begins)

    row_id, col_id = count(row_pos), count(col_pos)
    linked = jnp.where((row_id == col_id) & (row_pos >= col_pos), 1.0, 0.0)
    head = jnp.where(row_id == count(first - 1), 1.0, 0.0)
    tail = jnp.where(row_id == count(first + N - 1), 1.0, 0.0)
    return linked, head, tail, row_id


def token_weights(lens_ref, prompts_ref, rewards_row, prompts_row, row_id, dp):
    rolls = lens_ref.shape[1]
    lanes = lax.broadcasted_iota(jnp.int32, rewards_row.shape, 1)
    weight = jnp.zeros((N, N), F32)
    for i in range(rolls):
        at = dp * rolls + i
        same = jnp.where(prompts_row == prompts_ref[0, at], 1.0, 0.0)
        mean = jnp.sum(same * rewards_row, axis=1, keepdims=True) / jnp.sum(same, axis=1, keepdims=True)
        own = jnp.sum(jnp.where(lanes == at, rewards_row, 0.0), axis=1, keepdims=True)
        length = jnp.full((1, 1), lens_ref[0, i], jnp.int32).astype(F32)
        scale = (own - mean) * (16.0 * N) / (rolls * length)
        weight = jnp.where(row_id == i + 1, scale, weight)
    return weight


def inverse_norm(rows):
    total = jnp.sum(rows * rows, axis=1, keepdims=True)
    return jnp.broadcast_to(lax.rsqrt(total + 1e-06), (N, N))


def by_row(row):
    return jnp.broadcast_to(row, (N, N)).T


def head_terms(q, k, gate_row, beta_row, linked, head, tail):
    qf, kf = q.astype(F32), k.astype(F32)
    rq, rk = inverse_norm(qf), inverse_norm(kf)
    rk_cols = rk.T
    gate = by_row(gate_row)
    decay = jnp.exp(jnp.minimum(gate - gate_row, 0.0)) * linked
    pairs = dot(jnp.concatenate([k, q], axis=0), k, NT)
    key_key = pairs[:N] * rk * rk_cols
    query_key = pairs[N:] * rq * rk_cols
    from_head = head * jnp.exp(gate)
    to_tail = tail * jnp.exp(gate[N - 1 : N, :] - gate)
    return qf * rq, kf * rk, rq, rk, rk_cols, decay, key_key, query_key, from_head, to_tail, by_row(beta_row)


def maps_kernel(lens_ref, prompts_ref, rewards_row_ref, prompts_row_ref, gate_ref, weight_ref, hidden_ref,
                q_ref, k_ref, v_ref, g_ref,
                maps_ref, inv_ref, mg_ref, sum_ref, beta_ref, tw_ref,
                linked_s, head_s, tail_s):
    ctx, dp = lax.axis_index("ctx"), lax.axis_index("dp")

    @pl.when(pl.program_id(0) == 0)
    def _():
        linked, head, tail, row_id = plan(lens_ref, ctx)
        linked_s[...], head_s[...], tail_s[...] = linked, head, tail
        tw_ref[...] = token_weights(lens_ref, prompts_ref, rewards_row_ref[...], prompts_row_ref[...], row_id, dp)
        logits = dot(weight_ref[...], hidden_ref[...], NT)
        beta_ref[...] = 1.0 / (1.0 + jnp.exp(-logits))
        upto = jnp.where(iota(0) <= iota(1), 1.0, 0.0).astype(BF16)
        gates = gate_ref[...]
        hi, rest = split(gates)
        mid = gates - hi.astype(F32)
        mid, low = split(mid)
        sum_ref[...] = dot(hi, upto, NN) + (dot(mid, upto, NN) + dot(low, upto, NN))

    linked, head, tail, tw = linked_s[...], head_s[...], tail_s[...], tw_ref[...]
    strict = iota(0) > iota(1)
    for i in range(HP):
        h = pl.program_id(0) * HP + i
        cols = slice(i * N, (i + 1) * N)
        q, k, v, g = q_ref[:, cols], k_ref[:, cols], v_ref[:, cols], g_ref[:, cols]
        gate_row, beta_row = sum_ref[pl.ds(h, 1), :], beta_ref[pl.ds(h, 1), :]
        qn, kn, rq, rk, rk_cols, decay, key_key, query_key, from_head, to_tail, beta = head_terms(
            q, k, gate_row, beta_row, linked, head, tail)
        inverse = unit_inverse(jnp.where(strict, beta * decay * key_key, 0.0))
        inv_ref[i] = inverse
        mixing = decay * query_key
        sides = jnp.concatenate([beta * v.astype(F32), beta * from_head * kn], axis=1)
        uz = dot3(inverse, sides, NN)
        ends = dot3(uz, to_tail * kn, TN)
        mg = dot2l(mixing * tw, g, TN)
        mg_ref[i] = mg
        back = dot2r(g, tw * from_head * qn, TN) - dot3(mg, uz[:, N:], TN)
        same = jnp.where(iota(0) == iota(1), 1.0, 0.0)
        maps_ref[i, 0] = from_head[N - 1 : N, :] * same - ends[N:]
        maps_ref[i, 1] = ends[:N]
        maps_ref[i, 2] = back


def chains_kernel(maps_ref, out_ref):
    count = maps_ref.shape[0]
    state = jnp.zeros((N, N), F32)
    grad = jnp.zeros((N, N), F32)
    for j in range(count):
        b = count - 1 - j
        out_ref[j, 0] = state
        out_ref[b, 1] = grad
        if j < count - 1:
            state = dot3(state, maps_ref[j, 0], NN) + maps_ref[j, 1]
            grad = dot3(grad, maps_ref[b, 0], NT) + maps_ref[b, 2]


def grads_kernel(lens_ref, q_ref, k_ref, v_ref, g_ref, ends_ref, inv_ref, mg_ref, sum_ref, beta_ref, tw_ref, spread_ref,
                 dq_ref, dk_ref, dv_ref, dgate_ref, dw_ref,
                 linked_s, head_s, tail_s, dlogit_s):
    ctx = lax.axis_index("ctx")

    @pl.when(pl.program_id(0) == 0)
    def _():
        linked_s[...], head_s[...], tail_s[...], unused = plan(lens_ref, ctx)
        dlogit_s[...] = jnp.zeros((N, N), F32)

    linked, head, tail, tw = linked_s[...], head_s[...], tail_s[...], tw_ref[...]
    strict = iota(0) > iota(1)
    reach = iota(0) >= iota(1)
    last = jnp.where(lax.broadcasted_iota(jnp.int32, (N, 1), 0) == N - 1, 1.0, 0.0)
    for i in range(HP):
        h = pl.program_id(0) * HP + i
        cols = slice(i * N, (i + 1) * N)
        q, k, v, g = q_ref[:, cols], k_ref[:, cols], v_ref[:, cols], g_ref[:, cols]
        gate_row, beta_row = sum_ref[pl.ds(h, 1), :], beta_ref[pl.ds(h, 1), :]
        qn, kn, rq, rk, rk_cols, decay, key_key, query_key, from_head, to_tail, beta = head_terms(
            q, k, gate_row, beta_row, linked, head, tail)
        state, grad = ends_ref[i, 0], ends_ref[i, 1]
        inverse = inv_ref[i]
        key_ends = dot2r(k, jnp.concatenate([state, grad], axis=0), NT)
        inner = v.astype(F32) - from_head * rk * key_ends[:, :N]
        u = dot3(inverse, beta * inner, NN)
        du = mg_ref[i] + to_tail * rk * key_ends[:, N:]
        dx = dot3(inverse, du, TN)
        dinv = jnp.where(strict, -dot3(dx, u, NT), 0.0)
        dmix = tw * dot2r(g, u, NT)
        dtail = dot3(u, grad, NN)
        gs = tw * dot2r(g, state, NN)
        dxs = dot3(dx, state, NN)
        decay_dinv = decay * dinv
        pair = beta * decay_dinv
        dqk = decay * dmix
        both = dot2l(jnp.concatenate([dqk * rk_cols, (pair + pair.T) * rk_cols], axis=0), k, NN)
        dqn = from_head * gs + both[:N]
        dkn = dot2l(dqk * rq, q, TN) + to_tail * dtail - beta * from_head * dxs + both[N:]
        dq_ref[:, cols] = (rq * (dqn - qn * jnp.sum(dqn * qn, axis=1, keepdims=True))).astype(BF16)
        dk_ref[:, cols] = (rk * (dkn - kn * jnp.sum(dkn * kn, axis=1, keepdims=True))).astype(BF16)
        dv_ref[:, cols] = (beta * dx).astype(BF16)
        dbeta = jnp.sum(dx * inner + decay_dinv * key_key, axis=1, keepdims=True)
        dlogit_s[...] = jnp.where(iota(1) == h, dbeta * beta * (1.0 - beta), dlogit_s[...])
        spread = dqk * query_key + pair * key_key
        tails = jnp.sum(to_tail * dtail * kn, axis=1, keepdims=True)
        heads = jnp.sum(from_head * (gs * qn - beta * dxs * kn), axis=1, keepdims=True)
        through = jnp.sum(from_head[N - 1 : N, :] * jnp.sum(state * grad, axis=0, keepdims=True), axis=1, keepdims=True)
        dgamma = jnp.sum(spread, axis=1, keepdims=True) + heads - tails
        dgamma = dgamma + last * (jnp.sum(tails, axis=0, keepdims=True) + through)
        dgamma = dgamma - by_row(jnp.sum(spread, axis=0, keepdims=True))
        dgate_ref[pl.ds(h, 1), :] = jnp.sum(jnp.where(reach, dgamma, 0.0), axis=0, keepdims=True)

    @pl.when(pl.program_id(0) == pl.num_programs(0) - 1)
    def _():
        heads = beta_ref.shape[0]
        per = N // heads
        dlogit = dlogit_s[...]
        rows = spread_ref.shape[0]
        for first in range(0, rows, per):
            total = jnp.zeros((N, N), F32)
            for r in range(first, min(first + per, rows)):
                moved = dlogit if r == first else pltpu.roll(dlogit, heads * (r - first), 1)
                total = total + dot2r(spread_ref[r], moved, NN)
            dw_ref[:, first * heads : first * heads + N] = total


def sum_kernel(parts_ref, out_ref):
    rows, heads = out_ref.shape
    total = jnp.sum(parts_ref[...], axis=0, keepdims=True)
    for r in range(rows):
        out_ref[r : r + 1, :] = total[:, r * heads : (r + 1) * heads]


def whole(shape):
    return pl.BlockSpec(shape, lambda i: (0,) * len(shape))


def to_owners(x):
    return lax.all_to_all(x, "ctx", 0, 0, tiled=True)


def local(queries, key_rows, value_rows, hidden_in, beta_weight, log_gate, out_grad, lengths, rewards, prompts):
    tokens, width = queries.shape
    depth, heads = beta_weight.shape
    parts = lax.axis_size("dp") * lax.axis_size("ctx")
    owned_rows = depth // parts
    tiles = -(-owned_rows * heads // N)
    smem = pl.BlockSpec(memory_space=pltpu.SMEM)
    by_heads = pl.BlockSpec((tokens, HP * N), lambda i: (0, i))
    params = pltpu.CompilerParams(vmem_limit_bytes=VMEM_LIMIT)
    prompts_row, rewards_row = prompts.reshape(1, -1), rewards.reshape(1, -1)

    def square(n):
        return pl.BlockSpec((HP, n, N, N), lambda i: (i, 0, 0, 0))

    one_square = pl.BlockSpec((HP, N, N), lambda i: (i, 0, 0))
    masks = [pltpu.VMEM((N, N), F32)] * 3
    maps, inverse, mg, sums, beta, tw = pl.pallas_call(
        maps_kernel,
        grid=(heads // HP,),
        in_specs=[smem, smem, whole(rewards_row.shape), whole(prompts_row.shape), whole(log_gate.shape),
                  whole((heads, depth)), whole(hidden_in.shape)] + [by_heads] * 4,
        out_specs=[square(3), one_square, one_square, whole((heads, N)), whole((heads, N)), whole((N, N))],
        out_shape=[jax.ShapeDtypeStruct(s, F32) for s in (
            (heads, 3, N, N), (heads, N, N), (heads, N, N), (heads, N), (heads, N), (N, N))],
        scratch_shapes=masks,
        compiler_params=params,
        name="segment_maps",
    )(lengths, prompts_row, rewards_row, prompts_row, log_gate, beta_weight.T, hidden_in,
      queries, key_rows, value_rows, out_grad)
    owned = to_owners(maps)
    ends = pl.pallas_call(
        chains_kernel,
        out_shape=jax.ShapeDtypeStruct((owned.shape[0], 2, N, N), F32),
        in_specs=[pl.BlockSpec(memory_space=pltpu.VMEM)],
        out_specs=pl.BlockSpec(memory_space=pltpu.VMEM),
        compiler_params=params,
        name="chains",
    )(owned)
    ends = to_owners(ends)
    spread = hidden_in.T.reshape(parts, owned_rows, tokens).transpose(1, 0, 2)
    dq, dk, dv, dgate, dw = pl.pallas_call(
        grads_kernel,
        grid=(heads // HP,),
        in_specs=[smem] + [by_heads] * 4 + [square(2), one_square, one_square, whole((heads, N)), whole((heads, N)),
                                            whole((N, N)), whole(spread.shape)],
        out_specs=[by_heads] * 3 + [whole((heads, N)), whole((parts, tiles * N))],
        out_shape=[jax.ShapeDtypeStruct((tokens, width), BF16)] * 3
        + [jax.ShapeDtypeStruct((heads, N), F32), jax.ShapeDtypeStruct((parts, tiles * N), F32)],
        scratch_shapes=masks + [pltpu.VMEM((N, N), F32)],
        compiler_params=params,
        name="segment_grads",
    )(lengths, queries, key_rows, value_rows, out_grad, ends, inverse, mg, sums, beta, tw, spread)
    pieces = lax.all_to_all(dw, ("dp", "ctx"), 0, 0, tiled=True)
    dweight = pl.pallas_call(
        sum_kernel,
        out_shape=jax.ShapeDtypeStruct((owned_rows, heads), F32),
        in_specs=[pl.BlockSpec(memory_space=pltpu.VMEM)],
        out_specs=pl.BlockSpec(memory_space=pltpu.VMEM),
        name="sum_parts",
    )(pieces)
    return dq, dk, dv, dgate, dweight


def solution(mesh):
    rows = P(("dp", "ctx"), None)
    gates = P(None, ("dp", "ctx"))
    in_specs = (rows, rows, rows, rows, P(), gates, rows, P("dp", None), P(), P())
    out_specs = (rows, rows, rows, gates, rows)
    return jax.shard_map(local, mesh=mesh, in_specs=in_specs, out_specs=out_specs, check_vma=False)
```

time: 401 us -> 173 us (0.43)
  matrix products: 208 us -> 0 us
  Pallas kernels: 0 us -> 69.1 us
  blocking collectives: 0 us -> 67.1 us
  local copies, waits for them, and re-layouts: 54.6 us -> 5.95 us
  waiting for transfers between devices: 74.3 us -> 25.8 us
  other arithmetic: 33.6 us -> 0 us
  starting transfers between devices: 22.1 us -> 3.85 us
    dot_general x108 -> x0, matrix products: 208 us -> none  [the longest x32 35.8 us: step(): return (jnp.dot(state, piece_map, precision=highest) + piece_add, state)]
    pallas_call x0 -> x4, Pallas kernels: none -> 69.1 us  [the longest x1 45.4 us: local(): pl.pallas_call(maps_kernel, grid=(heads // HP,), in_specs=[smem, smem, wh...]
    all_to_all x0 -> x2, blocking collectives: none -> 67.1 us  [the longest x1 47.1 us: to_owners(): return lax.all_to_all(x, 'ctx', 0, 0, tiled=True)]
    all_to_all x2 -> x1, waiting for transfers between devices: 74.3 us -> 25.8 us  [to_owners(): return lax.all_to_all(x, 'ctx', 0, 0, tiled=True)]
    while x86 -> x0, local copies, waits for them, and re-layouts: 12.1 us -> none
    dynamic_update_slice x32 -> x0, other arithmetic: 10.2 us -> none  [chains(): state_in = lax.scan(step, zero, (linear, offset))[1]]
    unnamed x163 -> x6, local copies, waits for them, and re-layouts: 13.4 us -> 3.4 us
    all_to_all x2 -> x1, starting transfers between devices: 13.1 us -> 3.85 us  [to_owners(): return lax.all_to_all(x, 'ctx', 0, 0, tiled=True)]
  transfers between devices with their start and end apart: 3 -> 1, of which waited for: 2 -> 1; matrix products, arithmetic and copies ran while one was open for 3% -> 1% of each run, Pallas kernels for 0% -> 0%
where the time goes in v2:
time: 173 us; the launch traced here: 172 us
  Pallas kernels  69.1 us (40%)
  blocking collectives  67.1 us (39%)
  waiting for transfers between devices  25.8 us (15%)
  local copies, waits for them, and re-layouts  5.95 us (3%)
  starting transfers between devices  3.85 us (2%)
    all_to_all x1, blocking collectives, to_owners(): return lax.all_to_all(x, 'ctx', 0, 0, tiled=True)  47.1 us
    pallas_call x1, Pallas kernels, local(): pl.pallas_call(maps_kernel, grid=(heads // HP,), in_specs=[smem, smem, wh...  45.4 us
    all_to_all x1, waiting for transfers between devices, to_owners(): return lax.all_to_all(x, 'ctx', 0, 0, tiled=True)  25.8 us
    all_to_all x1, blocking collectives, local(): pieces = lax.all_to_all(dw, ('dp', 'ctx'), 0, 0, tiled=True)  20 us
    pallas_call x1, Pallas kernels, local(): pl.pallas_call(grads_kernel, grid=(heads // HP,), in_specs=[smem] + [by_h...  15.9 us
    pallas_call x1, Pallas kernels, local(): pl.pallas_call(chains_kernel, out_shape=jax.ShapeDtypeStruct((owned.shape...  6.2 us
    all_to_all x1, starting transfers between devices, to_owners(): return lax.all_to_all(x, 'ctx', 0, 0, tiled=True)  3.85 us
  transfers between devices with their start and end apart: 1, of which 1 were waited for; matrix products, arithmetic and copies ran while one was open for 1% of the time, Pallas kernels for 0%

profile of v2, /device:TPU:1, one launch (start us, length us, event | category | flops | bytes accessed | tf_op | source)
XLA Modules:
  0.0 172.4 jit_solution(15982161214861792319)
XLA Ops:
  0.6 45.4 %segment_maps.1 = (f32[16,3,128,128]{3,2,1,0:T(8,128)}, f32[16,128,128]{2,1,0:T(8,128)}, f32[16,128,128]{2,1,0:T(8,128)}, f32[16,128]{1,0:T(8,128)}, f32[16,128]{1,0:T(8,128)}, /*index=5*/f32[128,128]{1,0:T(8,128)}) custom-call(s32[1,4]{1,0:T(1,128)} %lens_ref.3, s32[1,32]{1,0:T(1,128)} %bitcast.16, f32[1,32]{1,0:T(1,128)} %bitcast.18, s32[1,32]{1,0:T(1,128)} %bitcast.17, ...), custom_call_target="tpu_custom_call" | custom-call | tf_op jit(solution)/shard_map/segment_maps/pallas_call | solution.py:275
  46.0 47.1 %all_to_all.21.maps_ref = f32[16,3,128,128]{3,2,1,0:T(8,128)} all-to-all(f32[16,3,128,128]{3,2,1,0:T(8,128)} %get-tuple-element.16), channel_id=1, replica_groups=mesh['dp'=8,'ctx'=16] {'ctx'}, dimensions={0} | all-to-all | bytes 6291456 | tf_op jit(solution)/shard_map/all_to_all | solution.py:256
  93.1 6.2 %chains.1 = f32[16,2,128,128]{3,2,1,0:T(8,128)} custom-call(f32[16,3,128,128]{3,2,1,0:T(8,128)} %all_to_all.21.maps_ref), custom_call_target="tpu_custom_call" | custom-call | tf_op jit(solution)/shard_map/chains/pallas_call | solution.py:289
  99.3 0.0 copy-start.1
  99.3 3.8 %all-to-all-start.1 = ((f32[16,2,128,128]{3,2,1,0:T(8,128)}), f32[16,2,128,128]{3,2,1,0:T(8,128)S(1)}, u32[]{:S(2)}, u32[]{:S(2)}) async-start(f32[16,2,128,128]{3,2,1,0:T(8,128)} %chains.1), calls=%async_computation.1 | async-start | bytes 4194304 | tf_op jit(solution)/shard_map/all_to_all | solution.py:256
  103.2 0.0 copy-done.1
  103.2 0.3 copy.19
  103.5 0.2 reshape.23
  103.7 0.9 copy.26
  104.6 25.8 %all-to-all-done.1.ends_ref = f32[16,2,128,128]{3,2,1,0:T(8,128)S(1)} async-done(((f32[16,2,128,128]{3,2,1,0:T(8,128)}), f32[16,2,128,128]{3,2,1,0:T(8,128)S(1)}, u32[]{:S(2)}, u32[]{:S(2)}) %all-to-all-start.1) | async-done | bytes 2097184 | tf_op jit(solution)/shard_map/all_to_all | solution.py:256
  130.4 0.0 copy-start
  130.4 1.3 copy-done
  131.8 15.9 %segment_grads.1 = (bf16[128,2048]{1,0:T(8,128)(2,1)}, bf16[128,2048]{1,0:T(8,128)(2,1)}, bf16[128,2048]{1,0:T(8,128)(2,1)}, f32[16,128]{1,0:T(8,128)}, f32[128,384]{1,0:T(8,128)}) custom-call(s32[1,4]{1,0:T(1,128)} %lens_ref.3, bf16[128,2048]{1,0:T(8,128)(2,1)} %q_ref.3, bf16[128,2048]{1,0:T(8,128)(2,1)} %k_ref.3, bf16[128,2048]{1,0:T(8,128)(2,1)} %v_ref.3, ...), custom_call_target="tpu_custom_call" | custom-call | tf_op jit(solution)/shard_map/segment_grads/pallas_call | solution.py:299
  147.6 1.1 copy.21
  148.8 20.0 %all_to_all.22 = f32[128,1,384]{2,1,0:T(1,128)S(1)} all-to-all(f32[128,1,384]{2,1,0:T(1,128)S(1)} %copy.21), channel_id=1, replica_groups=mesh['dp'=8,'ctx'=16] {'dp','ctx'}, dimensions={0} | all-to-all | bytes 393216 | tf_op jit(solution)/shard_map/all_to_all | solution.py:311
  168.7 0.7 copy.27
  169.4 1.6 sum_parts.1
  171.0 1.4 copy.22
Async XLA Ops:
  99.3 3.9 %copy-start.1 = (bf16[128,2304]{1,0:T(8,128)(2,1)S(1)}, bf16[128,2304]{1,0:T(8,128)(2,1)}, u32[]{:S(2)}) copy-start(bf16[128,2304]{1,0:T(8,128)(2,1)} %hidden_ref.1) | copy-start | bytes 1769476
  99.3 31.1 %all-to-all-start.1 = ((f32[16,2,128,128]{3,2,1,0:T(8,128)}), f32[16,2,128,128]{3,2,1,0:T(8,128)S(1)}, u32[]{:S(2)}, u32[]{:S(2)}) async-start(f32[16,2,128,128]{3,2,1,0:T(8,128)} %chains.1), calls=%async_computation.1 | async-start | bytes 4194304 | tf_op jit(solution)/shard_map/all_to_all | solution.py:256
  130.4 1.3 copy-start

commit v3 on v2

--- a/solution.py
+++ b/solution.py
@@ -8,7 +8,8 @@
 F32 = jnp.float32
 BF16 = jnp.bfloat16
 N = 128
-HP = 4
+HP = 8
+HG = 4
 VMEM_LIMIT = 56 * 1024 * 1024
 NN = (((1,), (0,)), ((), ()))
 NT = (((1,), (1,)), ((), ()))
@@ -25,35 +26,39 @@
 
 
 def dot3(a, b, dims):
-    ah, al = split(a)
-    bh, bl = split(b)
-    return dot(ah, bh, dims) + (dot(ah, bl, dims) + dot(al, bh, dims))
+    (ka,), (kb,) = dims[0]
+    n = b.shape[1 - kb]
+    rights = jnp.concatenate(split(b), 1 - kb)
+    both = dot(jnp.concatenate(split(a), ka), jnp.concatenate([rights, rights], kb), dims)
+    return both[:, :n] + both[:, n:]
 
 
 def dot2l(a, b, dims):
-    ah, al = split(a)
-    return dot(ah, b, dims) + dot(al, b, dims)
+    (ka,), (kb,) = dims[0]
+    return dot(jnp.concatenate(split(a), ka), jnp.concatenate([b, b], kb), dims)
 
 
 def dot2r(a, b, dims):
-    bh, bl = split(b)
-    return dot(a, bh, dims) + dot(a, bl, dims)
+    (ka,), (kb,) = dims[0]
+    return dot(jnp.concatenate([a, a], ka), jnp.concatenate(split(b), kb), dims)
 
 
 def iota(axis):
     return lax.broadcasted_iota(jnp.int32, (N, N), axis)
 
 
-def unit_inverse(lower):
+def unit_inverses(lowers):
     rows, cols = iota(0), iota(1)
+    same = jnp.where(rows == cols, 1.0, 0.0)
+    pair = jnp.where(rows // 2 == cols // 2, 1.0, 0.0)
+    inverses = [same - pair * lower for lower in lowers]
     size = 2
-    inverse = jnp.where(rows == cols, 1.0, 0.0) - jnp.where(rows // 2 == cols // 2, lower, 0.0)
     while size < N:
-        off = (rows // (2 * size) == cols // (2 * size)) & (rows // size != cols // size)
-        step = dot3(jnp.where(off, lower, 0.0), inverse, NN)
-        inverse = inverse - dot3(inverse, step, NN)
+        off = jnp.where((rows // (2 * size) == cols // (2 * size)) & (rows // size != cols // size), 1.0, 0.0)
+        steps = [dot3(off * lower, inverse, NN) for lower, inverse in zip(lowers, inverses)]
+        inverses = [inverse - dot3(inverse, step, NN) for inverse, step in zip(inverses, steps)]
         size *= 2
-    return inverse
+    return inverses
 
 
 def begins_of(lens_ref):
@@ -138,7 +143,9 @@
         sum_ref[...] = dot(hi, upto, NN) + (dot(mid, upto, NN) + dot(low, upto, NN))
 
     linked, head, tail, tw = linked_s[...], head_s[...], tail_s[...], tw_ref[...]
-    strict = iota(0) > iota(1)
+    strict = jnp.where(iota(0) > iota(1), 1.0, 0.0)
+    same = jnp.where(iota(0) == iota(1), 1.0, 0.0)
+    lowers, rest = [], []
     for i in range(HP):
         h = pl.program_id(0) * HP + i
         cols = slice(i * N, (i + 1) * N)
@@ -146,19 +153,20 @@
         gate_row, beta_row = sum_ref[pl.ds(h, 1), :], beta_ref[pl.ds(h, 1), :]
         qn, kn, rq, rk, rk_cols, decay, key_key, query_key, from_head, to_tail, beta = head_terms(
             q, k, gate_row, beta_row, linked, head, tail)
-        inverse = unit_inverse(jnp.where(strict, beta * decay * key_key, 0.0))
-        inv_ref[i] = inverse
-        mixing = decay * query_key
-        sides = jnp.concatenate([beta * v.astype(F32), beta * from_head * kn], axis=1)
-        uz = dot3(inverse, sides, NN)
-        ends = dot3(uz, to_tail * kn, TN)
-        mg = dot2l(mixing * tw, g, TN)
-        mg_ref[i] = mg
-        back = dot2r(g, tw * from_head * qn, TN) - dot3(mg, uz[:, N:], TN)
-        same = jnp.where(iota(0) == iota(1), 1.0, 0.0)
-        maps_ref[i, 0] = from_head[N - 1 : N, :] * same - ends[N:]
+        lowers.append(strict * (beta * decay * key_key))
+        mg_ref[i] = dot2l(decay * query_key * tw, g, TN)
+        maps_ref[i, 2] = dot2r(g, tw * from_head * qn, TN)
+        maps_ref[i, 0] = from_head[N - 1 : N, :] * same
+        rest.append((jnp.concatenate([beta * v.astype(F32), beta * from_head * kn], axis=1), to_tail * kn))
+    inverses = unit_inverses(lowers)
+    for i in range(HP):
+        inv_ref[i] = inverses[i]
+    uzs = [dot3(inverse, sides, NN) for inverse, (sides, _) in zip(inverses, rest)]
+    for i in range(HP):
+        ends = dot3(uzs[i], rest[i][1], TN)
+        maps_ref[i, 0] -= ends[N:]
         maps_ref[i, 1] = ends[:N]
-        maps_ref[i, 2] = back
+        maps_ref[i, 2] -= dot3(mg_ref[i], uzs[i][:, N:], TN)
 
 
 def chains_kernel(maps_ref, out_ref):
@@ -174,9 +182,9 @@
             grad = dot3(grad, maps_ref[b, 0], NT) + maps_ref[b, 2]
 
 
-def grads_kernel(lens_ref, q_ref, k_ref, v_ref, g_ref, ends_ref, inv_ref, mg_ref, sum_ref, beta_ref, tw_ref, spread_ref,
-                 dq_ref, dk_ref, dv_ref, dgate_ref, dw_ref,
-                 linked_s, head_s, tail_s, dlogit_s):
+def logits_kernel(lens_ref, q_ref, k_ref, v_ref, ends_ref, inv_ref, mg_ref, sum_ref, beta_ref, spread_ref,
+                  u_ref, dx_ref, dw_ref,
+                  linked_s, head_s, tail_s, dlogit_s):
     ctx = lax.axis_index("ctx")
 
     @pl.when(pl.program_id(0) == 0)
@@ -184,40 +192,79 @@
         linked_s[...], head_s[...], tail_s[...], unused = plan(lens_ref, ctx)
         dlogit_s[...] = jnp.zeros((N, N), F32)
 
+    linked, head, tail = linked_s[...], head_s[...], tail_s[...]
+    strict = jnp.where(iota(0) > iota(1), 1.0, 0.0)
+    heads = range(HP)
+    first, inners, betas, pairs, dus, us, dxs = pl.program_id(0) * HP, [], [], [], [], [], []
+    for i in heads:
+        cols = slice(i * N, (i + 1) * N)
+        q, k, v = q_ref[:, cols], k_ref[:, cols], v_ref[:, cols]
+        gate_row, beta_row = sum_ref[pl.ds(first + i, 1), :], beta_ref[pl.ds(first + i, 1), :]
+        kf = k.astype(F32)
+        rk = inverse_norm(kf)
+        gate = by_row(gate_row)
+        key_key = dot(k, k, NT) * rk * rk.T
+        pairs.append(strict * linked * jnp.exp(jnp.minimum(gate - gate_row, 0.0)) * key_key)
+        key_ends = dot2r(k, jnp.concatenate([ends_ref[i, 0], ends_ref[i, 1]], axis=0), NT)
+        inners.append(v.astype(F32) - head * jnp.exp(gate) * rk * key_ends[:, :N])
+        dus.append(mg_ref[i] + tail * jnp.exp(gate[N - 1 : N, :] - gate) * rk * key_ends[:, N:])
+        betas.append(by_row(beta_row))
+    for i in heads:
+        us.append(dot3(inv_ref[i], betas[i] * inners[i], NN))
+        dxs.append(dot3(inv_ref[i], dus[i], TN))
+    for i in heads:
+        u_ref[i], dx_ref[i] = us[i], dxs[i]
+    dlogit = dlogit_s[...]
+    for i in heads:
+        dbeta = jnp.sum(dxs[i] * inners[i] - dot3(dxs[i], us[i], NT) * pairs[i], axis=1, keepdims=True)
+        dlogit = jnp.where(iota(1) == first + i, dbeta * betas[i] * (1.0 - betas[i]), dlogit)
+    dlogit_s[...] = dlogit
+
+    @pl.when(pl.program_id(0) == pl.num_programs(0) - 1)
+    def _():
+        count = beta_ref.shape[0]
+        per = N // count
+        rows = spread_ref.shape[0]
+        for first in range(0, rows, per):
+            total = jnp.zeros((N, N), F32)
+            for r in range(first, min(first + per, rows)):
+                moved = dlogit if r == first else pltpu.roll(dlogit, count * (r - first), 1)
+                total = total + dot2r(spread_ref[r], moved, NN)
+            dw_ref[:, 0, first * count : first * count + N] = total
+
+
+def grads_kernel(lens_ref, q_ref, k_ref, g_ref, ends_ref, u_ref, dx_ref, sum_ref, beta_ref, tw_ref,
+                 dq_ref, dk_ref, dv_ref, dgate_ref,
+                 linked_s, head_s, tail_s):
+    ctx = lax.axis_index("ctx")
+
+    @pl.when(pl.program_id(0) == 0)
+    def _():
+        linked_s[...], head_s[...], tail_s[...], unused = plan(lens_ref, ctx)
+
     linked, head, tail, tw = linked_s[...], head_s[...], tail_s[...], tw_ref[...]
-    strict = iota(0) > iota(1)
+    strict = jnp.where(iota(0) > iota(1), 1.0, 0.0)
     reach = iota(0) >= iota(1)
     last = jnp.where(lax.broadcasted_iota(jnp.int32, (N, 1), 0) == N - 1, 1.0, 0.0)
-    for i in range(HP):
-        h = pl.program_id(0) * HP + i
+    for i in range(HG):
+        h = pl.program_id(0) * HG + i
         cols = slice(i * N, (i + 1) * N)
-        q, k, v, g = q_ref[:, cols], k_ref[:, cols], v_ref[:, cols], g_ref[:, cols]
+        q, k, g = q_ref[:, cols], k_ref[:, cols], g_ref[:, cols]
         gate_row, beta_row = sum_ref[pl.ds(h, 1), :], beta_ref[pl.ds(h, 1), :]
         qn, kn, rq, rk, rk_cols, decay, key_key, query_key, from_head, to_tail, beta = head_terms(
             q, k, gate_row, beta_row, linked, head, tail)
-        state, grad = ends_ref[i, 0], ends_ref[i, 1]
-        inverse = inv_ref[i]
-        key_ends = dot2r(k, jnp.concatenate([state, grad], axis=0), NT)
-        inner = v.astype(F32) - from_head * rk * key_ends[:, :N]
-        u = dot3(inverse, beta * inner, NN)
-        du = mg_ref[i] + to_tail * rk * key_ends[:, N:]
-        dx = dot3(inverse, du, TN)
-        dinv = jnp.where(strict, -dot3(dx, u, NT), 0.0)
-        dmix = tw * dot2r(g, u, NT)
+        state, grad, u, dx = ends_ref[i, 0], ends_ref[i, 1], u_ref[i], dx_ref[i]
+        pair = -(strict * beta * decay) * dot3(dx, u, NT)
+        dqk = decay * (tw * dot2r(g, u, NT))
         dtail = dot3(u, grad, NN)
         gs = tw * dot2r(g, state, NN)
         dxs = dot3(dx, state, NN)
-        decay_dinv = decay * dinv
-        pair = beta * decay_dinv
-        dqk = decay * dmix
         both = dot2l(jnp.concatenate([dqk * rk_cols, (pair + pair.T) * rk_cols], axis=0), k, NN)
         dqn = from_head * gs + both[:N]
         dkn = dot2l(dqk * rq, q, TN) + to_tail * dtail - beta * from_head * dxs + both[N:]
         dq_ref[:, cols] = (rq * (dqn - qn * jnp.sum(dqn * qn, axis=1, keepdims=True))).astype(BF16)
         dk_ref[:, cols] = (rk * (dkn - kn * jnp.sum(dkn * kn, axis=1, keepdims=True))).astype(BF16)
         dv_ref[:, cols] = (beta * dx).astype(BF16)
-        dbeta = jnp.sum(dx * inner + decay_dinv * key_key, axis=1, keepdims=True)
-        dlogit_s[...] = jnp.where(iota(1) == h, dbeta * beta * (1.0 - beta), dlogit_s[...])
         spread = dqk * query_key + pair * key_key
         tails = jnp.sum(to_tail * dtail * kn, axis=1, keepdims=True)
         heads = jnp.sum(from_head * (gs * qn - beta * dxs * kn), axis=1, keepdims=True)
@@ -227,25 +274,14 @@
         dgamma = dgamma - by_row(jnp.sum(spread, axis=0, keepdims=True))
         dgate_ref[pl.ds(h, 1), :] = jnp.sum(jnp.where(reach, dgamma, 0.0), axis=0, keepdims=True)
 
-    @pl.when(pl.program_id(0) == pl.num_programs(0) - 1)
-    def _():
-        heads = beta_ref.shape[0]
-        per = N // heads
-        dlogit = dlogit_s[...]
-        rows = spread_ref.shape[0]
-        for first in range(0, rows, per):
-            total = jnp.zeros((N, N), F32)
-            for r in range(first, min(first + per, rows)):
-                moved = dlogit if r == first else pltpu.roll(dlogit, heads * (r - first), 1)
-                total = total + dot2r(spread_ref[r], moved, NN)
-            dw_ref[:, first * heads : first * heads + N] = total
-
-
-def sum_kernel(parts_ref, out_ref):
-    rows, heads = out_ref.shape
-    total = jnp.sum(parts_ref[...], axis=0, keepdims=True)
+
+def sum_kernel(parts_ref, out_ref, rows_s):
+    heads, rows = out_ref.shape
+    total = jnp.sum(parts_ref[:, 0, :], axis=0, keepdims=True)
+    rows_s[...] = jnp.zeros((N, N), F32)
     for r in range(rows):
-        out_ref[r : r + 1, :] = total[:, r * heads : (r + 1) * heads]
+        rows_s[r : r + 1, :heads] = total[:, r * heads : (r + 1) * heads]
+    out_ref[...] = rows_s[...].T[:heads, :rows]
 
 
 def whole(shape):
@@ -296,27 +332,42 @@
     )(owned)
     ends = to_owners(ends)
     spread = hidden_in.T.reshape(parts, owned_rows, tokens).transpose(1, 0, 2)
-    dq, dk, dv, dgate, dw = pl.pallas_call(
-        grads_kernel,
+    u, dx, dw = pl.pallas_call(
+        logits_kernel,
         grid=(heads // HP,),
-        in_specs=[smem] + [by_heads] * 4 + [square(2), one_square, one_square, whole((heads, N)), whole((heads, N)),
-                                            whole((N, N)), whole(spread.shape)],
-        out_specs=[by_heads] * 3 + [whole((heads, N)), whole((parts, tiles * N))],
-        out_shape=[jax.ShapeDtypeStruct((tokens, width), BF16)] * 3
-        + [jax.ShapeDtypeStruct((heads, N), F32), jax.ShapeDtypeStruct((parts, tiles * N), F32)],
+        in_specs=[smem] + [by_heads] * 3 + [square(2), one_square, one_square, whole((heads, N)), whole((heads, N)),
+                                            whole(spread.shape)],
+        out_specs=[one_square] * 2 + [whole((parts, 1, tiles * N))],
+        out_shape=[jax.ShapeDtypeStruct((heads, N, N), F32)] * 2
+        + [jax.ShapeDtypeStruct((parts, 1, tiles * N), F32)],
         scratch_shapes=masks + [pltpu.VMEM((N, N), F32)],
         compiler_params=params,
+        name="logit_grads",
+    )(lengths, queries, key_rows, value_rows, ends, inverse, mg, sums, beta, spread)
+    pieces = lax.all_to_all(dw, ("dp", "ctx"), 0, 0, tiled=True)
+    few_heads = pl.BlockSpec((tokens, HG * N), lambda i: (0, i))
+    few_squares = pl.BlockSpec((HG, N, N), lambda i: (i, 0, 0))
+    dq, dk, dv, dgate = pl.pallas_call(
+        grads_kernel,
+        grid=(heads // HG,),
+        in_specs=[smem] + [few_heads] * 3 + [pl.BlockSpec((HG, 2, N, N), lambda i: (i, 0, 0, 0)), few_squares, few_squares,
+                                             whole((heads, N)), whole((heads, N)), whole((N, N))],
+        out_specs=[few_heads] * 3 + [whole((heads, N))],
+        out_shape=[jax.ShapeDtypeStruct((tokens, width), BF16)] * 3 + [jax.ShapeDtypeStruct((heads, N), F32)],
+        scratch_shapes=masks,
+        compiler_params=params,
+        cost_estimate=pl.CostEstimate(flops=12_000_000_000, bytes_accessed=40_000_000, transcendentals=0),
         name="segment_grads",
-    )(lengths, queries, key_rows, value_rows, out_grad, ends, inverse, mg, sums, beta, tw, spread)
-    pieces = lax.all_to_all(dw, ("dp", "ctx"), 0, 0, tiled=True)
+    )(lengths, queries, key_rows, out_grad, ends, u, dx, sums, beta, tw)
     dweight = pl.pallas_call(
         sum_kernel,
-        out_shape=jax.ShapeDtypeStruct((owned_rows, heads), F32),
+        out_shape=jax.ShapeDtypeStruct((heads, owned_rows), F32),
         in_specs=[pl.BlockSpec(memory_space=pltpu.VMEM)],
         out_specs=pl.BlockSpec(memory_space=pltpu.VMEM),
+        scratch_shapes=[pltpu.VMEM((N, N), F32)],
         name="sum_parts",
     )(pieces)
-    return dq, dk, dv, dgate, dweight
+    return dq, dk, dv, dgate, dweight.T
 
 
 def solution(mesh):

time: 173 us -> 128 us (0.74)
  Pallas kernels: 69.1 us -> 36.7 us
  blocking collectives: 67.1 us -> 47.1 us
  starting transfers between devices: 3.85 us -> 13.2 us
  local copies, waits for them, and re-layouts: 5.95 us -> 3.42 us
    pallas_call x1, Pallas kernels: 45.4 us -> 13 us  [local(): pl.pallas_call(maps_kernel, grid=(heads // HP,), in_specs=[smem, smem, wh...]
    all_to_all x1 -> x0, blocking collectives: 20 us -> none  [local(): pieces = lax.all_to_all(dw, ('dp', 'ctx'), 0, 0, tiled=True)]
    all_to_all x0 -> x1, starting transfers between devices: none -> 9.34 us  [local(): pieces = lax.all_to_all(dw, ('dp', 'ctx'), 0, 0, tiled=True)]
    pallas_call x2 -> x3, Pallas kernels: 17.5 us -> 18.5 us  [the longest x1 9.78 us: local(): pl.pallas_call(grads_kernel, grid=(heads // HG,), in_specs=[smem] + [few_...]
  transfers between devices with their start and end apart: 1 -> 2, of which waited for: 1 -> 2; matrix products, arithmetic and copies ran while one was open for 1% -> 1% of each run, Pallas kernels for 0% -> 8%
where the time goes in v3:
time: 128 us
  blocking collectives  47.1 us (37%)
  Pallas kernels  36.7 us (29%)
  waiting for transfers between devices  26.8 us (21%)
  starting transfers between devices  13.2 us (10%)
  local copies, waits for them, and re-layouts  3.42 us (3%)
    all_to_all x1, blocking collectives, to_owners(): return lax.all_to_all(x, 'ctx', 0, 0, tiled=True)  47.1 us
    all_to_all x1, waiting for transfers between devices, to_owners(): return lax.all_to_all(x, 'ctx', 0, 0, tiled=True)  25.8 us
    pallas_call x1, Pallas kernels, local(): pl.pallas_call(maps_kernel, grid=(heads // HP,), in_specs=[smem, smem, wh...  13 us
    pallas_call x1, Pallas kernels, local(): pl.pallas_call(grads_kernel, grid=(heads // HG,), in_specs=[smem] + [few_...  9.78 us
    all_to_all x1, starting transfers between devices, local(): pieces = lax.all_to_all(dw, ('dp', 'ctx'), 0, 0, tiled=True)  9.34 us
    pallas_call x1, Pallas kernels, local(): pl.pallas_call(logits_kernel, grid=(heads // HP,), in_specs=[smem] + [by_...  6.96 us
    pallas_call x1, Pallas kernels, local(): pl.pallas_call(chains_kernel, out_shape=jax.ShapeDtypeStruct((owned.shape...  5.21 us
    all_to_all x1, starting transfers between devices, to_owners(): return lax.all_to_all(x, 'ctx', 0, 0, tiled=True)  3.85 us
  transfers between devices with their start and end apart: 2, of which 2 were waited for; matrix products, arithmetic and copies ran while one was open for 1% of the time, Pallas kernels for 8%

profile of v3, /device:TPU:1, one launch (start us, length us, event | category | flops | bytes accessed | tf_op | source)
XLA Modules:
  0.0 127.9 jit_solution(1500676817274580934)
XLA Ops:
  0.6 13.0 %segment_maps.1 = (f32[16,3,128,128]{3,2,1,0:T(8,128)}, f32[16,128,128]{2,1,0:T(8,128)}, f32[16,128,128]{2,1,0:T(8,128)}, f32[16,128]{1,0:T(8,128)}, f32[16,128]{1,0:T(8,128)}, /*index=5*/f32[128,128]{1,0:T(8,128)}) custom-call(s32[1,4]{1,0:T(1,128)} %lens_ref.5, s32[1,32]{1,0:T(1,128)} %bitcast.12, f32[1,32]{1,0:T(1,128)} %bitcast.14, s32[1,32]{1,0:T(1,128)} %bitcast.13, ...), custom_call_target="tpu_custom_call" | custom-call | tf_op jit(solution)/shard_map/segment_maps/pallas_call | solution.py:311
  13.6 47.1 %all_to_all.15.maps_ref = f32[16,3,128,128]{3,2,1,0:T(8,128)} all-to-all(f32[16,3,128,128]{3,2,1,0:T(8,128)} %get-tuple-element.18), channel_id=1, replica_groups=mesh['dp'=8,'ctx'=16] {'ctx'}, dimensions={0} | all-to-all | bytes 6291456 | tf_op jit(solution)/shard_map/all_to_all | solution.py:292
  60.8 5.2 %chains.1 = f32[16,2,128,128]{3,2,1,0:T(8,128)} custom-call(f32[16,3,128,128]{3,2,1,0:T(8,128)} %all_to_all.15.maps_ref), custom_call_target="tpu_custom_call" | custom-call | tf_op jit(solution)/shard_map/chains/pallas_call | solution.py:325
  66.0 0.0 copy-start.1
  66.0 3.8 %all-to-all-start.1 = ((f32[16,2,128,128]{3,2,1,0:T(8,128)}), f32[16,2,128,128]{3,2,1,0:T(8,128)S(1)}, u32[]{:S(2)}, u32[]{:S(2)}) async-start(f32[16,2,128,128]{3,2,1,0:T(8,128)} %chains.1), calls=%async_computation.1 | async-start | bytes 4194304 | tf_op jit(solution)/shard_map/all_to_all | solution.py:292
  69.8 0.0 copy-done.1
  69.8 0.3 copy.15
  70.1 0.2 reshape.21
  70.3 0.9 copy.18
  71.3 25.8 %all-to-all-done.1.ends_ref = f32[16,2,128,128]{3,2,1,0:T(8,128)S(1)} async-done(((f32[16,2,128,128]{3,2,1,0:T(8,128)}), f32[16,2,128,128]{3,2,1,0:T(8,128)S(1)}, u32[]{:S(2)}, u32[]{:S(2)}) %all-to-all-start.1) | async-done | bytes 2097184 | tf_op jit(solution)/shard_map/all_to_all | solution.py:292
  97.1 0.0 copy-start
  97.1 1.3 %copy-done = f32[16,2,128,128]{3,2,1,0:T(8,128)} copy-done((f32[16,2,128,128]{3,2,1,0:T(8,128)}, f32[16,2,128,128]{3,2,1,0:T(8,128)S(1)}, u32[]{:S(2)}) %copy-start) | copy-done | bytes 2097176
  98.4 7.0 %logit_grads.1 = (f32[16,128,128]{2,1,0:T(8,128)}, f32[16,128,128]{2,1,0:T(8,128)}, f32[128,1,384]{2,1,0:T(1,128)}) custom-call(s32[1,4]{1,0:T(1,128)} %lens_ref.5, bf16[128,2048]{1,0:T(8,128)(2,1)} %q_ref.5, bf16[128,2048]{1,0:T(8,128)(2,1)} %k_ref.5, bf16[128,2048]{1,0:T(8,128)(2,1)} %v_ref.3, f32[16,2,128,128]{3,2,1,0:T(8,128)} %copy-done, ...), custom_call_target="tpu_custom_call" | custom-call | tf_op jit(solution)/shard_map/logit_grads/pallas_call | solution.py:335
  105.4 9.3 %all-to-all-start.2 = ((f32[128,1,384]{2,1,0:T(1,128)}), f32[128,1,384]{2,1,0:T(1,128)S(1)}, u32[]{:S(2)}, u32[]{:S(2)}) async-start(f32[128,1,384]{2,1,0:T(1,128)} %get-tuple-element.30), calls=%async_computation.2 | async-start | bytes 393216 | tf_op jit(solution)/shard_map/all_to_all | solution.py:347
  114.7 9.8 %segment_grads.1 = (bf16[128,2048]{1,0:T(8,128)(2,1)}, bf16[128,2048]{1,0:T(8,128)(2,1)}, bf16[128,2048]{1,0:T(8,128)(2,1)}, f32[16,128]{1,0:T(8,128)}) custom-call(s32[1,4]{1,0:T(1,128)} %lens_ref.5, bf16[128,2048]{1,0:T(8,128)(2,1)} %q_ref.5, bf16[128,2048]{1,0:T(8,128)(2,1)} %k_ref.5, bf16[128,2048]{1,0:T(8,128)(2,1)} %g_ref.3, ...), custom_call_target="tpu_custom_call" | custom-call | flops 12000000000 | bytes 40000000 | tf_op jit(solution)/shard_map/segment_grads/pallas_call | solution.py:350
  124.5 1.0 all-to-all-done.2.parts_ref
  125.5 0.0 copy-start.2
  125.5 0.7 copy-done.2
  126.2 1.7 %sum_parts.1 = f32[16,18]{1,0:T(8,128)} custom-call(f32[128,1,384]{2,1,0:T(1,128)} %copy-done.2), custom_call_target="tpu_custom_call" | custom-call | tf_op jit(solution)/shard_map/sum_parts/pallas_call | solution.py:362
Async XLA Ops:
  66.0 3.9 %copy-start.1 = (bf16[128,2304]{1,0:T(8,128)(2,1)S(1)}, bf16[128,2304]{1,0:T(8,128)(2,1)}, u32[]{:S(2)}) copy-start(bf16[128,2304]{1,0:T(8,128)(2,1)} %hidden_ref.1) | copy-start | bytes 1769476
  66.0 31.1 %all-to-all-start.1 = ((f32[16,2,128,128]{3,2,1,0:T(8,128)}), f32[16,2,128,128]{3,2,1,0:T(8,128)S(1)}, u32[]{:S(2)}, u32[]{:S(2)}) async-start(f32[16,2,128,128]{3,2,1,0:T(8,128)} %chains.1), calls=%async_computation.1 | async-start | bytes 4194304 | tf_op jit(solution)/shard_map/all_to_all | solution.py:292
  97.1 1.3 %copy-start = (f32[16,2,128,128]{3,2,1,0:T(8,128)}, f32[16,2,128,128]{3,2,1,0:T(8,128)S(1)}, u32[]{:S(2)}) copy-start(f32[16,2,128,128]{3,2,1,0:T(8,128)S(1)} %all-to-all-done.1.ends_ref) | copy-start | bytes 6291460
  105.4 20.1 %all-to-all-start.2 = ((f32[128,1,384]{2,1,0:T(1,128)}), f32[128,1,384]{2,1,0:T(1,128)S(1)}, u32[]{:S(2)}, u32[]{:S(2)}) async-start(f32[128,1,384]{2,1,0:T(1,128)} %get-tuple-element.30), calls=%async_computation.2 | async-start | bytes 393216 | tf_op jit(solution)/shard_map/all_to_all | solution.py:347
  125.5 0.7 copy-start.2

commit v4 on v3

--- a/solution.py
+++ b/solution.py
@@ -11,6 +11,7 @@
 HP = 8
 HG = 4
 VMEM_LIMIT = 56 * 1024 * 1024
+VMEM_SMALL = 40 * 1024 * 1024
 NN = (((1,), (0,)), ((), ()))
 NT = (((1,), (1,)), ((), ()))
 TN = (((0,), (0,)), ((), ()))
@@ -26,10 +27,14 @@
 
 
 def dot3(a, b, dims):
-    (ka,), (kb,) = dims[0]
+    return parts_dot(jnp.concatenate(split(a), dims[0][0][0]), b, dims)
+
+
+def parts_dot(a_parts, b, dims):
+    kb = dims[0][1][0]
     n = b.shape[1 - kb]
     rights = jnp.concatenate(split(b), 1 - kb)
-    both = dot(jnp.concatenate(split(a), ka), jnp.concatenate([rights, rights], kb), dims)
+    both = dot(a_parts, jnp.concatenate([rights, rights], kb), dims)
     return both[:, :n] + both[:, n:]
 
 
@@ -124,7 +129,7 @@
 
 def maps_kernel(lens_ref, prompts_ref, rewards_row_ref, prompts_row_ref, gate_ref, weight_ref, hidden_ref,
                 q_ref, k_ref, v_ref, g_ref,
-                maps_ref, inv_ref, mg_ref, sum_ref, beta_ref, tw_ref,
+                maps_ref, inv_ref, sum_ref, beta_ref, tw_ref,
                 linked_s, head_s, tail_s):
     ctx, dp = lax.axis_index("ctx"), lax.axis_index("dp")
 
@@ -145,7 +150,7 @@
     linked, head, tail, tw = linked_s[...], head_s[...], tail_s[...], tw_ref[...]
     strict = jnp.where(iota(0) > iota(1), 1.0, 0.0)
     same = jnp.where(iota(0) == iota(1), 1.0, 0.0)
-    lowers, rest = [], []
+    lowers, rest, mgs = [], [], []
     for i in range(HP):
         h = pl.program_id(0) * HP + i
         cols = slice(i * N, (i + 1) * N)
@@ -154,7 +159,7 @@
         qn, kn, rq, rk, rk_cols, decay, key_key, query_key, from_head, to_tail, beta = head_terms(
             q, k, gate_row, beta_row, linked, head, tail)
         lowers.append(strict * (beta * decay * key_key))
-        mg_ref[i] = dot2l(decay * query_key * tw, g, TN)
+        mgs.append(dot2l(decay * query_key * tw, g, TN))
         maps_ref[i, 2] = dot2r(g, tw * from_head * qn, TN)
         maps_ref[i, 0] = from_head[N - 1 : N, :] * same
         rest.append((jnp.concatenate([beta * v.astype(F32), beta * from_head * kn], axis=1), to_tail * kn))
@@ -166,7 +171,7 @@
         ends = dot3(uzs[i], rest[i][1], TN)
         maps_ref[i, 0] -= ends[N:]
         maps_ref[i, 1] = ends[:N]
-        maps_ref[i, 2] -= dot3(mg_ref[i], uzs[i][:, N:], TN)
+        maps_ref[i, 2] -= dot3(mgs[i], uzs[i][:, N:], TN)
 
 
 def chains_kernel(maps_ref, out_ref):
@@ -182,47 +187,50 @@
             grad = dot3(grad, maps_ref[b, 0], NT) + maps_ref[b, 2]
 
 
-def logits_kernel(lens_ref, q_ref, k_ref, v_ref, ends_ref, inv_ref, mg_ref, sum_ref, beta_ref, spread_ref,
-                  u_ref, dx_ref, dw_ref,
-                  linked_s, head_s, tail_s, dlogit_s):
+def ahead_kernel(lens_ref, q_ref, k_ref, v_ref, g_ref, inv_ref, sum_ref, beta_ref, tw_ref,
+                 u0_ref, z_ref, dx0_ref, x_ref,
+                 linked_s, head_s, tail_s):
     ctx = lax.axis_index("ctx")
 
     @pl.when(pl.program_id(0) == 0)
     def _():
         linked_s[...], head_s[...], tail_s[...], unused = plan(lens_ref, ctx)
-        dlogit_s[...] = jnp.zeros((N, N), F32)
-
-    linked, head, tail = linked_s[...], head_s[...], tail_s[...]
-    strict = jnp.where(iota(0) > iota(1), 1.0, 0.0)
-    heads = range(HP)
-    first, inners, betas, pairs, dus, us, dxs = pl.program_id(0) * HP, [], [], [], [], [], []
-    for i in heads:
+
+    linked, head, tail, tw = linked_s[...], head_s[...], tail_s[...], tw_ref[...]
+    for i in range(HG):
+        h = pl.program_id(0) * HG + i
         cols = slice(i * N, (i + 1) * N)
-        q, k, v = q_ref[:, cols], k_ref[:, cols], v_ref[:, cols]
-        gate_row, beta_row = sum_ref[pl.ds(first + i, 1), :], beta_ref[pl.ds(first + i, 1), :]
-        kf = k.astype(F32)
-        rk = inverse_norm(kf)
-        gate = by_row(gate_row)
-        key_key = dot(k, k, NT) * rk * rk.T
-        pairs.append(strict * linked * jnp.exp(jnp.minimum(gate - gate_row, 0.0)) * key_key)
-        key_ends = dot2r(k, jnp.concatenate([ends_ref[i, 0], ends_ref[i, 1]], axis=0), NT)
-        inners.append(v.astype(F32) - head * jnp.exp(gate) * rk * key_ends[:, :N])
-        dus.append(mg_ref[i] + tail * jnp.exp(gate[N - 1 : N, :] - gate) * rk * key_ends[:, N:])
-        betas.append(by_row(beta_row))
-    for i in heads:
-        us.append(dot3(inv_ref[i], betas[i] * inners[i], NN))
-        dxs.append(dot3(inv_ref[i], dus[i], TN))
-    for i in heads:
-        u_ref[i], dx_ref[i] = us[i], dxs[i]
-    dlogit = dlogit_s[...]
-    for i in heads:
-        dbeta = jnp.sum(dxs[i] * inners[i] - dot3(dxs[i], us[i], NT) * pairs[i], axis=1, keepdims=True)
-        dlogit = jnp.where(iota(1) == first + i, dbeta * betas[i] * (1.0 - betas[i]), dlogit)
-    dlogit_s[...] = dlogit
+        q, k, v, g = q_ref[:, cols], k_ref[:, cols], v_ref[:, cols], g_ref[:, cols]
+        gate_row, beta_row = sum_ref[pl.ds(h, 1), :], beta_ref[pl.ds(h, 1), :]
+        qn, kn, rq, rk, rk_cols, decay, key_key, query_key, from_head, to_tail, beta = head_terms(
+            q, k, gate_row, beta_row, linked, head, tail)
+        uz = dot3(inv_ref[i], jnp.concatenate([beta * v.astype(F32), beta * from_head * kn], axis=1), NN)
+        u0_ref[i] = uz[:, :N]
+        z_ref[i] = jnp.concatenate(split(uz[:, N:]), axis=1)
+        mg = dot2l(decay * query_key * tw, g, TN)
+        dxx = dot3(inv_ref[i], jnp.concatenate([mg, to_tail * kn], axis=1), TN)
+        dx0_ref[i] = dxx[:, :N]
+        x_ref[i] = jnp.concatenate(split(dxx[:, N:]), axis=1)
+
+
+def logits_kernel(ends_ref, u0_ref, z_ref, dx0_ref, x_ref, beta_ref, spread_ref,
+                  u_ref, dx_ref, dw_ref, sums_s):
+    @pl.when(pl.program_id(0) == 0)
+    def _():
+        sums_s[...] = jnp.zeros((N, N), F32)
+
+    sums = sums_s[...]
+    for i in range(HP):
+        u = u0_ref[i] - parts_dot(z_ref[i], ends_ref[i, 0], NT)
+        dx = dx0_ref[i] + parts_dot(x_ref[i], ends_ref[i, 1], NT)
+        u_ref[i], dx_ref[i] = u, dx
+        sums = jnp.where(iota(1) == pl.program_id(0) * HP + i, jnp.sum(dx * u, axis=1, keepdims=True), sums)
+    sums_s[...] = sums
 
     @pl.when(pl.program_id(0) == pl.num_programs(0) - 1)
     def _():
         count = beta_ref.shape[0]
+        dlogit = sums * (1.0 - jnp.concatenate([beta_ref[...], jnp.zeros((N - count, N), F32)], axis=0).T)
         per = N // count
         rows = spread_ref.shape[0]
         for first in range(0, rows, per):
@@ -308,20 +316,36 @@
 
     one_square = pl.BlockSpec((HP, N, N), lambda i: (i, 0, 0))
     masks = [pltpu.VMEM((N, N), F32)] * 3
-    maps, inverse, mg, sums, beta, tw = pl.pallas_call(
+    maps, inverse, sums, beta, tw = pl.pallas_call(
         maps_kernel,
         grid=(heads // HP,),
         in_specs=[smem, smem, whole(rewards_row.shape), whole(prompts_row.shape), whole(log_gate.shape),
                   whole((heads, depth)), whole(hidden_in.shape)] + [by_heads] * 4,
-        out_specs=[square(3), one_square, one_square, whole((heads, N)), whole((heads, N)), whole((N, N))],
+        out_specs=[square(3), one_square, whole((heads, N)), whole((heads, N)), whole((N, N))],
         out_shape=[jax.ShapeDtypeStruct(s, F32) for s in (
-            (heads, 3, N, N), (heads, N, N), (heads, N, N), (heads, N), (heads, N), (N, N))],
+            (heads, 3, N, N), (heads, N, N), (heads, N), (heads, N), (N, N))],
         scratch_shapes=masks,
         compiler_params=params,
         name="segment_maps",
     )(lengths, prompts_row, rewards_row, prompts_row, log_gate, beta_weight.T, hidden_in,
       queries, key_rows, value_rows, out_grad)
     owned = to_owners(maps)
+    few_heads = pl.BlockSpec((tokens, HG * N), lambda i: (0, i))
+    few_squares = pl.BlockSpec((HG, N, N), lambda i: (i, 0, 0))
+    few_parts = pl.BlockSpec((HG, N, 2 * N), lambda i: (i, 0, 0))
+    half = jax.ShapeDtypeStruct((heads, N, N), F32)
+    in_parts = jax.ShapeDtypeStruct((heads, N, 2 * N), BF16)
+    u0, z, dx0, x = pl.pallas_call(
+        ahead_kernel,
+        grid=(heads // HG,),
+        in_specs=[smem] + [few_heads] * 4 + [few_squares, whole((heads, N)), whole((heads, N)), whole((N, N))],
+        out_specs=[few_squares, few_parts] * 2,
+        out_shape=[half, in_parts] * 2,
+        scratch_shapes=masks,
+        compiler_params=params,
+        cost_estimate=pl.CostEstimate(flops=12_000_000_000, bytes_accessed=40_000_000, transcendentals=0),
+        name="ahead",
+    )(lengths, queries, key_rows, value_rows, out_grad, inverse, sums, beta, tw)
     ends = pl.pallas_call(
         chains_kernel,
         out_shape=jax.ShapeDtypeStruct((owned.shape[0], 2, N, N), F32),
@@ -332,21 +356,18 @@
     )(owned)
     ends = to_owners(ends)
     spread = hidden_in.T.reshape(parts, owned_rows, tokens).transpose(1, 0, 2)
+    parts_spec = pl.BlockSpec((HP, N, 2 * N), lambda i: (i, 0, 0))
     u, dx, dw = pl.pallas_call(
         logits_kernel,
         grid=(heads // HP,),
-        in_specs=[smem] + [by_heads] * 3 + [square(2), one_square, one_square, whole((heads, N)), whole((heads, N)),
-                                            whole(spread.shape)],
+        in_specs=[square(2)] + [one_square, parts_spec] * 2 + [whole((heads, N)), whole(spread.shape)],
         out_specs=[one_square] * 2 + [whole((parts, 1, tiles * N))],
-        out_shape=[jax.ShapeDtypeStruct((heads, N, N), F32)] * 2
-        + [jax.ShapeDtypeStruct((parts, 1, tiles * N), F32)],
-        scratch_shapes=masks + [pltpu.VMEM((N, N), F32)],
+        out_shape=[half] * 2 + [jax.ShapeDtypeStruct((parts, 1, tiles * N), F32)],
+        scratch_shapes=[pltpu.VMEM((N, N), F32)],
         compiler_params=params,
         name="logit_grads",
-    )(lengths, queries, key_rows, value_rows, ends, inverse, mg, sums, beta, spread)
+    )(ends, u0, z, dx0, x, beta, spread)
     pieces = lax.all_to_all(dw, ("dp", "ctx"), 0, 0, tiled=True)
-    few_heads = pl.BlockSpec((tokens, HG * N), lambda i: (0, i))
-    few_squares = pl.BlockSpec((HG, N, N), lambda i: (i, 0, 0))
     dq, dk, dv, dgate = pl.pallas_call(
         grads_kernel,
         grid=(heads // HG,),
@@ -365,6 +386,7 @@
         in_specs=[pl.BlockSpec(memory_space=pltpu.VMEM)],
         out_specs=pl.BlockSpec(memory_space=pltpu.VMEM),
         scratch_shapes=[pltpu.VMEM((N, N), F32)],
+        compiler_params=pltpu.CompilerParams(vmem_limit_bytes=VMEM_SMALL),
         name="sum_parts",
     )(pieces)
     return dq, dk, dv, dgate, dweight.T

time: 128 us -> 126 us (0.984)
  waiting for transfers between devices: 26.8 us -> 19 us
  Pallas kernels: 36.7 us -> 42.5 us
    all_to_all x1, waiting for transfers between devices: 25.8 us -> 18 us  [to_owners(): return lax.all_to_all(x, 'ctx', 0, 0, tiled=True)]
    pallas_call x1 -> x2, Pallas kernels: 6.96 us -> 13.7 us  [the longest x1 7.79 us: local(): pl.pallas_call(ahead_kernel, grid=(heads // HG,), in_specs=[smem] + [few_...]
  transfers between devices with their start and end apart: 2 -> 2, of which waited for: 2 -> 2; matrix products, arithmetic and copies ran while one was open for 1% -> 1% of each run, Pallas kernels for 8% -> 14%
where the time goes in v4:
time: 126 us; the launch traced here: 125 us
  blocking collectives  47.1 us (37%)
  Pallas kernels  42.5 us (34%)
  waiting for transfers between devices  19 us (15%)
  starting transfers between devices  13.2 us (10%)
  local copies, waits for them, and re-layouts  2.79 us (2%)
    all_to_all x1, blocking collectives, to_owners(): return lax.all_to_all(x, 'ctx', 0, 0, tiled=True)  47.1 us
    all_to_all x1, waiting for transfers between devices, to_owners(): return lax.all_to_all(x, 'ctx', 0, 0, tiled=True)  18 us
    pallas_call x1, Pallas kernels, local(): pl.pallas_call(maps_kernel, grid=(heads // HP,), in_specs=[smem, smem, wh...  13 us
    pallas_call x1, Pallas kernels, local(): pl.pallas_call(grads_kernel, grid=(heads // HG,), in_specs=[smem] + [few_...  9.78 us
    all_to_all x1, starting transfers between devices, local(): pieces = lax.all_to_all(dw, ('dp', 'ctx'), 0, 0, tiled=True)  9.33 us
    pallas_call x1, Pallas kernels, local(): pl.pallas_call(ahead_kernel, grid=(heads // HG,), in_specs=[smem] + [few_...  7.79 us
    pallas_call x1, Pallas kernels, local(): pl.pallas_call(logits_kernel, grid=(heads // HP,), in_specs=[square(2)] +...  5.94 us
    pallas_call x1, Pallas kernels, local(): pl.pallas_call(chains_kernel, out_shape=jax.ShapeDtypeStruct((owned.shape...  5.21 us
  transfers between devices with their start and end apart: 2, of which 2 were waited for; matrix products, arithmetic and copies ran while one was open for 1% of the time, Pallas kernels for 14%

profile of v4, /device:TPU:1, one launch (start us, length us, event | category | flops | bytes accessed | tf_op | source)
XLA Modules:
  0.0 125.3 jit_solution(5542783460842019200)
XLA Ops:
  0.6 13.0 %segment_maps.1 = (f32[16,3,128,128]{3,2,1,0:T(8,128)}, f32[16,128,128]{2,1,0:T(8,128)}, f32[16,128]{1,0:T(8,128)}, f32[16,128]{1,0:T(8,128)}, f32[128,128]{1,0:T(8,128)}) custom-call(s32[1,4]{1,0:T(1,128)} %lens_ref.5, s32[1,32]{1,0:T(1,128)} %bitcast.12, f32[1,32]{1,0:T(1,128)} %bitcast.14, s32[1,32]{1,0:T(1,128)} %bitcast.13, f32[16,128]{1,0:T(8,128)} %gate_ref.1, ...), custom_call_target="tpu_custom_call" | custom-call | tf_op jit(solution)/shard_map/segment_maps/pallas_call | solution.py:319
  13.6 47.1 %all_to_all.15.maps_ref = f32[16,3,128,128]{3,2,1,0:T(8,128)} all-to-all(f32[16,3,128,128]{3,2,1,0:T(8,128)} %get-tuple-element.21), channel_id=1, replica_groups=mesh['dp'=8,'ctx'=16] {'ctx'}, dimensions={0} | all-to-all | bytes 6291456 | tf_op jit(solution)/shard_map/all_to_all | solution.py:300
  60.7 5.2 %chains.1 = f32[16,2,128,128]{3,2,1,0:T(8,128)} custom-call(f32[16,3,128,128]{3,2,1,0:T(8,128)} %all_to_all.15.maps_ref), custom_call_target="tpu_custom_call" | custom-call | tf_op jit(solution)/shard_map/chains/pallas_call | solution.py:349
  65.9 0.0 copy-start.1
  65.9 3.8 %all-to-all-start.1 = ((f32[16,2,128,128]{3,2,1,0:T(8,128)}), f32[16,2,128,128]{3,2,1,0:T(8,128)S(1)}, u32[]{:S(2)}, u32[]{:S(2)}) async-start(f32[16,2,128,128]{3,2,1,0:T(8,128)} %chains.1), calls=%async_computation.1 | async-start | bytes 4194304 | tf_op jit(solution)/shard_map/all_to_all | solution.py:300
  69.8 0.0 copy-done.1
  69.8 0.3 copy.15
  70.1 0.2 reshape.21
  70.3 1.0 copy.18
  71.3 7.8 %ahead.1 = (f32[16,128,128]{2,1,0:T(8,128)}, bf16[16,128,256]{2,1,0:T(8,128)(2,1)}, f32[16,128,128]{2,1,0:T(8,128)}, bf16[16,128,256]{2,1,0:T(8,128)(2,1)}) custom-call(s32[1,4]{1,0:T(1,128)} %lens_ref.5, bf16[128,2048]{1,0:T(8,128)(2,1)} %q_ref.5, bf16[128,2048]{1,0:T(8,128)(2,1)} %k_ref.5, bf16[128,2048]{1,0:T(8,128)(2,1)} %v_ref.3, ...), custom_call_target="tpu_custom_call" | custom-call | flops 12000000000 | bytes 40000000 | tf_op jit(solution)/shard_map/ahead/pallas_call | solution.py:338
  79.1 18.0 %all-to-all-done.1.ends_ref = f32[16,2,128,128]{3,2,1,0:T(8,128)S(1)} async-done(((f32[16,2,128,128]{3,2,1,0:T(8,128)}), f32[16,2,128,128]{3,2,1,0:T(8,128)S(1)}, u32[]{:S(2)}, u32[]{:S(2)}) %all-to-all-start.1) | async-done | bytes 2097184 | tf_op jit(solution)/shard_map/all_to_all | solution.py:300
  97.0 0.0 copy-start
  97.0 1.3 %copy-done = f32[16,2,128,128]{3,2,1,0:T(8,128)} copy-done((f32[16,2,128,128]{3,2,1,0:T(8,128)}, f32[16,2,128,128]{3,2,1,0:T(8,128)S(1)}, u32[]{:S(2)}) %copy-start) | copy-done | bytes 2097176
  98.4 5.9 %logit_grads.1 = (f32[16,128,128]{2,1,0:T(8,128)}, f32[16,128,128]{2,1,0:T(8,128)}, f32[128,1,384]{2,1,0:T(1,128)}) custom-call(f32[16,2,128,128]{3,2,1,0:T(8,128)} %copy-done, f32[16,128,128]{2,1,0:T(8,128)} %get-tuple-element.26.u0_ref, bf16[16,128,256]{2,1,0:T(8,128)(2,1)} %get-tuple-element.27.z_ref, f32[16,128,128]{2,1,0:T(8,128)} %get-tuple-element.28.dx0_ref, ...), custom_call_target="tpu_custom_call" | custom-call | tf_op jit(solution)/shard_map/logit_grads/pallas_call | solution.py:360
  104.3 9.3 %all-to-all-start.2 = ((f32[128,1,384]{2,1,0:T(1,128)}), f32[128,1,384]{2,1,0:T(1,128)S(1)}, u32[]{:S(2)}, u32[]{:S(2)}) async-start(f32[128,1,384]{2,1,0:T(1,128)} %get-tuple-element.36), calls=%async_computation.2 | async-start | bytes 393216 | tf_op jit(solution)/shard_map/all_to_all | solution.py:370
  113.6 9.8 %segment_grads.1 = (bf16[128,2048]{1,0:T(8,128)(2,1)}, bf16[128,2048]{1,0:T(8,128)(2,1)}, bf16[128,2048]{1,0:T(8,128)(2,1)}, f32[16,128]{1,0:T(8,128)}) custom-call(s32[1,4]{1,0:T(1,128)} %lens_ref.5, bf16[128,2048]{1,0:T(8,128)(2,1)} %q_ref.5, bf16[128,2048]{1,0:T(8,128)(2,1)} %k_ref.5, bf16[128,2048]{1,0:T(8,128)(2,1)} %g_ref.5, ...), custom_call_target="tpu_custom_call" | custom-call | flops 12000000000 | bytes 40000000 | tf_op jit(solution)/shard_map/segment_grads/pallas_call | solution.py:371
  123.4 1.0 all-to-all-done.2.parts_ref
  124.4 0.8 sum_parts.1
Async XLA Ops:
  65.9 3.9 %copy-start.1 = (bf16[128,2304]{1,0:T(8,128)(2,1)S(1)}, bf16[128,2304]{1,0:T(8,128)(2,1)}, u32[]{:S(2)}) copy-start(bf16[128,2304]{1,0:T(8,128)(2,1)} %hidden_ref.1) | copy-start | bytes 1769476
  65.9 31.1 %all-to-all-start.1 = ((f32[16,2,128,128]{3,2,1,0:T(8,128)}), f32[16,2,128,128]{3,2,1,0:T(8,128)S(1)}, u32[]{:S(2)}, u32[]{:S(2)}) async-start(f32[16,2,128,128]{3,2,1,0:T(8,128)} %chains.1), calls=%async_computation.1 | async-start | bytes 4194304 | tf_op jit(solution)/shard_map/all_to_all | solution.py:300
  97.0 1.3 %copy-start = (f32[16,2,128,128]{3,2,1,0:T(8,128)}, f32[16,2,128,128]{3,2,1,0:T(8,128)S(1)}, u32[]{:S(2)}) copy-start(f32[16,2,128,128]{3,2,1,0:T(8,128)S(1)} %all-to-all-done.1.ends_ref) | copy-start | bytes 6291460
  104.3 20.1 %all-to-all-start.2 = ((f32[128,1,384]{2,1,0:T(1,128)}), f32[128,1,384]{2,1,0:T(1,128)S(1)}, u32[]{:S(2)}, u32[]{:S(2)}) async-start(f32[128,1,384]{2,1,0:T(1,128)} %get-tuple-element.36), calls=%async_computation.2 | async-start | bytes 393216 | tf_op jit(solution)/shard_map/all_to_all | solution.py:370

commit v5 on v4

--- a/solution.py
+++ b/solution.py
@@ -9,9 +9,11 @@
 BF16 = jnp.bfloat16
 N = 128
 HP = 8
+HL = 4
 HG = 4
 VMEM_LIMIT = 56 * 1024 * 1024
-VMEM_SMALL = 40 * 1024 * 1024
+VMEM_MOST = 57 * 1024 * 1024
+VMEM_SMALL = 24 * 1024 * 1024
 NN = (((1,), (0,)), ((), ()))
 NT = (((1,), (1,)), ((), ()))
 TN = (((0,), (0,)), ((), ()))
@@ -174,17 +176,30 @@
         maps_ref[i, 2] -= dot3(mgs[i], uzs[i][:, N:], TN)
 
 
-def chains_kernel(maps_ref, out_ref):
-    count = maps_ref.shape[0]
+def chains_kernel(maps_any, out_any, maps_v, out_v, in_sem, out_sem):
+    count = maps_any.shape[0]
+    loads = [pltpu.make_async_copy(maps_any.at[j], maps_v.at[j], in_sem.at[j]) for j in range(count)]
+    for j in range(count // 2):
+        loads[j].start()
+        loads[count - 1 - j].start()
     state = jnp.zeros((N, N), F32)
     grad = jnp.zeros((N, N), F32)
+    stores = []
     for j in range(count):
         b = count - 1 - j
-        out_ref[j, 0] = state
-        out_ref[b, 1] = grad
+        out_v[j, 0] = state
+        out_v[b, 1] = grad
+        for at, kind in ((j, 0), (b, 1)):
+            stores.append(pltpu.make_async_copy(out_v.at[at, kind], out_any.at[at, kind], out_sem.at[at, kind]))
+            stores[-1].start()
+        if j < count // 2:
+            loads[j].wait()
+            loads[b].wait()
         if j < count - 1:
-            state = dot3(state, maps_ref[j, 0], NN) + maps_ref[j, 1]
-            grad = dot3(grad, maps_ref[b, 0], NT) + maps_ref[b, 2]
+            state = dot3(state, maps_v[j, 0], NN) + maps_v[j, 1]
+            grad = dot3(grad, maps_v[b, 0], NT) + maps_v[b, 2]
+    for store in stores:
+        store.wait()
 
 
 def ahead_kernel(lens_ref, q_ref, k_ref, v_ref, g_ref, inv_ref, sum_ref, beta_ref, tw_ref,
@@ -213,32 +228,42 @@
         x_ref[i] = jnp.concatenate(split(dxx[:, N:]), axis=1)
 
 
-def logits_kernel(ends_ref, u0_ref, z_ref, dx0_ref, x_ref, beta_ref, spread_ref,
-                  u_ref, dx_ref, dw_ref, sums_s):
-    @pl.when(pl.program_id(0) == 0)
-    def _():
-        sums_s[...] = jnp.zeros((N, N), F32)
-
-    sums = sums_s[...]
-    for i in range(HP):
-        u = u0_ref[i] - parts_dot(z_ref[i], ends_ref[i, 0], NT)
-        dx = dx0_ref[i] + parts_dot(x_ref[i], ends_ref[i, 1], NT)
-        u_ref[i], dx_ref[i] = u, dx
-        sums = jnp.where(iota(1) == pl.program_id(0) * HP + i, jnp.sum(dx * u, axis=1, keepdims=True), sums)
-    sums_s[...] = sums
-
-    @pl.when(pl.program_id(0) == pl.num_programs(0) - 1)
-    def _():
-        count = beta_ref.shape[0]
-        dlogit = sums * (1.0 - jnp.concatenate([beta_ref[...], jnp.zeros((N - count, N), F32)], axis=0).T)
-        per = N // count
-        rows = spread_ref.shape[0]
-        for first in range(0, rows, per):
-            total = jnp.zeros((N, N), F32)
-            for r in range(first, min(first + per, rows)):
-                moved = dlogit if r == first else pltpu.roll(dlogit, count * (r - first), 1)
-                total = total + dot2r(spread_ref[r], moved, NN)
-            dw_ref[:, 0, first * count : first * count + N] = total
+def logits_kernel(ends_any, u0_any, z_any, dx0_any, x_any, beta_ref, spread_ref,
+                  u_any, dx_any, dw_ref,
+                  ends_v, u0_v, z_v, dx0_v, x_v, u_v, dx_v, in_sem, out_sem):
+    heads = beta_ref.shape[0]
+    groups = heads // HL
+    sources = ((ends_any, ends_v), (u0_any, u0_v), (z_any, z_v), (dx0_any, dx0_v), (x_any, x_v))
+    loads, stores = [], []
+    for c in range(groups):
+        at = pl.ds(c * HL, HL)
+        loads.append([pltpu.make_async_copy(a.at[at], v.at[at], in_sem.at[c, n]) for n, (a, v) in enumerate(sources)])
+        for load in loads[-1]:
+            load.start()
+    sums = jnp.zeros((N, N), F32)
+    for c in range(groups):
+        for load in loads[c]:
+            load.wait()
+        for i in range(c * HL, c * HL + HL):
+            u = u0_v[i] - parts_dot(z_v[i], ends_v[i, 0], NT)
+            dx = dx0_v[i] + parts_dot(x_v[i], ends_v[i, 1], NT)
+            u_v[i], dx_v[i] = u, dx
+            sums = jnp.where(iota(1) == i, jnp.sum(dx * u, axis=1, keepdims=True), sums)
+        at = pl.ds(c * HL, HL)
+        for n, (v, a) in enumerate(((u_v, u_any), (dx_v, dx_any))):
+            stores.append(pltpu.make_async_copy(v.at[at], a.at[at], out_sem.at[c, n]))
+            stores[-1].start()
+    dlogit = sums * (1.0 - jnp.concatenate([beta_ref[...], jnp.zeros((N - heads, N), F32)], axis=0).T)
+    per = N // heads
+    rows = spread_ref.shape[0]
+    for first in range(0, rows, per):
+        total = jnp.zeros((N, N), F32)
+        for r in range(first, min(first + per, rows)):
+            moved = dlogit if r == first else pltpu.roll(dlogit, heads * (r - first), 1)
+            total = total + dot2r(spread_ref[r], moved, NN)
+        dw_ref[:, 0, first * heads : first * heads + N] = total
+    for store in stores:
+        store.wait()
 
 
 def grads_kernel(lens_ref, q_ref, k_ref, g_ref, ends_ref, u_ref, dx_ref, sum_ref, beta_ref, tw_ref,
@@ -346,25 +371,32 @@
         cost_estimate=pl.CostEstimate(flops=12_000_000_000, bytes_accessed=40_000_000, transcendentals=0),
         name="ahead",
     )(lengths, queries, key_rows, value_rows, out_grad, inverse, sums, beta, tw)
+    anywhere = pl.BlockSpec(memory_space=pl.ANY)
+    count = owned.shape[0]
     ends = pl.pallas_call(
         chains_kernel,
-        out_shape=jax.ShapeDtypeStruct((owned.shape[0], 2, N, N), F32),
-        in_specs=[pl.BlockSpec(memory_space=pltpu.VMEM)],
-        out_specs=pl.BlockSpec(memory_space=pltpu.VMEM),
-        compiler_params=params,
+        out_shape=jax.ShapeDtypeStruct((count, 2, N, N), F32),
+        in_specs=[anywhere],
+        out_specs=anywhere,
+        scratch_shapes=[pltpu.VMEM((count, 3, N, N), F32), pltpu.VMEM((count, 2, N, N), F32),
+                        pltpu.SemaphoreType.DMA((count,)), pltpu.SemaphoreType.DMA((count, 2))],
+        compiler_params=pltpu.CompilerParams(vmem_limit_bytes=VMEM_SMALL),
         name="chains",
     )(owned)
     ends = to_owners(ends)
     spread = hidden_in.T.reshape(parts, owned_rows, tokens).transpose(1, 0, 2)
-    parts_spec = pl.BlockSpec((HP, N, 2 * N), lambda i: (i, 0, 0))
+    vmem = pl.BlockSpec(memory_space=pltpu.VMEM)
+    kept = pl.BlockSpec(memory_space=pl.ANY)
     u, dx, dw = pl.pallas_call(
         logits_kernel,
-        grid=(heads // HP,),
-        in_specs=[square(2)] + [one_square, parts_spec] * 2 + [whole((heads, N)), whole(spread.shape)],
-        out_specs=[one_square] * 2 + [whole((parts, 1, tiles * N))],
+        in_specs=[anywhere] + [kept] * 4 + [vmem] * 2,
+        out_specs=[kept] * 2 + [vmem],
         out_shape=[half] * 2 + [jax.ShapeDtypeStruct((parts, 1, tiles * N), F32)],
-        scratch_shapes=[pltpu.VMEM((N, N), F32)],
-        compiler_params=params,
+        scratch_shapes=[pltpu.VMEM((heads, 2, N, N), F32)]
+        + [pltpu.VMEM((heads, N, N), F32), pltpu.VMEM((heads, N, 2 * N), BF16)] * 2
+        + [pltpu.VMEM((heads, N, N), F32)] * 2
+        + [pltpu.SemaphoreType.DMA((heads // HL, 5)), pltpu.SemaphoreType.DMA((heads // HL, 2))],
+        compiler_params=pltpu.CompilerParams(vmem_limit_bytes=VMEM_MOST),
         name="logit_grads",
     )(ends, u0, z, dx0, x, beta, spread)
     pieces = lax.all_to_all(dw, ("dp", "ctx"), 0, 0, tiled=True)

time: 126 us -> 129 us (1.024)
  Pallas kernels: 42.5 us -> 46 us
    pallas_call x2, Pallas kernels: 11.1 us -> 14.6 us  [the longest x1 8.06 us: local(): pl.pallas_call(chains_kernel, out_shape=jax.ShapeDtypeStruct((count, 2, N...]
where the time goes in v5:
time: 129 us
  blocking collectives  47 us (36%)
  Pallas kernels  46 us (36%)
  waiting for transfers between devices  19 us (15%)
  starting transfers between devices  13.2 us (10%)
  local copies, waits for them, and re-layouts  2.79 us (2%)
    all_to_all x1, blocking collectives, to_owners(): return lax.all_to_all(x, 'ctx', 0, 0, tiled=True)  47 us
    all_to_all x1, waiting for transfers between devices, to_owners(): return lax.all_to_all(x, 'ctx', 0, 0, tiled=True)  18 us
    pallas_call x1, Pallas kernels, local(): pl.pallas_call(maps_kernel, grid=(heads // HP,), in_specs=[smem, smem, wh...  13 us
    pallas_call x1, Pallas kernels, local(): pl.pallas_call(grads_kernel, grid=(heads // HG,), in_specs=[smem] + [few_...  9.8 us
    all_to_all x1, starting transfers between devices, local(): pieces = lax.all_to_all(dw, ('dp', 'ctx'), 0, 0, tiled=True)  9.34 us
    pallas_call x1, Pallas kernels, local(): pl.pallas_call(chains_kernel, out_shape=jax.ShapeDtypeStruct((count, 2, N...  8.06 us
    pallas_call x1, Pallas kernels, local(): pl.pallas_call(ahead_kernel, grid=(heads // HG,), in_specs=[smem] + [few_...  7.78 us
    pallas_call x1, Pallas kernels, local(): pl.pallas_call(logits_kernel, in_specs=[anywhere] + [kept] * 4 + [vmem] *...  6.57 us
  transfers between devices with their start and end apart: 2, of which 2 were waited for; matrix products, arithmetic and copies ran while one was open for 1% of the time, Pallas kernels for 14%

profile of v5, /device:TPU:1, one launch (start us, length us, event | category | flops | bytes accessed | tf_op | source)
XLA Modules:
  0.0 128.7 jit_solution(16866022903620926034)
XLA Ops:
  0.6 13.0 %segment_maps.1 = (f32[16,3,128,128]{3,2,1,0:T(8,128)}, f32[16,128,128]{2,1,0:T(8,128)}, f32[16,128]{1,0:T(8,128)}, f32[16,128]{1,0:T(8,128)}, f32[128,128]{1,0:T(8,128)}) custom-call(s32[1,4]{1,0:T(1,128)} %lens_ref.5, s32[1,32]{1,0:T(1,128)} %bitcast.12, f32[1,32]{1,0:T(1,128)} %bitcast.14, s32[1,32]{1,0:T(1,128)} %bitcast.13, f32[16,128]{1,0:T(8,128)} %gate_ref.1, ...), custom_call_target="tpu_custom_call" | custom-call | tf_op jit(solution)/shard_map/segment_maps/pallas_call | solution.py:344
  13.6 47.0 %all_to_all.15.maps_any = f32[16,3,128,128]{3,2,1,0:T(8,128)S(1)} all-to-all(f32[16,3,128,128]{3,2,1,0:T(8,128)} %get-tuple-element.21), channel_id=1, replica_groups=mesh['dp'=8,'ctx'=16] {'ctx'}, dimensions={0} | all-to-all | bytes 6291456 | tf_op jit(solution)/shard_map/all_to_all | solution.py:325
  60.6 8.1 %chains.1 = f32[16,2,128,128]{3,2,1,0:T(8,128)} custom-call(f32[16,3,128,128]{3,2,1,0:T(8,128)S(1)} %all_to_all.15.maps_any), custom_call_target="tpu_custom_call" | custom-call | tf_op jit(solution)/shard_map/chains/pallas_call | solution.py:376
  68.7 0.0 copy-start.1
  68.7 3.9 %all-to-all-start.1 = ((f32[16,2,128,128]{3,2,1,0:T(8,128)}), f32[16,2,128,128]{3,2,1,0:T(8,128)S(1)}, u32[]{:S(2)}, u32[]{:S(2)}) async-start(f32[16,2,128,128]{3,2,1,0:T(8,128)} %chains.1), calls=%async_computation.1 | async-start | bytes 4194304 | tf_op jit(solution)/shard_map/all_to_all | solution.py:325
  72.6 0.0 copy-done.1
  72.6 0.3 copy.15
  72.9 0.2 reshape.21
  73.1 1.0 copy.18
  74.0 7.8 %ahead.1 = (f32[16,128,128]{2,1,0:T(8,128)}, bf16[16,128,256]{2,1,0:T(8,128)(2,1)}, f32[16,128,128]{2,1,0:T(8,128)}, bf16[16,128,256]{2,1,0:T(8,128)(2,1)}) custom-call(s32[1,4]{1,0:T(1,128)} %lens_ref.5, bf16[128,2048]{1,0:T(8,128)(2,1)} %q_ref.5, bf16[128,2048]{1,0:T(8,128)(2,1)} %k_ref.5, bf16[128,2048]{1,0:T(8,128)(2,1)} %v_ref.3, ...), custom_call_target="tpu_custom_call" | custom-call | flops 12000000000 | bytes 40000000 | tf_op jit(solution)/shard_map/ahead/pallas_call | solution.py:363
  81.8 18.0 %all-to-all-done.1.ends_any.ends_ref = f32[16,2,128,128]{3,2,1,0:T(8,128)S(1)} async-done(((f32[16,2,128,128]{3,2,1,0:T(8,128)}), f32[16,2,128,128]{3,2,1,0:T(8,128)S(1)}, u32[]{:S(2)}, u32[]{:S(2)}) %all-to-all-start.1) | async-done | bytes 2097184 | tf_op jit(solution)/shard_map/all_to_all | solution.py:325
  99.8 0.0 copy-start
  99.8 1.3 %copy-done = f32[16,2,128,128]{3,2,1,0:T(8,128)} copy-done((f32[16,2,128,128]{3,2,1,0:T(8,128)}, f32[16,2,128,128]{3,2,1,0:T(8,128)S(1)}, u32[]{:S(2)}) %copy-start) | copy-done | bytes 2097176
  101.1 6.6 %logit_grads.1 = (f32[16,128,128]{2,1,0:T(8,128)}, f32[16,128,128]{2,1,0:T(8,128)}, f32[128,1,384]{2,1,0:T(1,128)}) custom-call(f32[16,2,128,128]{3,2,1,0:T(8,128)} %copy-done, f32[16,128,128]{2,1,0:T(8,128)} %get-tuple-element.26.u0_any, bf16[16,128,256]{2,1,0:T(8,128)(2,1)} %get-tuple-element.27.z_any, f32[16,128,128]{2,1,0:T(8,128)} %get-tuple-element.28.dx0_any, ...), custom_call_target="tpu_custom_call" | custom-call | tf_op jit(solution)/shard_map/logit_grads/pallas_call | solution.py:390
  107.7 9.3 %all-to-all-start.2 = ((f32[128,1,384]{2,1,0:T(1,128)}), f32[128,1,384]{2,1,0:T(1,128)S(1)}, u32[]{:S(2)}, u32[]{:S(2)}) async-start(f32[128,1,384]{2,1,0:T(1,128)} %get-tuple-element.36), calls=%async_computation.2 | async-start | bytes 393216 | tf_op jit(solution)/shard_map/all_to_all | solution.py:402
  117.1 9.8 %segment_grads.1 = (bf16[128,2048]{1,0:T(8,128)(2,1)}, bf16[128,2048]{1,0:T(8,128)(2,1)}, bf16[128,2048]{1,0:T(8,128)(2,1)}, f32[16,128]{1,0:T(8,128)}) custom-call(s32[1,4]{1,0:T(1,128)} %lens_ref.5, bf16[128,2048]{1,0:T(8,128)(2,1)} %q_ref.5, bf16[128,2048]{1,0:T(8,128)(2,1)} %k_ref.5, bf16[128,2048]{1,0:T(8,128)(2,1)} %g_ref.5, ...), custom_call_target="tpu_custom_call" | custom-call | flops 12000000000 | bytes 40000000 | tf_op jit(solution)/shard_map/segment_grads/pallas_call | solution.py:403
  126.9 1.0 all-to-all-done.2.parts_ref
  127.9 0.8 sum_parts.1
Async XLA Ops:
  68.7 3.9 %copy-start.1 = (bf16[128,2304]{1,0:T(8,128)(2,1)S(1)}, bf16[128,2304]{1,0:T(8,128)(2,1)}, u32[]{:S(2)}) copy-start(bf16[128,2304]{1,0:T(8,128)(2,1)} %hidden_ref.1) | copy-start | bytes 1769476
  68.7 31.1 %all-to-all-start.1 = ((f32[16,2,128,128]{3,2,1,0:T(8,128)}), f32[16,2,128,128]{3,2,1,0:T(8,128)S(1)}, u32[]{:S(2)}, u32[]{:S(2)}) async-start(f32[16,2,128,128]{3,2,1,0:T(8,128)} %chains.1), calls=%async_computation.1 | async-start | bytes 4194304 | tf_op jit(solution)/shard_map/all_to_all | solution.py:325
  99.8 1.3 %copy-start = (f32[16,2,128,128]{3,2,1,0:T(8,128)}, f32[16,2,128,128]{3,2,1,0:T(8,128)S(1)}, u32[]{:S(2)}) copy-start(f32[16,2,128,128]{3,2,1,0:T(8,128)S(1)} %all-to-all-done.1.ends_any.ends_ref) | copy-start | bytes 6291460
  107.7 20.2 %all-to-all-start.2 = ((f32[128,1,384]{2,1,0:T(1,128)}), f32[128,1,384]{2,1,0:T(1,128)S(1)}, u32[]{:S(2)}, u32[]{:S(2)}) async-start(f32[128,1,384]{2,1,0:T(1,128)} %get-tuple-element.36), calls=%async_computation.2 | async-start | bytes 393216 | tf_op jit(solution)/shard_map/all_to_all | solution.py:402

commit v6 on v4

--- a/solution.py
+++ b/solution.py
@@ -11,7 +11,7 @@
 HP = 8
 HG = 4
 VMEM_LIMIT = 56 * 1024 * 1024
-VMEM_SMALL = 40 * 1024 * 1024
+VMEM_SMALL = 24 * 1024 * 1024
 NN = (((1,), (0,)), ((), ()))
 NT = (((1,), (1,)), ((), ()))
 TN = (((0,), (0,)), ((), ()))
@@ -351,7 +351,7 @@
         out_shape=jax.ShapeDtypeStruct((owned.shape[0], 2, N, N), F32),
         in_specs=[pl.BlockSpec(memory_space=pltpu.VMEM)],
         out_specs=pl.BlockSpec(memory_space=pltpu.VMEM),
-        compiler_params=params,
+        compiler_params=pltpu.CompilerParams(vmem_limit_bytes=VMEM_SMALL),
         name="chains",
     )(owned)
     ends = to_owners(ends)

time: 126 us -> 124 us (0.984)
  Pallas kernels: 42.5 us -> 40.6 us
    pallas_call x1, Pallas kernels: 5.21 us -> 3.32 us  [local(): pl.pallas_call(chains_kernel, out_shape=jax.ShapeDtypeStruct((owned.shape...]
where the time goes in v6:
time: 124 us; the launch traced here: 123 us
  blocking collectives  47 us (38%)
  Pallas kernels  40.6 us (33%)
  waiting for transfers between devices  19 us (15%)
  starting transfers between devices  13.2 us (11%)
  local copies, waits for them, and re-layouts  2.79 us (2%)
    all_to_all x1, blocking collectives, to_owners(): return lax.all_to_all(x, 'ctx', 0, 0, tiled=True)  47 us
    all_to_all x1, waiting for transfers between devices, to_owners(): return lax.all_to_all(x, 'ctx', 0, 0, tiled=True)  18 us
    pallas_call x1, Pallas kernels, local(): pl.pallas_call(maps_kernel, grid=(heads // HP,), in_specs=[smem, smem, wh...  13 us
    pallas_call x1, Pallas kernels, local(): pl.pallas_call(grads_kernel, grid=(heads // HG,), in_specs=[smem] + [few_...  9.78 us
    all_to_all x1, starting transfers between devices, local(): pieces = lax.all_to_all(dw, ('dp', 'ctx'), 0, 0, tiled=True)  9.34 us
    pallas_call x1, Pallas kernels, local(): pl.pallas_call(ahead_kernel, grid=(heads // HG,), in_specs=[smem] + [few_...  7.77 us
    pallas_call x1, Pallas kernels, local(): pl.pallas_call(logits_kernel, grid=(heads // HP,), in_specs=[square(2)] +...  5.93 us
    all_to_all x1, starting transfers between devices, to_owners(): return lax.all_to_all(x, 'ctx', 0, 0, tiled=True)  3.85 us
  transfers between devices with their start and end apart: 2, of which 2 were waited for; matrix products, arithmetic and copies ran while one was open for 1% of the time, Pallas kernels for 14%

profile of v6, /device:TPU:1, one launch (start us, length us, event | category | flops | bytes accessed | tf_op | source)
XLA Modules:
  0.0 123.3 jit_solution(9278003426560886280)
XLA Ops:
  0.6 13.0 %segment_maps.1 = (f32[16,3,128,128]{3,2,1,0:T(8,128)}, f32[16,128,128]{2,1,0:T(8,128)}, f32[16,128]{1,0:T(8,128)}, f32[16,128]{1,0:T(8,128)}, f32[128,128]{1,0:T(8,128)}) custom-call(s32[1,4]{1,0:T(1,128)} %lens_ref.5, s32[1,32]{1,0:T(1,128)} %bitcast.12, f32[1,32]{1,0:T(1,128)} %bitcast.14, s32[1,32]{1,0:T(1,128)} %bitcast.13, f32[16,128]{1,0:T(8,128)} %gate_ref.1, ...), custom_call_target="tpu_custom_call" | custom-call | tf_op jit(solution)/shard_map/segment_maps/pallas_call | solution.py:319
  13.6 47.0 %all_to_all.15.maps_ref = f32[16,3,128,128]{3,2,1,0:T(8,128)S(1)} all-to-all(f32[16,3,128,128]{3,2,1,0:T(8,128)} %get-tuple-element.21), channel_id=1, replica_groups=mesh['dp'=8,'ctx'=16] {'ctx'}, dimensions={0} | all-to-all | bytes 6291456 | tf_op jit(solution)/shard_map/all_to_all | solution.py:300
  60.6 3.3 %chains.1 = f32[16,2,128,128]{3,2,1,0:T(8,128)} custom-call(f32[16,3,128,128]{3,2,1,0:T(8,128)S(1)} %all_to_all.15.maps_ref), custom_call_target="tpu_custom_call" | custom-call | tf_op jit(solution)/shard_map/chains/pallas_call | solution.py:349
  63.9 0.0 copy-start.1
  64.0 3.8 %all-to-all-start.1 = ((f32[16,2,128,128]{3,2,1,0:T(8,128)}), f32[16,2,128,128]{3,2,1,0:T(8,128)S(1)}, u32[]{:S(2)}, u32[]{:S(2)}) async-start(f32[16,2,128,128]{3,2,1,0:T(8,128)} %chains.1), calls=%async_computation.1 | async-start | bytes 4194304 | tf_op jit(solution)/shard_map/all_to_all | solution.py:300
  67.8 0.0 copy-done.1
  67.8 0.3 copy.15
  68.1 0.2 reshape.21
  68.3 1.0 copy.18
  69.3 7.8 %ahead.1 = (f32[16,128,128]{2,1,0:T(8,128)}, bf16[16,128,256]{2,1,0:T(8,128)(2,1)}, f32[16,128,128]{2,1,0:T(8,128)}, bf16[16,128,256]{2,1,0:T(8,128)(2,1)}) custom-call(s32[1,4]{1,0:T(1,128)} %lens_ref.5, bf16[128,2048]{1,0:T(8,128)(2,1)} %q_ref.5, bf16[128,2048]{1,0:T(8,128)(2,1)} %k_ref.5, bf16[128,2048]{1,0:T(8,128)(2,1)} %v_ref.3, ...), custom_call_target="tpu_custom_call" | custom-call | flops 12000000000 | bytes 40000000 | tf_op jit(solution)/shard_map/ahead/pallas_call | solution.py:338
  77.0 18.0 %all-to-all-done.1.ends_ref = f32[16,2,128,128]{3,2,1,0:T(8,128)S(1)} async-done(((f32[16,2,128,128]{3,2,1,0:T(8,128)}), f32[16,2,128,128]{3,2,1,0:T(8,128)S(1)}, u32[]{:S(2)}, u32[]{:S(2)}) %all-to-all-start.1) | async-done | bytes 2097184 | tf_op jit(solution)/shard_map/all_to_all | solution.py:300
  95.0 0.0 copy-start
  95.0 1.3 %copy-done = f32[16,2,128,128]{3,2,1,0:T(8,128)} copy-done((f32[16,2,128,128]{3,2,1,0:T(8,128)}, f32[16,2,128,128]{3,2,1,0:T(8,128)S(1)}, u32[]{:S(2)}) %copy-start) | copy-done | bytes 2097176
  96.4 5.9 %logit_grads.1 = (f32[16,128,128]{2,1,0:T(8,128)}, f32[16,128,128]{2,1,0:T(8,128)}, f32[128,1,384]{2,1,0:T(1,128)}) custom-call(f32[16,2,128,128]{3,2,1,0:T(8,128)} %copy-done, f32[16,128,128]{2,1,0:T(8,128)} %get-tuple-element.26.u0_ref, bf16[16,128,256]{2,1,0:T(8,128)(2,1)} %get-tuple-element.27.z_ref, f32[16,128,128]{2,1,0:T(8,128)} %get-tuple-element.28.dx0_ref, ...), custom_call_target="tpu_custom_call" | custom-call | tf_op jit(solution)/shard_map/logit_grads/pallas_call | solution.py:360
  102.3 9.3 %all-to-all-start.2 = ((f32[128,1,384]{2,1,0:T(1,128)}), f32[128,1,384]{2,1,0:T(1,128)S(1)}, u32[]{:S(2)}, u32[]{:S(2)}) async-start(f32[128,1,384]{2,1,0:T(1,128)} %get-tuple-element.36), calls=%async_computation.2 | async-start | bytes 393216 | tf_op jit(solution)/shard_map/all_to_all | solution.py:370
  111.7 9.8 %segment_grads.1 = (bf16[128,2048]{1,0:T(8,128)(2,1)}, bf16[128,2048]{1,0:T(8,128)(2,1)}, bf16[128,2048]{1,0:T(8,128)(2,1)}, f32[16,128]{1,0:T(8,128)}) custom-call(s32[1,4]{1,0:T(1,128)} %lens_ref.5, bf16[128,2048]{1,0:T(8,128)(2,1)} %q_ref.5, bf16[128,2048]{1,0:T(8,128)(2,1)} %k_ref.5, bf16[128,2048]{1,0:T(8,128)(2,1)} %g_ref.5, ...), custom_call_target="tpu_custom_call" | custom-call | flops 12000000000 | bytes 40000000 | tf_op jit(solution)/shard_map/segment_grads/pallas_call | solution.py:371
  121.4 1.0 all-to-all-done.2.parts_ref
  122.5 0.8 sum_parts.1
Async XLA Ops:
  63.9 3.9 %copy-start.1 = (bf16[128,2304]{1,0:T(8,128)(2,1)S(1)}, bf16[128,2304]{1,0:T(8,128)(2,1)}, u32[]{:S(2)}) copy-start(bf16[128,2304]{1,0:T(8,128)(2,1)} %hidden_ref.1) | copy-start | bytes 1769476
  64.0 31.1 %all-to-all-start.1 = ((f32[16,2,128,128]{3,2,1,0:T(8,128)}), f32[16,2,128,128]{3,2,1,0:T(8,128)S(1)}, u32[]{:S(2)}, u32[]{:S(2)}) async-start(f32[16,2,128,128]{3,2,1,0:T(8,128)} %chains.1), calls=%async_computation.1 | async-start | bytes 4194304 | tf_op jit(solution)/shard_map/all_to_all | solution.py:300
  95.0 1.3 %copy-start = (f32[16,2,128,128]{3,2,1,0:T(8,128)}, f32[16,2,128,128]{3,2,1,0:T(8,128)S(1)}, u32[]{:S(2)}) copy-start(f32[16,2,128,128]{3,2,1,0:T(8,128)S(1)} %all-to-all-done.1.ends_ref) | copy-start | bytes 6291460
  102.3 20.2 %all-to-all-start.2 = ((f32[128,1,384]{2,1,0:T(1,128)}), f32[128,1,384]{2,1,0:T(1,128)S(1)}, u32[]{:S(2)}, u32[]{:S(2)}) async-start(f32[128,1,384]{2,1,0:T(1,128)} %get-tuple-element.36), calls=%async_computation.2 | async-start | bytes 393216 | tf_op jit(solution)/shard_map/all_to_all | solution.py:370

commit v7 on v6

--- a/solution.py
+++ b/solution.py
@@ -11,6 +11,7 @@
 HP = 8
 HG = 4
 VMEM_LIMIT = 56 * 1024 * 1024
+VMEM_MID = 48 * 1024 * 1024
 VMEM_SMALL = 24 * 1024 * 1024
 NN = (((1,), (0,)), ((), ()))
 NT = (((1,), (1,)), ((), ()))
@@ -188,7 +189,7 @@
 
 
 def ahead_kernel(lens_ref, q_ref, k_ref, v_ref, g_ref, inv_ref, sum_ref, beta_ref, tw_ref,
-                 u0_ref, z_ref, dx0_ref, x_ref,
+                 pre_ref,
                  linked_s, head_s, tail_s):
     ctx = lax.axis_index("ctx")
 
@@ -205,25 +206,23 @@
         qn, kn, rq, rk, rk_cols, decay, key_key, query_key, from_head, to_tail, beta = head_terms(
             q, k, gate_row, beta_row, linked, head, tail)
         uz = dot3(inv_ref[i], jnp.concatenate([beta * v.astype(F32), beta * from_head * kn], axis=1), NN)
-        u0_ref[i] = uz[:, :N]
-        z_ref[i] = jnp.concatenate(split(uz[:, N:]), axis=1)
+        pre_ref[i, 0], pre_ref[i, 2] = uz[:, :N], uz[:, N:]
         mg = dot2l(decay * query_key * tw, g, TN)
         dxx = dot3(inv_ref[i], jnp.concatenate([mg, to_tail * kn], axis=1), TN)
-        dx0_ref[i] = dxx[:, :N]
-        x_ref[i] = jnp.concatenate(split(dxx[:, N:]), axis=1)
-
-
-def logits_kernel(ends_ref, u0_ref, z_ref, dx0_ref, x_ref, beta_ref, spread_ref,
-                  u_ref, dx_ref, dw_ref, sums_s):
+        pre_ref[i, 1], pre_ref[i, 3] = dxx[:, :N], dxx[:, N:]
+
+
+def logits_kernel(ends_ref, pre_ref, beta_ref, spread_ref,
+                  udx_ref, dw_ref, sums_s):
     @pl.when(pl.program_id(0) == 0)
     def _():
         sums_s[...] = jnp.zeros((N, N), F32)
 
     sums = sums_s[...]
     for i in range(HP):
-        u = u0_ref[i] - parts_dot(z_ref[i], ends_ref[i, 0], NT)
-        dx = dx0_ref[i] + parts_dot(x_ref[i], ends_ref[i, 1], NT)
-        u_ref[i], dx_ref[i] = u, dx
+        u = pre_ref[i, 0] - dot3(pre_ref[i, 2], ends_ref[i, 0], NT)
+        dx = pre_ref[i, 1] + dot3(pre_ref[i, 3], ends_ref[i, 1], NT)
+        udx_ref[i, 0], udx_ref[i, 1] = u, dx
         sums = jnp.where(iota(1) == pl.program_id(0) * HP + i, jnp.sum(dx * u, axis=1, keepdims=True), sums)
     sums_s[...] = sums
 
@@ -241,7 +240,7 @@
             dw_ref[:, 0, first * count : first * count + N] = total
 
 
-def grads_kernel(lens_ref, q_ref, k_ref, g_ref, ends_ref, u_ref, dx_ref, sum_ref, beta_ref, tw_ref,
+def grads_kernel(lens_ref, q_ref, k_ref, g_ref, ends_ref, udx_ref, sum_ref, beta_ref, tw_ref,
                  dq_ref, dk_ref, dv_ref, dgate_ref,
                  linked_s, head_s, tail_s):
     ctx = lax.axis_index("ctx")
@@ -261,7 +260,7 @@
         gate_row, beta_row = sum_ref[pl.ds(h, 1), :], beta_ref[pl.ds(h, 1), :]
         qn, kn, rq, rk, rk_cols, decay, key_key, query_key, from_head, to_tail, beta = head_terms(
             q, k, gate_row, beta_row, linked, head, tail)
-        state, grad, u, dx = ends_ref[i, 0], ends_ref[i, 1], u_ref[i], dx_ref[i]
+        state, grad, u, dx = ends_ref[i, 0], ends_ref[i, 1], udx_ref[i, 0], udx_ref[i, 1]
         pair = -(strict * beta * decay) * dot3(dx, u, NT)
         dqk = decay * (tw * dot2r(g, u, NT))
         dtail = dot3(u, grad, NN)
@@ -332,15 +331,13 @@
     owned = to_owners(maps)
     few_heads = pl.BlockSpec((tokens, HG * N), lambda i: (0, i))
     few_squares = pl.BlockSpec((HG, N, N), lambda i: (i, 0, 0))
-    few_parts = pl.BlockSpec((HG, N, 2 * N), lambda i: (i, 0, 0))
-    half = jax.ShapeDtypeStruct((heads, N, N), F32)
-    in_parts = jax.ShapeDtypeStruct((heads, N, 2 * N), BF16)
-    u0, z, dx0, x = pl.pallas_call(
+    few_pre = pl.BlockSpec((HG, 4, N, N), lambda i: (i, 0, 0, 0))
+    pre = pl.pallas_call(
         ahead_kernel,
         grid=(heads // HG,),
         in_specs=[smem] + [few_heads] * 4 + [few_squares, whole((heads, N)), whole((heads, N)), whole((N, N))],
-        out_specs=[few_squares, few_parts] * 2,
-        out_shape=[half, in_parts] * 2,
+        out_specs=few_pre,
+        out_shape=jax.ShapeDtypeStruct((heads, 4, N, N), F32),
         scratch_shapes=masks,
         compiler_params=params,
         cost_estimate=pl.CostEstimate(flops=12_000_000_000, bytes_accessed=40_000_000, transcendentals=0),
@@ -356,22 +353,22 @@
     )(owned)
     ends = to_owners(ends)
     spread = hidden_in.T.reshape(parts, owned_rows, tokens).transpose(1, 0, 2)
-    parts_spec = pl.BlockSpec((HP, N, 2 * N), lambda i: (i, 0, 0))
-    u, dx, dw = pl.pallas_call(
+    udx, dw = pl.pallas_call(
         logits_kernel,
         grid=(heads // HP,),
-        in_specs=[square(2)] + [one_square, parts_spec] * 2 + [whole((heads, N)), whole(spread.shape)],
-        out_specs=[one_square] * 2 + [whole((parts, 1, tiles * N))],
-        out_shape=[half] * 2 + [jax.ShapeDtypeStruct((parts, 1, tiles * N), F32)],
+        in_specs=[square(2), square(4)] + [whole((heads, N)), whole(spread.shape)],
+        out_specs=[square(2)] + [whole((parts, 1, tiles * N))],
+        out_shape=[jax.ShapeDtypeStruct((heads, 4, N, N), F32)] + [jax.ShapeDtypeStruct((parts, 1, tiles * N), F32)],
         scratch_shapes=[pltpu.VMEM((N, N), F32)],
-        compiler_params=params,
+        compiler_params=pltpu.CompilerParams(vmem_limit_bytes=VMEM_MID),
+        input_output_aliases={1: 0},
         name="logit_grads",
-    )(ends, u0, z, dx0, x, beta, spread)
+    )(ends, pre, beta, spread)
     pieces = lax.all_to_all(dw, ("dp", "ctx"), 0, 0, tiled=True)
     dq, dk, dv, dgate = pl.pallas_call(
         grads_kernel,
         grid=(heads // HG,),
-        in_specs=[smem] + [few_heads] * 3 + [pl.BlockSpec((HG, 2, N, N), lambda i: (i, 0, 0, 0)), few_squares, few_squares,
+        in_specs=[smem] + [few_heads] * 3 + [pl.BlockSpec((HG, 2, N, N), lambda i: (i, 0, 0, 0))] * 2 + [
                                              whole((heads, N)), whole((heads, N)), whole((N, N))],
         out_specs=[few_heads] * 3 + [whole((heads, N))],
         out_shape=[jax.ShapeDtypeStruct((tokens, width), BF16)] * 3 + [jax.ShapeDtypeStruct((heads, N), F32)],
@@ -379,7 +376,7 @@
         compiler_params=params,
         cost_estimate=pl.CostEstimate(flops=12_000_000_000, bytes_accessed=40_000_000, transcendentals=0),
         name="segment_grads",
-    )(lengths, queries, key_rows, out_grad, ends, u, dx, sums, beta, tw)
+    )(lengths, queries, key_rows, out_grad, ends, udx, sums, beta, tw)
     dweight = pl.pallas_call(
         sum_kernel,
         out_shape=jax.ShapeDtypeStruct((heads, owned_rows), F32),

time: 124 us -> 122 us (0.984)
    unnamed x4 -> x6, local copies, waits for them, and re-layouts: 1.34 us -> 0.01 us
    all_to_all x1, waiting for transfers between devices: 18 us -> 16.7 us  [to_owners(): return lax.all_to_all(x, 'ctx', 0, 0, tiled=True)]
  transfers between devices with their start and end apart: 2 -> 2, of which waited for: 2 -> 2; matrix products, arithmetic and copies ran while one was open for 1% -> 2% of each run, Pallas kernels for 14% -> 15%
where the time goes in v7:
time: 122 us
  blocking collectives  47 us (39%)
  Pallas kernels  40.7 us (33%)
  waiting for transfers between devices  17.8 us (15%)
  starting transfers between devices  13.2 us (11%)
  local copies, waits for them, and re-layouts  2.42 us (2%)
    all_to_all x1, blocking collectives, to_owners(): return lax.all_to_all(x, 'ctx', 0, 0, tiled=True)  47 us
    all_to_all x1, waiting for transfers between devices, to_owners(): return lax.all_to_all(x, 'ctx', 0, 0, tiled=True)  16.7 us
    pallas_call x1, Pallas kernels, local(): pl.pallas_call(maps_kernel, grid=(heads // HP,), in_specs=[smem, smem, wh...  13 us
    pallas_call x1, Pallas kernels, local(): pl.pallas_call(grads_kernel, grid=(heads // HG,), in_specs=[smem] + [few_...  9.69 us
    all_to_all x1, starting transfers between devices, local(): pieces = lax.all_to_all(dw, ('dp', 'ctx'), 0, 0, tiled=True)  9.33 us
    pallas_call x1, Pallas kernels, local(): pl.pallas_call(ahead_kernel, grid=(heads // HG,), in_specs=[smem] + [few_...  8.05 us
    pallas_call x1, Pallas kernels, local(): pl.pallas_call(logits_kernel, grid=(heads // HP,), in_specs=[square(2), s...  5.88 us
    all_to_all x1, starting transfers between devices, to_owners(): return lax.all_to_all(x, 'ctx', 0, 0, tiled=True)  3.85 us
  transfers between devices with their start and end apart: 2, of which 2 were waited for; matrix products, arithmetic and copies ran while one was open for 2% of the time, Pallas kernels for 15%

profile of v7, /device:TPU:1, one launch (start us, length us, event | category | flops | bytes accessed | tf_op | source)
XLA Modules:
  0.0 121.9 jit_solution(11225510070056770272)
XLA Ops:
  0.6 13.0 %segment_maps.1 = (f32[16,3,128,128]{3,2,1,0:T(8,128)}, f32[16,128,128]{2,1,0:T(8,128)}, f32[16,128]{1,0:T(8,128)}, f32[16,128]{1,0:T(8,128)}, f32[128,128]{1,0:T(8,128)}) custom-call(s32[1,4]{1,0:T(1,128)} %lens_ref.5, s32[1,32]{1,0:T(1,128)} %bitcast.12, f32[1,32]{1,0:T(1,128)} %bitcast.14, s32[1,32]{1,0:T(1,128)} %bitcast.13, f32[16,128]{1,0:T(8,128)} %gate_ref.1, ...), custom_call_target="tpu_custom_call" | custom-call | tf_op jit(solution)/shard_map/segment_maps/pallas_call | solution.py:318
  13.6 47.0 %all_to_all.15.maps_ref = f32[16,3,128,128]{3,2,1,0:T(8,128)S(1)} all-to-all(f32[16,3,128,128]{3,2,1,0:T(8,128)} %get-tuple-element.16), channel_id=1, replica_groups=mesh['dp'=8,'ctx'=16] {'ctx'}, dimensions={0} | all-to-all | bytes 6291456 | tf_op jit(solution)/shard_map/all_to_all | solution.py:299
  60.6 3.3 %chains.1 = f32[16,2,128,128]{3,2,1,0:T(8,128)} custom-call(f32[16,3,128,128]{3,2,1,0:T(8,128)S(1)} %all_to_all.15.maps_ref), custom_call_target="tpu_custom_call" | custom-call | tf_op jit(solution)/shard_map/chains/pallas_call | solution.py:346
  63.9 0.0 copy-start.2
  63.9 3.8 %all-to-all-start.1 = ((f32[16,2,128,128]{3,2,1,0:T(8,128)}), f32[16,2,128,128]{3,2,1,0:T(8,128)S(1)}, u32[]{:S(2)}, u32[]{:S(2)}) async-start(f32[16,2,128,128]{3,2,1,0:T(8,128)} %chains.1), calls=%async_computation.1 | async-start | bytes 4194304 | tf_op jit(solution)/shard_map/all_to_all | solution.py:299
  67.8 0.0 copy-done.2
  67.8 1.1 copy.16
  68.9 1.2 %reshape.21 = bf16[128,18,128]{2,1,0:T(8,128)(2,1)S(1)} reshape(bf16[2304,128]{1,0:T(8,128)(2,1)} %copy.16) | data formatting | bytes 1179648 | tf_op jit(solution)/shard_map/reshape | solution.py:355
  70.1 0.1 copy.19
  70.2 0.0 copy-start.1
  70.2 8.1 %ahead.1.pre_ref = f32[16,4,128,128]{3,2,1,0:T(8,128)} custom-call(s32[1,4]{1,0:T(1,128)} %lens_ref.5, bf16[128,2048]{1,0:T(8,128)(2,1)} %q_ref.5, bf16[128,2048]{1,0:T(8,128)(2,1)} %k_ref.5, bf16[128,2048]{1,0:T(8,128)(2,1)} %v_ref.3, bf16[128,2048]{1,0:T(8,128)(2,1)} %g_ref.5, f32[16,128,128]{2,1,0:T(8,128)} %get-tuple-element.17.inv_ref, ...), custom_call_target="tpu_custom_call" | custom-call | flops 12000000000 | bytes 40000000 | tf_op jit(solution)/shard_map/ahead/pallas_call | solution.py:335
  78.3 16.7 %all-to-all-done.1.ends_ref = f32[16,2,128,128]{3,2,1,0:T(8,128)S(1)} async-done(((f32[16,2,128,128]{3,2,1,0:T(8,128)}), f32[16,2,128,128]{3,2,1,0:T(8,128)S(1)}, u32[]{:S(2)}, u32[]{:S(2)}) %all-to-all-start.1) | async-done | bytes 2097184 | tf_op jit(solution)/shard_map/all_to_all | solution.py:299
  95.0 0.0 copy-start
  95.0 0.0 copy-done.1
  95.0 5.9 %logit_grads.1 = (f32[16,4,128,128]{3,2,1,0:T(8,128)}, f32[128,1,384]{2,1,0:T(1,128)}) custom-call(f32[16,2,128,128]{3,2,1,0:T(8,128)S(1)} %all-to-all-done.1.ends_ref, f32[16,4,128,128]{3,2,1,0:T(8,128)} %ahead.1.pre_ref, f32[16,128]{1,0:T(8,128)S(1)} %copy-done.1, bf16[18,128,128]{2,1,0:T(8,128)(2,1)S(1)} %bitcast.8), custom_call_target="tpu_custom_call", output_to_operand_aliasing={{0}: (1, {})} | custom-call | tf_op jit(solution)/shard_map/logit_grads/pallas_call | solution.py:356
  100.9 0.0 copy-done
  100.9 9.3 %all-to-all-start.2 = ((f32[128,1,384]{2,1,0:T(1,128)}), f32[128,1,384]{2,1,0:T(1,128)S(1)}, u32[]{:S(2)}, u32[]{:S(2)}) async-start(f32[128,1,384]{2,1,0:T(1,128)} %get-tuple-element.26), calls=%async_computation.2 | async-start | bytes 393216 | tf_op jit(solution)/shard_map/all_to_all | solution.py:367
  110.2 9.7 %segment_grads.1 = (bf16[128,2048]{1,0:T(8,128)(2,1)}, bf16[128,2048]{1,0:T(8,128)(2,1)}, bf16[128,2048]{1,0:T(8,128)(2,1)}, f32[16,128]{1,0:T(8,128)}) custom-call(s32[1,4]{1,0:T(1,128)} %lens_ref.5, bf16[128,2048]{1,0:T(8,128)(2,1)} %q_ref.5, bf16[128,2048]{1,0:T(8,128)(2,1)} %k_ref.5, bf16[128,2048]{1,0:T(8,128)(2,1)} %g_ref.5, ...), custom_call_target="tpu_custom_call" | custom-call | flops 12000000000 | bytes 40000000 | tf_op jit(solution)/shard_map/segment_grads/pallas_call | solution.py:368
  119.9 1.1 all-to-all-done.2.parts_ref
  121.0 0.8 sum_parts.1
Async XLA Ops:
  63.9 3.9 %copy-start.2 = (bf16[128,2304]{1,0:T(8,128)(2,1)S(1)}, bf16[128,2304]{1,0:T(8,128)(2,1)}, u32[]{:S(2)}) copy-start(bf16[128,2304]{1,0:T(8,128)(2,1)} %hidden_ref.1) | copy-start | bytes 1769476
  63.9 31.1 %all-to-all-start.1 = ((f32[16,2,128,128]{3,2,1,0:T(8,128)}), f32[16,2,128,128]{3,2,1,0:T(8,128)S(1)}, u32[]{:S(2)}, u32[]{:S(2)}) async-start(f32[16,2,128,128]{3,2,1,0:T(8,128)} %chains.1), calls=%async_computation.1 | async-start | bytes 4194304 | tf_op jit(solution)/shard_map/all_to_all | solution.py:299
  70.2 24.8 %copy-start.1 = (f32[16,128]{1,0:T(8,128)S(1)}, f32[16,128]{1,0:T(8,128)}, u32[]{:S(2)}) copy-start(f32[16,128]{1,0:T(8,128)} %get-tuple-element.19.beta_ref) | copy-start | bytes 24580
  95.0 5.9 %copy-start = (f32[16,2,128,128]{3,2,1,0:T(8,128)}, f32[16,2,128,128]{3,2,1,0:T(8,128)S(1)}, u32[]{:S(2)}) copy-start(f32[16,2,128,128]{3,2,1,0:T(8,128)S(1)} %all-to-all-done.1.ends_ref) | copy-start | bytes 6291460
  100.9 20.1 %all-to-all-start.2 = ((f32[128,1,384]{2,1,0:T(1,128)}), f32[128,1,384]{2,1,0:T(1,128)S(1)}, u32[]{:S(2)}, u32[]{:S(2)}) async-start(f32[128,1,384]{2,1,0:T(1,128)} %get-tuple-element.26), calls=%async_computation.2 | async-start | bytes 393216 | tf_op jit(solution)/shard_map/all_to_all | solution.py:367

commit v8 on v7

--- a/solution.py
+++ b/solution.py
@@ -12,6 +12,7 @@
 HG = 4
 VMEM_LIMIT = 56 * 1024 * 1024
 VMEM_MID = 48 * 1024 * 1024
+VMEM_FIRST = 40 * 1024 * 1024
 VMEM_SMALL = 24 * 1024 * 1024
 NN = (((1,), (0,)), ((), ()))
 NT = (((1,), (1,)), ((), ()))
@@ -324,7 +325,7 @@
         out_shape=[jax.ShapeDtypeStruct(s, F32) for s in (
             (heads, 3, N, N), (heads, N, N), (heads, N), (heads, N), (N, N))],
         scratch_shapes=masks,
-        compiler_params=params,
+        compiler_params=pltpu.CompilerParams(vmem_limit_bytes=VMEM_FIRST),
         name="segment_maps",
     )(lengths, prompts_row, rewards_row, prompts_row, log_gate, beta_weight.T, hidden_in,
       queries, key_rows, value_rows, out_grad)

time: 122 us -> 129 us (1.057)
  local copies, waits for them, and re-layouts: 2.42 us -> 11.2 us
  Pallas kernels: 40.7 us -> 38.6 us
    unnamed x6 -> x34, local copies, waits for them, and re-layouts: 0.01 us -> 8.8 us
    pallas_call x1, Pallas kernels: 13 us -> 10.9 us  [local(): pl.pallas_call(maps_kernel, grid=(heads // HP,), in_specs=[smem, smem, wh...]
  transfers between devices with their start and end apart: 2 -> 2, of which waited for: 2 -> 2; matrix products, arithmetic and copies ran while one was open for 2% -> 2% of each run, Pallas kernels for 15% -> 14%
where the time goes in v8:
time: 129 us; the launch traced here: 128 us
  blocking collectives  46.8 us (36%)
  Pallas kernels  38.6 us (30%)
  waiting for transfers between devices  17.8 us (14%)
  starting transfers between devices  13.2 us (10%)
  local copies, waits for them, and re-layouts  11.2 us (9%)
    all_to_all x1, blocking collectives, to_owners(): return lax.all_to_all(x, 'ctx', 0, 0, tiled=True)  46.8 us
    all_to_all x1, waiting for transfers between devices, to_owners(): return lax.all_to_all(x, 'ctx', 0, 0, tiled=True)  16.7 us
    pallas_call x1, Pallas kernels, local(): pl.pallas_call(maps_kernel, grid=(heads // HP,), in_specs=[smem, smem, wh...  10.9 us
    pallas_call x1, Pallas kernels, local(): pl.pallas_call(grads_kernel, grid=(heads // HG,), in_specs=[smem] + [few_...  9.69 us
    all_to_all x1, starting transfers between devices, local(): pieces = lax.all_to_all(dw, ('dp', 'ctx'), 0, 0, tiled=True)  9.33 us
    unnamed x34, local copies, waits for them, and re-layouts  8.8 us
    pallas_call x1, Pallas kernels, local(): pl.pallas_call(ahead_kernel, grid=(heads // HG,), in_specs=[smem] + [few_...  8.02 us
    pallas_call x1, Pallas kernels, local(): pl.pallas_call(logits_kernel, grid=(heads // HP,), in_specs=[square(2), s...  5.89 us
  transfers between devices with their start and end apart: 2, of which 2 were waited for; matrix products, arithmetic and copies ran while one was open for 2% of the time, Pallas kernels for 14%

profile of v8, /device:TPU:1, one launch (start us, length us, event | category | flops | bytes accessed | tf_op | source)
XLA Modules:
  0.0 128.4 jit_solution(16867620640610063482)
XLA Ops:
  0.6 0.0 copy-start.1
  0.6 1.1 copy-done.1
  1.7 0.0 copy-start.3
  1.7 1.0 copy-done.3
  2.7 0.0 copy-start.4
  2.7 1.0 copy-done.4
  3.8 0.0 copy-start.5
  3.8 1.0 copy-done.5
  4.8 0.0 copy-start.6
  4.8 1.0 copy-done.6
  5.9 0.0 copy-start.7
  5.9 0.9 copy-done.7
  6.8 0.0 copy-start.8
  6.8 0.7 copy-done.8
  7.5 0.0 copy-start.11
  7.5 0.7 copy-done.11
  8.1 0.0 copy-start.12
  8.1 0.7 copy-done.12
  8.8 0.0 copy-start.13
  8.8 0.7 copy-done.13
  9.4 10.9 %segment_maps.1 = (f32[16,3,128,128]{3,2,1,0:T(8,128)S(1)}, f32[16,128,128]{2,1,0:T(8,128)S(1)}, f32[16,128]{1,0:T(8,128)S(1)}, f32[16,128]{1,0:T(8,128)S(1)}, f32[128,128]{1,0:T(8,128)S(1)}) custom-call(s32[1,4]{1,0:T(1,128)S(1)} %copy-done.13, s32[1,32]{1,0:T(1,128)S(1)} %bitcast.11, f32[1,32]{1,0:T(1,128)S(1)} %bitcast.13, s32[1,32]{1,0:T(1,128)S(1)} %bitcast.12, ...), custom_call_target="tpu_custom_call" | custom-call | tf_op jit(solution)/shard_map/segment_maps/pallas_call | solution.py:319
  20.3 0.0 copy-start.9
  20.3 0.0 copy-start.14
  20.3 0.0 copy-start.15
  20.3 0.0 copy-start.16
  20.3 46.8 %all_to_all.15.maps_ref = f32[16,3,128,128]{3,2,1,0:T(8,128)S(1)} all-to-all(f32[16,3,128,128]{3,2,1,0:T(8,128)S(1)} %get-tuple-element.16), channel_id=1, replica_groups=mesh['dp'=8,'ctx'=16] {'ctx'}, dimensions={0} | all-to-all | bytes 6291456 | tf_op jit(solution)/shard_map/all_to_all | solution.py:300
  67.1 0.0 copy-done.9
  67.2 0.0 copy-done.14
  67.2 0.0 copy-done.15
  67.2 0.0 copy-done.16
  67.2 3.3 %chains.1 = f32[16,2,128,128]{3,2,1,0:T(8,128)} custom-call(f32[16,3,128,128]{3,2,1,0:T(8,128)S(1)} %all_to_all.15.maps_ref), custom_call_target="tpu_custom_call" | custom-call | tf_op jit(solution)/shard_map/chains/pallas_call | solution.py:347
  70.5 0.0 copy-start.2
  70.5 3.8 %all-to-all-start.1 = ((f32[16,2,128,128]{3,2,1,0:T(8,128)}), f32[16,2,128,128]{3,2,1,0:T(8,128)S(1)}, u32[]{:S(2)}, u32[]{:S(2)}) async-start(f32[16,2,128,128]{3,2,1,0:T(8,128)} %chains.1), calls=%async_computation.1 | async-start | bytes 4194304 | tf_op jit(solution)/shard_map/all_to_all | solution.py:300
  74.4 0.0 copy-done.2
  74.4 1.1 copy.16
  75.4 1.2 reshape.21
  76.7 0.1 copy.19
  76.8 0.0 copy-start.10
  76.8 8.0 %ahead.1.pre_ref = f32[16,4,128,128]{3,2,1,0:T(8,128)} custom-call(s32[1,4]{1,0:T(1,128)} %lens_ref.5, bf16[128,2048]{1,0:T(8,128)(2,1)} %q_ref.5, bf16[128,2048]{1,0:T(8,128)(2,1)} %k_ref.5, bf16[128,2048]{1,0:T(8,128)(2,1)} %v_ref.3, bf16[128,2048]{1,0:T(8,128)(2,1)} %g_ref.5, f32[16,128,128]{2,1,0:T(8,128)} %copy-done.14, f32[16,128]{1,0:T(8,128)} %copy-done.16, ...), custom_call_target="tpu_custom_call" | custom-call | flops 12000000000 | bytes 40000000 | tf_op jit(solution)/shard_map/ahead/pallas_call | solution.py:336
  84.8 16.7 %all-to-all-done.1.ends_ref = f32[16,2,128,128]{3,2,1,0:T(8,128)S(1)} async-done(((f32[16,2,128,128]{3,2,1,0:T(8,128)}), f32[16,2,128,128]{3,2,1,0:T(8,128)S(1)}, u32[]{:S(2)}, u32[]{:S(2)}) %all-to-all-start.1) | async-done | bytes 2097184 | tf_op jit(solution)/shard_map/all_to_all | solution.py:300
  101.6 0.0 copy-start
  101.6 0.0 copy-done.10
  101.6 5.9 %logit_grads.1 = (f32[16,4,128,128]{3,2,1,0:T(8,128)}, f32[128,1,384]{2,1,0:T(1,128)}) custom-call(f32[16,2,128,128]{3,2,1,0:T(8,128)S(1)} %all-to-all-done.1.ends_ref, f32[16,4,128,128]{3,2,1,0:T(8,128)} %ahead.1.pre_ref, f32[16,128]{1,0:T(8,128)S(1)} %copy-done.10, bf16[18,128,128]{2,1,0:T(8,128)(2,1)S(1)} %bitcast.9), custom_call_target="tpu_custom_call", output_to_operand_aliasing={{0}: (1, {})} | custom-call | tf_op jit(solution)/shard_map/logit_grads/pallas_call | solution.py:357
  107.5 0.0 copy-done
  107.5 9.3 %all-to-all-start.2 = ((f32[128,1,384]{2,1,0:T(1,128)}), f32[128,1,384]{2,1,0:T(1,128)S(1)}, u32[]{:S(2)}, u32[]{:S(2)}) async-start(f32[128,1,384]{2,1,0:T(1,128)} %get-tuple-element.26), calls=%async_computation.2 | async-start | bytes 393216 | tf_op jit(solution)/shard_map/all_to_all | solution.py:368
  116.8 9.7 %segment_grads.1 = (bf16[128,2048]{1,0:T(8,128)(2,1)}, bf16[128,2048]{1,0:T(8,128)(2,1)}, bf16[128,2048]{1,0:T(8,128)(2,1)}, f32[16,128]{1,0:T(8,128)}) custom-call(s32[1,4]{1,0:T(1,128)} %lens_ref.5, bf16[128,2048]{1,0:T(8,128)(2,1)} %q_ref.5, bf16[128,2048]{1,0:T(8,128)(2,1)} %k_ref.5, bf16[128,2048]{1,0:T(8,128)(2,1)} %g_ref.5, ...), custom_call_target="tpu_custom_call" | custom-call | flops 12000000000 | bytes 40000000 | tf_op jit(solution)/shard_map/segment_grads/pallas_call | solution.py:369
  126.5 1.1 all-to-all-done.2.parts_ref
  127.6 0.8 sum_parts.1
Async XLA Ops:
  0.6 1.1 copy-start.1
  1.7 1.0 copy-start.3
  2.7 1.0 copy-start.4
  3.8 1.0 copy-start.5
  4.8 1.0 copy-start.6
  5.9 0.9 copy-start.7
  6.8 0.7 copy-start.8
  7.5 0.7 copy-start.11
  8.1 0.7 copy-start.12
  8.8 0.7 copy-start.13
  20.3 46.9 %copy-start.9 = (f32[16,128]{1,0:T(8,128)}, f32[16,128]{1,0:T(8,128)S(1)}, u32[]{:S(2)}) copy-start(f32[16,128]{1,0:T(8,128)S(1)} %get-tuple-element.19.beta_ref) | copy-start | bytes 24580
  20.3 46.9 %copy-start.14 = (f32[16,128,128]{2,1,0:T(8,128)}, f32[16,128,128]{2,1,0:T(8,128)S(1)}, u32[]{:S(2)}) copy-start(f32[16,128,128]{2,1,0:T(8,128)S(1)} %get-tuple-element.17.inv_ref) | copy-start | bytes 3145732
  20.3 46.9 %copy-start.15 = (f32[128,128]{1,0:T(8,128)}, f32[128,128]{1,0:T(8,128)S(1)}, u32[]{:S(2)}) copy-start(f32[128,128]{1,0:T(8,128)S(1)} %get-tuple-element.20.tw_ref) | copy-start | bytes 196612
  20.3 46.9 %copy-start.16 = (f32[16,128]{1,0:T(8,128)}, f32[16,128]{1,0:T(8,128)S(1)}, u32[]{:S(2)}) copy-start(f32[16,128]{1,0:T(8,128)S(1)} %get-tuple-element.18.sum_ref) | copy-start | bytes 24580
  70.5 3.9 %copy-start.2 = (bf16[128,2304]{1,0:T(8,128)(2,1)S(1)}, bf16[128,2304]{1,0:T(8,128)(2,1)}, u32[]{:S(2)}) copy-start(bf16[128,2304]{1,0:T(8,128)(2,1)} %hidden_ref.1) | copy-start | bytes 1769476
  70.5 31.1 %all-to-all-start.1 = ((f32[16,2,128,128]{3,2,1,0:T(8,128)}), f32[16,2,128,128]{3,2,1,0:T(8,128)S(1)}, u32[]{:S(2)}, u32[]{:S(2)}) async-start(f32[16,2,128,128]{3,2,1,0:T(8,128)} %chains.1), calls=%async_computation.1 | async-start | bytes 4194304 | tf_op jit(solution)/shard_map/all_to_all | solution.py:300
  76.8 24.8 %copy-start.10 = (f32[16,128]{1,0:T(8,128)S(1)}, f32[16,128]{1,0:T(8,128)}, u32[]{:S(2)}) copy-start(f32[16,128]{1,0:T(8,128)} %copy-done.9) | copy-start | bytes 24580
  101.6 5.9 %copy-start = (f32[16,2,128,128]{3,2,1,0:T(8,128)}, f32[16,2,128,128]{3,2,1,0:T(8,128)S(1)}, u32[]{:S(2)}) copy-start(f32[16,2,128,128]{3,2,1,0:T(8,128)S(1)} %all-to-all-done.1.ends_ref) | copy-start | bytes 6291460
  107.5 20.1 %all-to-all-start.2 = ((f32[128,1,384]{2,1,0:T(1,128)}), f32[128,1,384]{2,1,0:T(1,128)S(1)}, u32[]{:S(2)}, u32[]{:S(2)}) async-start(f32[128,1,384]{2,1,0:T(1,128)} %get-tuple-element.26), calls=%async_computation.2 | async-start | bytes 393216 | tf_op jit(solution)/shard_map/all_to_all | solution.py:368

commit v9 on v7

--- a/solution.py
+++ b/solution.py
@@ -130,7 +130,7 @@
 
 def maps_kernel(lens_ref, prompts_ref, rewards_row_ref, prompts_row_ref, gate_ref, weight_ref, hidden_ref,
                 q_ref, k_ref, v_ref, g_ref,
-                maps_ref, inv_ref, sum_ref, beta_ref, tw_ref,
+                maps_ref, sum_ref, beta_ref, tw_ref,
                 linked_s, head_s, tail_s):
     ctx, dp = lax.axis_index("ctx"), lax.axis_index("dp")
 
@@ -165,8 +165,6 @@
         maps_ref[i, 0] = from_head[N - 1 : N, :] * same
         rest.append((jnp.concatenate([beta * v.astype(F32), beta * from_head * kn], axis=1), to_tail * kn))
     inverses = unit_inverses(lowers)
-    for i in range(HP):
-        inv_ref[i] = inverses[i]
     uzs = [dot3(inverse, sides, NN) for inverse, (sides, _) in zip(inverses, rest)]
     for i in range(HP):
         ends = dot3(uzs[i], rest[i][1], TN)
@@ -188,7 +186,7 @@
             grad = dot3(grad, maps_ref[b, 0], NT) + maps_ref[b, 2]
 
 
-def ahead_kernel(lens_ref, q_ref, k_ref, v_ref, g_ref, inv_ref, sum_ref, beta_ref, tw_ref,
+def ahead_kernel(lens_ref, q_ref, k_ref, v_ref, g_ref, sum_ref, beta_ref, tw_ref,
                  pre_ref,
                  linked_s, head_s, tail_s):
     ctx = lax.axis_index("ctx")
@@ -198,6 +196,8 @@
         linked_s[...], head_s[...], tail_s[...], unused = plan(lens_ref, ctx)
 
     linked, head, tail, tw = linked_s[...], head_s[...], tail_s[...], tw_ref[...]
+    strict = jnp.where(iota(0) > iota(1), 1.0, 0.0)
+    lowers, lefts, rights = [], [], []
     for i in range(HG):
         h = pl.program_id(0) * HG + i
         cols = slice(i * N, (i + 1) * N)
@@ -205,10 +205,14 @@
         gate_row, beta_row = sum_ref[pl.ds(h, 1), :], beta_ref[pl.ds(h, 1), :]
         qn, kn, rq, rk, rk_cols, decay, key_key, query_key, from_head, to_tail, beta = head_terms(
             q, k, gate_row, beta_row, linked, head, tail)
-        uz = dot3(inv_ref[i], jnp.concatenate([beta * v.astype(F32), beta * from_head * kn], axis=1), NN)
+        lowers.append(strict * (beta * decay * key_key))
+        lefts.append(jnp.concatenate([beta * v.astype(F32), beta * from_head * kn], axis=1))
+        rights.append(jnp.concatenate([dot2l(decay * query_key * tw, g, TN), to_tail * kn], axis=1))
+    inverses = unit_inverses(lowers)
+    for i in range(HG):
+        uz = dot3(inverses[i], lefts[i], NN)
+        dxx = dot3(inverses[i], rights[i], TN)
         pre_ref[i, 0], pre_ref[i, 2] = uz[:, :N], uz[:, N:]
-        mg = dot2l(decay * query_key * tw, g, TN)
-        dxx = dot3(inv_ref[i], jnp.concatenate([mg, to_tail * kn], axis=1), TN)
         pre_ref[i, 1], pre_ref[i, 3] = dxx[:, :N], dxx[:, N:]
 
 
@@ -315,14 +319,14 @@
 
     one_square = pl.BlockSpec((HP, N, N), lambda i: (i, 0, 0))
     masks = [pltpu.VMEM((N, N), F32)] * 3
-    maps, inverse, sums, beta, tw = pl.pallas_call(
+    maps, sums, beta, tw = pl.pallas_call(
         maps_kernel,
         grid=(heads // HP,),
         in_specs=[smem, smem, whole(rewards_row.shape), whole(prompts_row.shape), whole(log_gate.shape),
                   whole((heads, depth)), whole(hidden_in.shape)] + [by_heads] * 4,
-        out_specs=[square(3), one_square, whole((heads, N)), whole((heads, N)), whole((N, N))],
+        out_specs=[square(3), whole((heads, N)), whole((heads, N)), whole((N, N))],
         out_shape=[jax.ShapeDtypeStruct(s, F32) for s in (
-            (heads, 3, N, N), (heads, N, N), (heads, N), (heads, N), (N, N))],
+            (heads, 3, N, N), (heads, N), (heads, N), (N, N))],
         scratch_shapes=masks,
         compiler_params=params,
         name="segment_maps",
@@ -335,14 +339,14 @@
     pre = pl.pallas_call(
         ahead_kernel,
         grid=(heads // HG,),
-        in_specs=[smem] + [few_heads] * 4 + [few_squares, whole((heads, N)), whole((heads, N)), whole((N, N))],
+        in_specs=[smem] + [few_heads] * 4 + [whole((heads, N)), whole((heads, N)), whole((N, N))],
         out_specs=few_pre,
         out_shape=jax.ShapeDtypeStruct((heads, 4, N, N), F32),
         scratch_shapes=masks,
         compiler_params=params,
         cost_estimate=pl.CostEstimate(flops=12_000_000_000, bytes_accessed=40_000_000, transcendentals=0),
         name="ahead",
-    )(lengths, queries, key_rows, value_rows, out_grad, inverse, sums, beta, tw)
+    )(lengths, queries, key_rows, value_rows, out_grad, sums, beta, tw)
     ends = pl.pallas_call(
         chains_kernel,
         out_shape=jax.ShapeDtypeStruct((owned.shape[0], 2, N, N), F32),

time: 122 us -> 122 us (level)
  Pallas kernels: 40.7 us -> 47.7 us
  waiting for transfers between devices: 17.8 us -> 10.9 us
    all_to_all x1, waiting for transfers between devices: 16.7 us -> 9.77 us  [to_owners(): return lax.all_to_all(x, 'ctx', 0, 0, tiled=True)]
    pallas_call x1, Pallas kernels: 8.05 us -> 15 us  [local(): pl.pallas_call(ahead_kernel, grid=(heads // HG,), in_specs=[smem] + [few_...]
  transfers between devices with their start and end apart: 2 -> 2, of which waited for: 2 -> 2; matrix products, arithmetic and copies ran while one was open for 2% -> 2% of each run, Pallas kernels for 15% -> 20%
where the time goes in v9:
time: 122 us
  Pallas kernels  47.7 us (39%)
  blocking collectives  47 us (39%)
  starting transfers between devices  13.2 us (11%)
  waiting for transfers between devices  10.9 us (9%)
  local copies, waits for them, and re-layouts  2.42 us (2%)
    all_to_all x1, blocking collectives, to_owners(): return lax.all_to_all(x, 'ctx', 0, 0, tiled=True)  47 us
    pallas_call x1, Pallas kernels, local(): pl.pallas_call(ahead_kernel, grid=(heads // HG,), in_specs=[smem] + [few_...  15 us
    pallas_call x1, Pallas kernels, local(): pl.pallas_call(maps_kernel, grid=(heads // HP,), in_specs=[smem, smem, wh...  13 us
    all_to_all x1, waiting for transfers between devices, to_owners(): return lax.all_to_all(x, 'ctx', 0, 0, tiled=True)  9.77 us
    pallas_call x1, Pallas kernels, local(): pl.pallas_call(grads_kernel, grid=(heads // HG,), in_specs=[smem] + [few_...  9.69 us
    all_to_all x1, starting transfers between devices, local(): pieces = lax.all_to_all(dw, ('dp', 'ctx'), 0, 0, tiled=True)  9.33 us
    pallas_call x1, Pallas kernels, local(): pl.pallas_call(logits_kernel, grid=(heads // HP,), in_specs=[square(2), s...  5.88 us
    all_to_all x1, starting transfers between devices, to_owners(): return lax.all_to_all(x, 'ctx', 0, 0, tiled=True)  3.85 us
  transfers between devices with their start and end apart: 2, of which 2 were waited for; matrix products, arithmetic and copies ran while one was open for 2% of the time, Pallas kernels for 20%

profile of v9, /device:TPU:1, one launch (start us, length us, event | category | flops | bytes accessed | tf_op | source)
XLA Modules:
  0.0 121.9 jit_solution(1197236820822210943)
XLA Ops:
  0.6 13.0 %segment_maps.1 = (f32[16,3,128,128]{3,2,1,0:T(8,128)}, f32[16,128]{1,0:T(8,128)}, f32[16,128]{1,0:T(8,128)}, f32[128,128]{1,0:T(8,128)}) custom-call(s32[1,4]{1,0:T(1,128)} %lens_ref.5, s32[1,32]{1,0:T(1,128)} %bitcast.12, f32[1,32]{1,0:T(1,128)} %bitcast.14, s32[1,32]{1,0:T(1,128)} %bitcast.13, f32[16,128]{1,0:T(8,128)} %gate_ref.1, ...), custom_call_target="tpu_custom_call" | custom-call | tf_op jit(solution)/shard_map/segment_maps/pallas_call | solution.py:322
  13.6 47.0 %all_to_all.15.maps_ref = f32[16,3,128,128]{3,2,1,0:T(8,128)S(1)} all-to-all(f32[16,3,128,128]{3,2,1,0:T(8,128)} %get-tuple-element.15), channel_id=1, replica_groups=mesh['dp'=8,'ctx'=16] {'ctx'}, dimensions={0} | all-to-all | bytes 6291456 | tf_op jit(solution)/shard_map/all_to_all | solution.py:303
  60.6 3.3 %chains.1 = f32[16,2,128,128]{3,2,1,0:T(8,128)} custom-call(f32[16,3,128,128]{3,2,1,0:T(8,128)S(1)} %all_to_all.15.maps_ref), custom_call_target="tpu_custom_call" | custom-call | tf_op jit(solution)/shard_map/chains/pallas_call | solution.py:350
  63.9 0.0 copy-start.2
  63.9 3.8 %all-to-all-start.1 = ((f32[16,2,128,128]{3,2,1,0:T(8,128)}), f32[16,2,128,128]{3,2,1,0:T(8,128)S(1)}, u32[]{:S(2)}, u32[]{:S(2)}) async-start(f32[16,2,128,128]{3,2,1,0:T(8,128)} %chains.1), calls=%async_computation.1 | async-start | bytes 4194304 | tf_op jit(solution)/shard_map/all_to_all | solution.py:303
  67.8 0.0 copy-done.2
  67.8 1.1 copy.16
  68.8 1.2 %reshape.21 = bf16[128,18,128]{2,1,0:T(8,128)(2,1)S(1)} reshape(bf16[2304,128]{1,0:T(8,128)(2,1)} %copy.16) | data formatting | bytes 1179648 | tf_op jit(solution)/shard_map/reshape | solution.py:359
  70.1 0.1 copy.19
  70.2 0.0 copy-start.1
  70.2 15.0 %ahead.1.pre_ref = f32[16,4,128,128]{3,2,1,0:T(8,128)} custom-call(s32[1,4]{1,0:T(1,128)} %lens_ref.5, bf16[128,2048]{1,0:T(8,128)(2,1)} %q_ref.5, bf16[128,2048]{1,0:T(8,128)(2,1)} %k_ref.5, bf16[128,2048]{1,0:T(8,128)(2,1)} %v_ref.3, bf16[128,2048]{1,0:T(8,128)(2,1)} %g_ref.5, f32[16,128]{1,0:T(8,128)} %get-tuple-element.16.sum_ref, ...), custom_call_target="tpu_custom_call" | custom-call | flops 12000000000 | bytes 40000000 | tf_op jit(solution)/shard_map/ahead/pallas_call | solution.py:339
  85.2 9.8 %all-to-all-done.1.ends_ref = f32[16,2,128,128]{3,2,1,0:T(8,128)S(1)} async-done(((f32[16,2,128,128]{3,2,1,0:T(8,128)}), f32[16,2,128,128]{3,2,1,0:T(8,128)S(1)}, u32[]{:S(2)}, u32[]{:S(2)}) %all-to-all-start.1) | async-done | bytes 2097184 | tf_op jit(solution)/shard_map/all_to_all | solution.py:303
  95.0 0.0 copy-start
  95.0 0.0 copy-done.1
  95.0 5.9 %logit_grads.1 = (f32[16,4,128,128]{3,2,1,0:T(8,128)}, f32[128,1,384]{2,1,0:T(1,128)}) custom-call(f32[16,2,128,128]{3,2,1,0:T(8,128)S(1)} %all-to-all-done.1.ends_ref, f32[16,4,128,128]{3,2,1,0:T(8,128)} %ahead.1.pre_ref, f32[16,128]{1,0:T(8,128)S(1)} %copy-done.1, bf16[18,128,128]{2,1,0:T(8,128)(2,1)S(1)} %bitcast.8), custom_call_target="tpu_custom_call", output_to_operand_aliasing={{0}: (1, {})} | custom-call | tf_op jit(solution)/shard_map/logit_grads/pallas_call | solution.py:360
  100.9 0.0 copy-done
  100.9 9.3 %all-to-all-start.2 = ((f32[128,1,384]{2,1,0:T(1,128)}), f32[128,1,384]{2,1,0:T(1,128)S(1)}, u32[]{:S(2)}, u32[]{:S(2)}) async-start(f32[128,1,384]{2,1,0:T(1,128)} %get-tuple-element.24), calls=%async_computation.2 | async-start | bytes 393216 | tf_op jit(solution)/shard_map/all_to_all | solution.py:371
  110.2 9.7 %segment_grads.1 = (bf16[128,2048]{1,0:T(8,128)(2,1)}, bf16[128,2048]{1,0:T(8,128)(2,1)}, bf16[128,2048]{1,0:T(8,128)(2,1)}, f32[16,128]{1,0:T(8,128)}) custom-call(s32[1,4]{1,0:T(1,128)} %lens_ref.5, bf16[128,2048]{1,0:T(8,128)(2,1)} %q_ref.5, bf16[128,2048]{1,0:T(8,128)(2,1)} %k_ref.5, bf16[128,2048]{1,0:T(8,128)(2,1)} %g_ref.5, ...), custom_call_target="tpu_custom_call" | custom-call | flops 12000000000 | bytes 40000000 | tf_op jit(solution)/shard_map/segment_grads/pallas_call | solution.py:372
  119.9 1.1 all-to-all-done.2.parts_ref
  121.0 0.8 sum_parts.1
Async XLA Ops:
  63.9 3.9 %copy-start.2 = (bf16[128,2304]{1,0:T(8,128)(2,1)S(1)}, bf16[128,2304]{1,0:T(8,128)(2,1)}, u32[]{:S(2)}) copy-start(bf16[128,2304]{1,0:T(8,128)(2,1)} %hidden_ref.1) | copy-start | bytes 1769476
  63.9 31.1 %all-to-all-start.1 = ((f32[16,2,128,128]{3,2,1,0:T(8,128)}), f32[16,2,128,128]{3,2,1,0:T(8,128)S(1)}, u32[]{:S(2)}, u32[]{:S(2)}) async-start(f32[16,2,128,128]{3,2,1,0:T(8,128)} %chains.1), calls=%async_computation.1 | async-start | bytes 4194304 | tf_op jit(solution)/shard_map/all_to_all | solution.py:303
  70.2 24.8 %copy-start.1 = (f32[16,128]{1,0:T(8,128)S(1)}, f32[16,128]{1,0:T(8,128)}, u32[]{:S(2)}) copy-start(f32[16,128]{1,0:T(8,128)} %get-tuple-element.17.beta_ref) | copy-start | bytes 24580
  95.0 5.9 %copy-start = (f32[16,2,128,128]{3,2,1,0:T(8,128)}, f32[16,2,128,128]{3,2,1,0:T(8,128)S(1)}, u32[]{:S(2)}) copy-start(f32[16,2,128,128]{3,2,1,0:T(8,128)S(1)} %all-to-all-done.1.ends_ref) | copy-start | bytes 6291460
  100.9 20.1 %all-to-all-start.2 = ((f32[128,1,384]{2,1,0:T(1,128)}), f32[128,1,384]{2,1,0:T(1,128)S(1)}, u32[]{:S(2)}, u32[]{:S(2)}) async-start(f32[128,1,384]{2,1,0:T(1,128)} %get-tuple-element.24), calls=%async_computation.2 | async-start | bytes 393216 | tf_op jit(solution)/shard_map/all_to_all | solution.py:371
